TPU v7x, 512 devices: a whole 4x4x16 slice. The times are simulated.
512 devices in a mesh: mp: 16 (over z), trow: 4 (over x), tcol: 8 (over y, core).
Axes of the slice: x: 4, y: 4, z: 16, core: 2. Of those that a mesh axis runs over, the one named last changes fastest.
Arguments:
- gram: float32 [16, 4096, 4096], P('mp', 'trow', 'tcol'), as said below
- rhs: float32 [256, 4096], P(('mp', 'tcol'), 'trow'), may hold values from -6 to 6
- guess: float32 [256, 4096], P(('mp', 'tcol'), 'trow'), may hold values from -6 to 6
Outputs:
- merged: float32 [256, 4096], P(('mp', 'tcol'), 'trow')
- residual: float32 [256, 4096], P(('mp', 'tcol'), 'trow')
Inputs may be any that keep to these rules, and one draw needn't show every extreme that they name: gram holds 16 symmetric positive definite matrices, one per model.
All inputs are finite; a program needn't handle non-finite values.
Results may differ from a plain program's by a relative error of at most 0.0003.
Values sent between devices are 32-bit elements; how exact they have to be, the bound alone decides.
No kernel may reach another device: no remote copies, remote signals or barrier semaphores. Data moves between devices by JAX's collectives and lax.ppermute only.
A program may use at most 64 MiB of HBM per device.

v0:
```python
import jax
import jax.numpy as jnp
from jax import lax
from jax.sharding import PartitionSpec as P

ITERS = 2


def contract(block, weights):
    return lax.dot_general(
        block,
        weights,
        (((1,), (1,)), ((), ())),
        precision=lax.Precision.HIGHEST,
        preferred_element_type=jnp.float32,
    )


def shards(gram, rhs, guess):
    gram_tile = gram[0]
    block_cols = gram_tile.shape[1]

    def partial_terms(vector):
        columns = lax.all_gather(vector, ("mp", "tcol"), axis=0, tiled=True)
        gathered = lax.all_gather(columns, "trow", axis=1, tiled=True)
        block = lax.dynamic_slice_in_dim(
            gathered, lax.axis_index("tcol") * block_cols, block_cols, 1
        )
        return contract(block, gram_tile)

    def apply_total(vector):
        terms = partial_terms(vector)
        return lax.psum_scatter(terms, ("mp", "tcol"), scatter_dimension=0, tiled=True)

    def squares(values):
        return lax.psum(jnp.sum(values * values, axis=1), "trow")

    merged = guess
    residual = rhs - apply_total(guess)
    direction = residual
    norm_now = squares(residual)
    for step in range(ITERS):
        image = apply_total(direction)
        curve = lax.psum(jnp.sum(direction * image, axis=1), "trow")
        alpha = norm_now / curve
        merged = merged + alpha[:, None] * direction
        residual = residual - alpha[:, None] * image
        if step + 1 < ITERS:
            norm_next = squares(residual)
            direction = residual + (norm_next / norm_now)[:, None] * direction
            norm_now = norm_next
    return (merged, residual)


def solution(mesh):
    in_specs = (P("mp", "trow", "tcol"), P(("mp", "tcol"), "trow"), P(("mp", "tcol"), "trow"))
    out_specs = (P(("mp", "tcol"), "trow"), P(("mp", "tcol"), "trow"))
    return jax.shard_map(shards, mesh=mesh, in_specs=in_specs, out_specs=out_specs, check_vma=False)
```

profile of v0, /device:TPU:8, one launch (start us, length us, event | category | flops | bytes accessed | tf_op | source)
XLA Modules:
  0.0 1627.1 jit_solution(7316392951566220621)
XLA Ops:
  7.2 0.7 all-gather.16.cloned.1.call-update
  8.0 138.1 %all-gather.16.cloned.1.call-done = f32[128,2,1024]{2,1,0:T(2,128)} async-done(((f32[1,2,1024]{2,1,0:T(2,128)}), f32[128,2,1024]{2,1,0:T(2,128)}) %all-gather.16.cloned.1.call-update) | async-done | bytes 1048592 | tf_op jit(solution)/shard_map/all_gather | solution.py:24
  146.0 2.9 reshape.8
  149.0 0.0 all-reduce.8.cloned.1.call-start
  149.1 51.7 %all-gather.10.cloned.1.call-done = f32[256,4096]{1,0:T(8,128)} async-done(((f32[256,1024]{1,0:T(8,128)}), f32[256,4096]{1,0:T(8,128)}) %all-gather.10.cloned.1.call-update) | async-done | bytes 4194320 | tf_op jit(solution)/shard_map/all_gather | solution.py:25
  200.7 3.9 fusion.4
  204.7 0.0 all-gather.18.cloned.1.call-start
  204.8 1.3 dynamic-slice
  206.7 333.7 %all-reduce.8.cloned.1.call-done = f32[256,1024]{1,0:T(8,128)} async-done(((f32[256,1024]{1,0:T(8,128)}), f32[256,1024]{1,0:T(8,128)}) %all-reduce.8.cloned.1.call-update) | async-done | bytes 1048592
  540.4 1.4 dynamic-slice_subtract_fusion
  541.7 0.0 all-gather.12.cloned.1.call-start
  541.8 129.9 %all-gather.18.cloned.1.call-done = f32[128,2,1024]{2,1,0:T(2,128)} async-done(((f32[1,2,1024]{2,1,0:T(2,128)}), f32[128,2,1024]{2,1,0:T(2,128)}) %all-gather.18.cloned.1.call-update) | async-done | bytes 1048592 | tf_op jit(solution)/shard_map/all_gather | solution.py:24
  671.7 2.9 reshape.10
  674.6 0.0 all-reduce.10.cloned.1.call-start
  674.7 51.7 %all-gather.12.cloned.1.call-done = f32[256,4096]{1,0:T(8,128)} async-done(((f32[256,1024]{1,0:T(8,128)}), f32[256,4096]{1,0:T(8,128)}) %all-gather.12.cloned.1.call-update) | async-done | bytes 4194320 | tf_op jit(solution)/shard_map/all_gather | solution.py:25
  726.4 3.9 fusion.2
  730.3 0.0 all-gather.20.cloned.1.call-start
  730.4 335.7 %all-reduce.10.cloned.1.call-done = f32[256,1024]{1,0:T(8,128)} async-done(((f32[256,1024]{1,0:T(8,128)}), f32[256,1024]{1,0:T(8,128)}) %all-reduce.10.cloned.1.call-update) | async-done | bytes 1048592
  1066.1 0.9 multiply_reduce_fusion.2
  1067.0 10.4 all-reduce.3
  1077.4 1.0 multiply_reduce_fusion.1
  1078.4 7.7 psum.30
  1086.1 0.7 multiply_add_fusion.1
  1086.8 0.0 all-gather.14.cloned.1.call-start
  1086.9 126.6 %all-gather.20.cloned.1.call-done = f32[128,2,1024]{2,1,0:T(2,128)} async-done(((f32[1,2,1024]{2,1,0:T(2,128)}), f32[128,2,1024]{2,1,0:T(2,128)}) %all-gather.20.cloned.1.call-update) | async-done | bytes 1048592 | tf_op jit(solution)/shard_map/all_gather | solution.py:24
  1213.5 2.9 reshape.12
  1216.5 51.7 %all-gather.14.cloned.1.call-done = f32[256,4096]{1,0:T(8,128)} async-done(((f32[256,1024]{1,0:T(8,128)}), f32[256,4096]{1,0:T(8,128)}) %all-gather.14.cloned.1.call-update) | async-done | bytes 4194320 | tf_op jit(solution)/shard_map/all_gather | solution.py:25
  1268.2 3.9 fusion
  1272.1 335.7 %all-reduce.12.cloned.1.call-done = f32[256,1024]{1,0:T(8,128)} async-done(((f32[256,1024]{1,0:T(8,128)}), f32[256,1024]{1,0:T(8,128)}) %all-reduce.12.cloned.1.call-update) | async-done | bytes 1048592
  1607.9 0.9 multiply_reduce_fusion
  1608.7 10.4 psum.31
  1619.2 1.4 multiply_subtract_fusion
  (24 shorter events, 0.3 us)
Async XLA Ops:
  7.2 193.6 %copy-start = (f32[1,1024,512]{2,1,0:T(8,128)S(1)}, f32[1,1024,512]{2,1,0:T(8,128)}, u32[]{:S(2)}) copy-start(f32[1,1024,512]{2,1,0:T(8,128)} %param.3) | copy-start | bytes 6291460
  7.2 138.9 %all-gather.16.cloned.1.call-start = ((), (), s32[]{:S(2)}) async-start(), calls=%async_computation.3 | async-start | bytes 1056768 | tf_op jit(solution)/shard_map/all_gather | solution.py:24
  7.9 192.8 %all-gather.10.cloned.1.call-start = ((), (), s32[]{:S(2)}) async-start(), calls=%async_computation | async-start | bytes 5242880 | tf_op jit(solution)/shard_map/all_gather | solution.py:25
  149.0 391.4 %all-reduce.8.cloned.1.call-start = ((), (), s32[]{:S(2)}) async-start(), calls=%async_computation.6 | async-start | bytes 2097152
  149.0 391.3 %copy-start.4 = (f32[2,1024]{1,0:T(2,128)S(1)}, f32[2,1024]{1,0:T(2,128)}, u32[]{:S(2)}) copy-start(f32[2,1024]{1,0:T(2,128)} %param.4) | copy-start | bytes 24580
  204.7 467.0 %all-gather.18.cloned.1.call-start = ((), (), s32[]{:S(2)}) async-start(), calls=%async_computation.4 | async-start | bytes 1056768 | tf_op jit(solution)/shard_map/all_gather | solution.py:24
  541.7 184.6 %all-gather.12.cloned.1.call-start = ((), (), s32[]{:S(2)}) async-start(), calls=%async_computation.1 | async-start | bytes 5242880 | tf_op jit(solution)/shard_map/all_gather | solution.py:25
  674.6 391.5 %copy-start.1 = (f32[2,1024]{1,0:T(2,128)S(1)}, f32[2,1024]{1,0:T(2,128)}, u32[]{:S(2)}) copy-start(f32[2,1024]{1,0:T(2,128)} %dynamic-slice_subtract_fusion) | copy-start | bytes 24580
  674.6 391.5 %all-reduce.10.cloned.1.call-start = ((), (), s32[]{:S(2)}) async-start(), calls=%async_computation.7 | async-start | bytes 2097152
  730.3 483.1 %all-gather.20.cloned.1.call-start = ((), (), s32[]{:S(2)}) async-start(), calls=%async_computation.5 | async-start | bytes 1056768 | tf_op jit(solution)/shard_map/all_gather | solution.py:24
  1086.8 181.3 %all-gather.14.cloned.1.call-start = ((), (), s32[]{:S(2)}) async-start(), calls=%async_computation.2 | async-start | bytes 5242880 | tf_op jit(solution)/shard_map/all_gather | solution.py:25
  1216.4 391.4 %copy-start.2 = (f32[2,1024]{1,0:T(2,128)S(1)}, f32[2,1024]{1,0:T(2,128)}, u32[]{:S(2)}) copy-start(f32[2,1024]{1,0:T(2,128)} %multiply_add_fusion.1) | copy-start | bytes 24580
  1216.4 402.7 %copy-start.3 = (f32[2,1024]{1,0:T(2,128)S(1)}, f32[2,1024]{1,0:T(2,128)}, u32[]{:S(2)}) copy-start(f32[2,1024]{1,0:T(2,128)} %param.5) | copy-start | bytes 24580
  1216.4 391.4 %all-reduce.12.cloned.1.call-start = ((), (), s32[]{:S(2)}) async-start(), calls=%async_computation.8 | async-start | bytes 2097152
Sparse Core Ops, SparseCore 0:
  11.0 135.0 all-gather.15
  149.1 51.5 all-gather.9
  204.8 335.4 all-reduce.7
  544.2 127.4 all-gather.17
  674.7 51.5 all-gather.11
  730.4 335.5 all-reduce.9
  1087.0 126.4 all-gather.19
  1216.5 51.5 all-gather.13
  1272.2 335.5 all-reduce.11
where the time goes:
time: 1630 us
  waiting for transfers between devices  1560 us (96%)
  blocking collectives  28.6 us (2%)
    unnamed x12, waiting for transfers between devices  1010 us
    all_gather x3, waiting for transfers between devices, partial_terms(): columns = lax.all_gather(vector, ('mp', 'tcol'), axis=0, tiled=True)  395 us
    all_gather x3, waiting for transfers between devices, partial_terms(): gathered = lax.all_gather(columns, 'trow', axis=1, tiled=True)  155 us
  transfers between devices with their start and end apart: 9, of which 9 were waited for; matrix products, arithmetic and copies ran while one was open for 0% of the time, Pallas kernels for 0%

commit v1 on v0

v1 whole, which is shorter than its diff:
```python
import jax
import jax.numpy as jnp
from jax import lax
from jax.sharding import Mesh, PartitionSpec as P

MP = ("zh", "zl")
PLANE = ("trow", "tcol")
HIGHEST = lax.Precision.HIGHEST


def dot(lhs, rhs, lhs_dim, rhs_dim):
    return lax.dot_general(
        lhs,
        rhs,
        (((lhs_dim,), (rhs_dim,)), ((), ())),
        precision=HIGHEST,
        preferred_element_type=jnp.float32,
    )


def exchange(pieces, axes):
    return lax.all_to_all(pieces, axes, 0, 0, tiled=True)


def spread(block, axes, count):
    return exchange(jnp.broadcast_to(block[None], (count,) + block.shape), axes)


def transposed(vector, sizes):
    trow, tcol = sizes["trow"], sizes["tcol"]
    own, wide = vector.shape
    half = wide // 2
    core = lax.axis_index("tcol") % 2
    halves = (vector[:, :half], vector[:, half:])
    got = []
    for turn in range(2):
        pairs = []
        for i in range(trow):
            for j in range(tcol):
                q, h = j // 2, j % 2
                pairs.append((i * tcol + j, q * tcol + 2 * i + (h ^ turn)))
        low = core == turn
        sent = jnp.where(low, halves[0], halves[1])
        got.append(lax.ppermute(sent, PLANE, pairs))
    first = core == 0
    return jnp.stack([jnp.where(first, got[0], got[1]), jnp.where(first, got[1], got[0])])


def shards(sizes, gram, rhs, guess):
    zh, zl, trow, tcol = sizes["zh"], sizes["zl"], sizes["trow"], sizes["tcol"]
    mp = zh * zl
    tile = gram[0]
    rows, cols = tile.shape
    own = rhs.shape[0]
    thin = cols // zh

    cut = tile.reshape(zl, rows // zl, zh, thin).transpose(2, 0, 1, 3).reshape(mp * (rows // zl), thin)
    part = lax.psum_scatter(cut, MP, scatter_dimension=0, tiled=True)
    total = lax.all_gather(part, "zl", axis=0, tiled=True)

    flipped = transposed(guess, sizes)
    over_mp = spread(flipped, MP, mp)
    over_mp = over_mp.transpose(1, 0, 2, 3).reshape(2 * mp * own, cols)
    block = spread(over_mp, "trow", trow).reshape(trow * 2 * mp * own, cols)
    terms = dot(block, tile, 1, 1)
    terms = exchange(terms.reshape(tcol, mp * own, rows), "tcol").sum(0)
    terms = exchange(terms.reshape(mp, own, rows), MP).sum(0)
    first = rhs - terms

    near = spread(first, "zh", zh).reshape(zh * own, rows)
    wide = spread(near, "tcol", tcol).reshape(tcol * zh * own, rows)
    second = spread(dot(wide, total, 1, 0), "trow", trow).sum(0)
    terms = dot(second, total, 1, 1)
    pieces = jnp.concatenate([terms, second], axis=1).reshape(tcol, zh * own, rows + thin)
    pieces = exchange(pieces, "tcol")
    terms = pieces[:, :, :rows].sum(0)
    mine = lax.dynamic_slice(
        pieces, (2 * lax.axis_index("trow"), 0, rows), (2, zh * own, thin)
    )
    pieces = jnp.concatenate([terms, mine[0], mine[1]], axis=1).reshape(zh, own, rows + 2 * thin)
    pieces = exchange(pieces, "zh")
    third = pieces[:, :, :rows].sum(0)
    second = pieces[:, :, rows:].reshape(zh, own, 2, thin).transpose(1, 2, 0, 3).reshape(own, rows)

    def norm(v):
        return jnp.sqrt(jnp.sum(v * v, axis=1))

    def inverse(x):
        return jnp.where(x > 0, 1.0 / jnp.where(x > 0, x, 1.0), 0.0)

    f0 = norm(first)
    e0 = first * inverse(f0)[:, None]
    s0 = jnp.sum(e0 * second, axis=1)
    rest = second - s0[:, None] * e0
    s1 = norm(rest)
    e1 = rest * inverse(s1)[:, None]
    t0 = jnp.sum(e0 * third, axis=1)
    t1 = jnp.sum(e1 * (third - t0[:, None] * e0), axis=1)
    f0, s0, s1, t0, t1 = jnp.moveaxis(spread(jnp.stack([f0, s0, s1, t0, t1]), "trow", trow), 1, 0)

    norm_first = jnp.sum(f0 * f0, 0)
    alpha = norm_first / jnp.sum(f0 * s0, 0)
    r0, r1 = f0 - alpha * s0, -alpha * s1
    norm_next = jnp.sum(r0 * r0 + r1 * r1, 0)
    beta = norm_next / norm_first
    d0, d1 = r0 + beta * f0, r1
    i0, i1 = s0 - alpha * t0 + beta * s0, s1 - alpha * t1 + beta * s1
    alpha_next = norm_next / jnp.sum(d0 * i0 + d1 * i1, 0)

    alpha, beta, alpha_next = alpha[:, None], beta[:, None], alpha_next[:, None]
    residual = first - alpha * second
    direction = residual + beta * first
    image = second - alpha * third + beta * second
    merged = guess + alpha * first + alpha_next * direction
    return merged, residual - alpha_next * image


def solution(mesh):
    mp, trow, tcol = (mesh.shape[a] for a in ("mp", "trow", "tcol"))
    zl = 4 if mp % 4 == 0 and mp > 4 else 2
    sizes = {"zh": mp // zl, "zl": zl, "trow": trow, "tcol": tcol}
    split = Mesh(mesh.devices.reshape(tuple(sizes.values())), tuple(sizes))
    in_specs = (P(MP, "trow", "tcol"), P(MP + ("tcol",), "trow"), P(MP + ("tcol",), "trow"))
    out_specs = (P(MP + ("tcol",), "trow"), P(MP + ("tcol",), "trow"))

    def body(gram, rhs, guess):
        return shards(sizes, gram, rhs, guess)

    return jax.shard_map(body, mesh=split, in_specs=in_specs, out_specs=out_specs, check_vma=False)
```

time: 1630 us -> 203 us (0.12)
  the two profiles are of different devices: /device:TPU:8 before, /device:TPU:32 now
where the time goes in v1:
time: 203 us; the launch traced here: 202 us
  blocking collectives  139 us (68%)
  waiting for transfers between devices  21.7 us (11%)
  between operations  14.3 us (7%)
  starting transfers between devices  14 us (7%)
  local copies, waits for them, and re-layouts  6.45 us (3%)
  other arithmetic  3.55 us (2%)
  matrix products  3.02 us (1%)
    all_to_all x7, blocking collectives, exchange(): return lax.all_to_all(pieces, axes, 0, 0, tiled=True)  122 us
    all_to_all x3, waiting for transfers between devices, exchange(): return lax.all_to_all(pieces, axes, 0, 0, tiled=True)  20.6 us
    all_gather x1, blocking collectives, shards(): total = lax.all_gather(part, 'zl', axis=0, tiled=True)  16.4 us
    all_to_all x3, starting transfers between devices, exchange(): return lax.all_to_all(pieces, axes, 0, 0, tiled=True)  11.4 us
  transfers between devices with their start and end apart: 6, of which 3 were waited for; matrix products, arithmetic and copies ran while one was open for 2% of the time, Pallas kernels for 0%

profile of v1, /device:TPU:32, one launch (start us, length us, event | category | flops | bytes accessed | tf_op | source)
XLA Modules:
  0.0 201.9 jit_solution(11589484859543571213)
XLA Ops:
  7.2 1.9 reshape_squeeze.3
  9.2 1.6 copy.47
  10.8 0.7 copy-done.1
  11.4 0.6 collective-permute-start
  12.1 1.9 collective-permute-start.1
  14.0 1.1 collective-permute-done.1
  15.2 30.3 %all_to_all.50 = f32[16,2,2,512]{3,2,1,0:T(2,128)S(1)} all-to-all(f32[16,2,2,512]{3,2,1,0:T(2,128)S(1)} %broadcast_in_dim.21), channel_id=1, replica_groups=mesh['zh'=4,'zl'=4,'trow'=4,'tcol'=8] {'zh','zl'}, dimensions={0} | all-to-all | bytes 262144 | tf_op jit(solution)/shard_map/all_to_all | solution.py:22
  45.7 21.8 %all_to_all.51 = f32[4,64,512]{2,1,0:T(8,128)S(1)} all-to-all(f32[4,64,512]{2,1,0:T(8,128)S(1)} %broadcast_in_dim.23), channel_id=1, replica_groups=mesh['zh'=4,'zl'=4,'trow'=4,'tcol'=8] {'trow'}, dimensions={0} | all-to-all | bytes 1048576 | tf_op jit(solution)/shard_map/all_to_all | solution.py:22
  67.5 1.9 fusion
  69.5 18.5 %all_to_all.52 = f32[8,32,1024]{2,1,0:T(8,128)S(1)} all-to-all(f32[8,32,1024]{2,1,0:T(8,128)S(1)} %fusion), channel_id=1, replica_groups=mesh['zh'=4,'zl'=4,'trow'=4,'tcol'=8] {'tcol'}, dimensions={0} | all-to-all | bytes 2097152 | tf_op jit(solution)/shard_map/all_to_all | solution.py:22
  88.1 19.7 %all_to_all.53 = f32[16,2,1024]{2,1,0:T(2,128)S(1)} all-to-all(f32[16,2,1024]{2,1,0:T(2,128)S(1)} %reshape.100), channel_id=1, replica_groups=mesh['zh'=4,'zl'=4,'trow'=4,'tcol'=8] {'zh','zl'}, dimensions={0} | all-to-all | bytes 262144 | tf_op jit(solution)/shard_map/all_to_all | solution.py:22
  108.0 16.2 %all_to_all.54 = f32[4,2,1024]{2,1,0:T(2,128)S(1)} all-to-all(f32[4,2,1024]{2,1,0:T(2,128)S(1)} %broadcast_in_dim.24), channel_id=1, replica_groups=mesh['zh'=4,'zl'=4,'trow'=4,'tcol'=8] {'zh'}, dimensions={0} | all-to-all | bytes 65536 | tf_op jit(solution)/shard_map/all_to_all | solution.py:22
  124.2 0.7 broadcast_in_dim.26
  124.9 3.4 %all-to-all-start.5 = ((f32[8,8,1024]{2,1,0:T(8,128)}), f32[8,8,1024]{2,1,0:T(8,128)S(1)}, u32[]{:S(2)}, u32[]{:S(2)}) async-start(f32[8,8,1024]{2,1,0:T(8,128)} %broadcast_in_dim.26), calls=%async_computation.5 | async-start | bytes 524288 | tf_op jit(solution)/shard_map/all_to_all | solution.py:22
  128.4 16.4 %all_gather.3 = f32[1024,128]{1,0:T(8,128)S(1)} all-gather(f32[256,128]{1,0:T(8,128)} %reduce-scatter.2.cloned.1.call-done), channel_id=1, replica_groups=mesh['zh'=4,'zl'=4,'trow'=4,'tcol'=8] {'zl'}, dimensions={0}, use_global_device_ids=true | all-gather | bytes 655360 | tf_op jit(solution)/shard_map/all_gather | solution.py:59
  144.8 0.4 fusion.2
  145.3 8.4 %all_to_all.55 = f32[4,64,128]{2,1,0:T(8,128)S(1)} all-to-all(f32[4,64,128]{2,1,0:T(8,128)S(1)} %broadcast_in_dim.27), channel_id=1, replica_groups=mesh['zh'=4,'zl'=4,'trow'=4,'tcol'=8] {'trow'}, dimensions={0} | all-to-all | bytes 262144 | tf_op jit(solution)/shard_map/all_to_all | solution.py:22
  153.6 0.7 fusion.21
  154.3 0.7 maximum_bitcast_fusion
  155.0 4.7 %all-to-all-start.7 = ((f32[8,8,1152]{2,1,0:T(8,128)}), f32[8,8,1152]{2,1,0:T(8,128)S(1)}, u32[]{:S(2)}, u32[]{:S(2)}) async-start(f32[8,8,1152]{2,1,0:T(8,128)} %maximum_bitcast_fusion), calls=%async_computation.8 | async-start | bytes 589824 | tf_op jit(solution)/shard_map/all_to_all | solution.py:22
  159.8 7.9 %all-to-all-done.7 = f32[8,8,1152]{2,1,0:T(8,128)S(1)} async-done(((f32[8,8,1152]{2,1,0:T(8,128)}), f32[8,8,1152]{2,1,0:T(8,128)S(1)}, u32[]{:S(2)}, u32[]{:S(2)}) %all-to-all-start.7) | async-done | bytes 294944 | tf_op jit(solution)/shard_map/all_to_all | solution.py:22
  167.7 0.6 pad_maximum_fusion
  168.4 3.3 %all-to-all-start.8 = ((f32[4,2,1280]{2,1,0:T(2,128)}), f32[4,2,1280]{2,1,0:T(2,128)S(1)}, u32[]{:S(2)}, u32[]{:S(2)}) async-start(f32[4,2,1280]{2,1,0:T(2,128)} %pad_maximum_fusion), calls=%async_computation.9 | async-start | bytes 81920 | tf_op jit(solution)/shard_map/all_to_all | solution.py:22
  171.8 12.7 %all-to-all-done.8 = f32[4,2,1280]{2,1,0:T(2,128)S(1)} async-done(((f32[4,2,1280]{2,1,0:T(2,128)}), f32[4,2,1280]{2,1,0:T(2,128)S(1)}, u32[]{:S(2)}, u32[]{:S(2)}) %all-to-all-start.8) | async-done | bytes 40992 | tf_op jit(solution)/shard_map/all_to_all | solution.py:22
  184.5 0.2 multiply_reduce_fusion.3
  184.8 0.2 multiply_reduce_fusion.1
  185.2 0.2 multiply_reduce_fusion
  185.6 7.6 %all_to_all.56 = f32[4,5,2]{1,2,0:T(2,128)S(1)} all-to-all(f32[4,5,2]{1,2,0:T(2,128)S(1)} %broadcast_in_dim.28), channel_id=1, replica_groups=mesh['zh'=4,'zl'=4,'trow'=4,'tcol'=8] {'trow'}, dimensions={0} | all-to-all | bytes 320 | tf_op jit(solution)/shard_map/all_to_all | solution.py:22
  193.6 0.2 fusion.14
  193.8 0.2 fusion.13
  194.2 0.2 fusion.18
  194.4 0.7 multiply_subtract_fusion
  (51 shorter events, 2.0 us)
Async XLA Ops:
  7.2 121.2 %reduce-scatter.2.cloned.1.call-start = ((), (), s32[]{:S(2)}) async-start(), calls=%async_computation.11 | async-start | bytes 2228224 | tf_op jit(solution)/shard_map/reduce_scatter | solution.py:58
  10.7 0.7 copy-start.1
  10.7 56.8 %copy-start = (f32[1,1024,512]{2,1,0:T(8,128)S(1)}, f32[1,1024,512]{2,1,0:T(8,128)}, u32[]{:S(2)}) copy-start(f32[1,1024,512]{2,1,0:T(8,128)} %param.3) | copy-start | bytes 6291460
  11.4 2.6 %collective-permute-start = (f32[2,512]{1,0:T(2,128)S(1)}, f32[2,512]{1,0:T(2,128)S(1)}, u32[]{:S(2)}, u32[]{:S(2)}) collective-permute-start(f32[2,512]{1,0:T(2,128)S(1)} %get-tuple-element.16), channel_id=1, source_target_pairs={{0,0},{1,1},{2,8},{3,9},{4,16},{5,17},{6,24},{7,25},{8,2},{9,3},{1... | collective-permute-start | bytes 12296 | tf_op jit(solution)/shard_map/ppermute | solution.py:44
  12.1 3.1 %collective-permute-start.1 = (f32[2,512]{1,0:T(2,128)S(1)}, f32[2,512]{1,0:T(2,128)S(1)}, u32[]{:S(2)}, u32[]{:S(2)}) collective-permute-start(f32[2,512]{1,0:T(2,128)S(1)} %get-tuple-element.17), channel_id=1, source_target_pairs={{0,1},{1,0},{2,9},{3,8},{4,17},{5,16},{6,25},{7,24},{8,3},{9,2},{1... | collective-permute-start | bytes 12296 | tf_op jit(solution)/shard_map/ppermute | solution.py:44
  69.5 38.4 %copy-start.2 = (f32[2,1024]{1,0:T(2,128)S(1)}, f32[2,1024]{1,0:T(2,128)}, u32[]{:S(2)}) copy-start(f32[2,1024]{1,0:T(2,128)} %param.4) | copy-start | bytes 24580
  124.9 19.9 %all-to-all-start.5 = ((f32[8,8,1024]{2,1,0:T(8,128)}), f32[8,8,1024]{2,1,0:T(8,128)S(1)}, u32[]{:S(2)}, u32[]{:S(2)}) async-start(f32[8,8,1024]{2,1,0:T(8,128)} %broadcast_in_dim.26), calls=%async_computation.5 | async-start | bytes 524288 | tf_op jit(solution)/shard_map/all_to_all | solution.py:22
  155.0 12.6 %all-to-all-start.7 = ((f32[8,8,1152]{2,1,0:T(8,128)}), f32[8,8,1152]{2,1,0:T(8,128)S(1)}, u32[]{:S(2)}, u32[]{:S(2)}) async-start(f32[8,8,1152]{2,1,0:T(8,128)} %maximum_bitcast_fusion), calls=%async_computation.8 | async-start | bytes 589824 | tf_op jit(solution)/shard_map/all_to_all | solution.py:22
  168.4 16.1 %all-to-all-start.8 = ((f32[4,2,1280]{2,1,0:T(2,128)}), f32[4,2,1280]{2,1,0:T(2,128)S(1)}, u32[]{:S(2)}, u32[]{:S(2)}) async-start(f32[4,2,1280]{2,1,0:T(2,128)} %pad_maximum_fusion), calls=%async_computation.9 | async-start | bytes 81920 | tf_op jit(solution)/shard_map/all_to_all | solution.py:22
Sparse Core Ops, SparseCore 0:
  10.9 80.2 reduce-scatter.1

commit v2 on v1

v2 whole, which is shorter than its diff:
```python
import jax
import jax.numpy as jnp
from jax import lax
from jax.sharding import Mesh, PartitionSpec as P

MP = ("zk", "zb")
PLANE = ("trow", "tcol")
SHARD = ("trow", "zb")
HIGHEST = lax.Precision.HIGHEST


def dot(lhs, rhs, lhs_dim, rhs_dim):
    return lax.dot_general(
        lhs,
        rhs,
        (((lhs_dim,), (rhs_dim,)), ((), ())),
        precision=HIGHEST,
        preferred_element_type=jnp.float32,
    )


def exchange(pieces, axes):
    return lax.all_to_all(pieces, axes, 0, 0, tiled=True)


def spread(block, axes, count):
    return exchange(jnp.broadcast_to(block[None], (count,) + block.shape), axes)


def ordered(flag, mine, other):
    return jnp.where(flag == 0, mine, other), jnp.where(flag == 0, other, mine)


def transposed(vector, sizes):
    trow, tcol = sizes["trow"], sizes["tcol"]
    half = vector.shape[1] // 2
    core = lax.axis_index("tcol") % 2
    halves = (vector[:, :half], vector[:, half:])
    got = []
    for turn in range(2):
        pairs = []
        for i in range(trow):
            for j in range(tcol):
                q, h = j // 2, j % 2
                pairs.append((i * tcol + j, q * tcol + 2 * i + (h ^ turn)))
        sent = jnp.where(core == turn, halves[0], halves[1])
        got.append(lax.ppermute(sent, PLANE, pairs))
    return jnp.stack(ordered(core, got[0], got[1]))


def shards(sizes, gram, rhs, guess):
    zk, zb, trow, tcol = sizes["zk"], sizes["zb"], sizes["trow"], sizes["tcol"]
    mp = zk * zb
    tile = gram[0]
    rows, cols = tile.shape
    own = rhs.shape[0]
    part_rows = rows // zb
    half = lax.axis_index("zb")

    cut = tile.reshape(zb, zk, part_rows // zk, cols).transpose(1, 0, 2, 3).reshape(rows, cols)
    part = lax.psum_scatter(cut, MP, scatter_dimension=0, tiled=True)
    total = lax.all_gather(part, "zk", axis=0, tiled=True)

    flipped = transposed(guess, sizes)
    over_mp = spread(flipped, MP, mp)
    over_mp = over_mp.transpose(1, 0, 2, 3).reshape(2 * mp * own, cols)
    block = spread(over_mp, "trow", trow).reshape(trow * 2 * mp * own, cols)
    terms = dot(block, tile, 1, 1)
    terms = exchange(terms.reshape(tcol, mp * own, rows), "tcol").sum(0)
    terms = exchange(terms.reshape(mp, own, rows), MP).sum(0)
    first = rhs - terms

    def halves(vector):
        low, high = vector[:, :part_rows], vector[:, part_rows:]
        return jnp.where(half == 0, low, high), jnp.where(half == 0, high, low)

    kept, given = halves(first)
    got = lax.ppermute(given, "zb", [(0, 1), (1, 0)])
    near = jnp.concatenate(ordered(half, kept, got))
    wide = spread(near, "tcol", tcol).reshape(tcol * zb * own, part_rows)
    second = spread(dot(wide, total, 1, 0), SHARD, trow * zb).sum(0)
    terms = dot(second, total, 1, 1)
    pieces = jnp.concatenate([terms, second], axis=1).reshape(tcol, zb * own, part_rows + cols)
    pieces = exchange(pieces, "tcol")
    third = pieces[:, :, :part_rows].sum(0)
    second = lax.dynamic_slice(
        pieces, (2 * lax.axis_index("trow"), 0, part_rows), (2, zb * own, cols)
    )
    second = jnp.concatenate([second[0], second[1]], axis=1)

    def inner(u, v):
        return jnp.sum(u * v, axis=1, keepdims=True)

    def inverse(x):
        return jnp.where(x > 0, 1.0 / jnp.where(x > 0, x, 1.0), 0.0)

    here, _ = halves(second)
    f0 = jnp.sqrt(inner(near, near))
    e0 = near * inverse(f0)
    s0 = inner(e0, here)
    rest = here - s0 * e0
    s1 = jnp.sqrt(inner(rest, rest))
    e1 = rest * inverse(s1)
    t0 = inner(e0, third)
    t1 = inner(e1, third - t0 * e0)
    known = jnp.concatenate([third, jnp.pad(jnp.concatenate([f0, s0, s1, t0, t1], axis=1), ((0, 0), (0, 123)))], axis=1)
    wide_known = part_rows + 128
    pieces = jnp.broadcast_to(known[None], (trow,) + known.shape).reshape(trow * zb, own, wide_known)
    pieces = exchange(pieces, SHARD)
    f0, s0, s1, t0, t1 = (pieces[:, :, part_rows + n : part_rows + n + 1] for n in range(5))
    third = lax.dynamic_slice(
        pieces, (zb * lax.axis_index("trow"), 0, 0), (zb, own, part_rows)
    )
    third = jnp.concatenate([third[0], third[1]], axis=1)
    second = jnp.where(half == 0, second[:own], second[own:])

    norm_first = jnp.sum(f0 * f0, 0)
    alpha = norm_first / jnp.sum(f0 * s0, 0)
    r0, r1 = f0 - alpha * s0, -alpha * s1
    norm_next = jnp.sum(r0 * r0 + r1 * r1, 0)
    beta = norm_next / norm_first
    d0, d1 = r0 + beta * f0, r1
    i0, i1 = s0 - alpha * t0 + beta * s0, s1 - alpha * t1 + beta * s1
    alpha_next = norm_next / jnp.sum(d0 * i0 + d1 * i1, 0)

    residual = first - alpha * second
    direction = residual + beta * first
    image = second - alpha * third + beta * second
    merged = guess + alpha * first + alpha_next * direction
    return merged, residual - alpha_next * image


def solution(mesh):
    mp, trow, tcol = (mesh.shape[a] for a in ("mp", "trow", "tcol"))
    sizes = {"zk": mp // 2, "zb": 2, "trow": trow, "tcol": tcol}
    split = Mesh(mesh.devices.reshape(tuple(sizes.values())), tuple(sizes))
    in_specs = (P(MP, "trow", "tcol"), P(MP + ("tcol",), "trow"), P(MP + ("tcol",), "trow"))
    out_specs = (P(MP + ("tcol",), "trow"), P(MP + ("tcol",), "trow"))

    def body(gram, rhs, guess):
        return shards(sizes, gram, rhs, guess)

    return jax.shard_map(body, mesh=split, in_specs=in_specs, out_specs=out_specs, check_vma=False)
```

time: 203 us -> 194 us (0.956)
  the two profiles are of different devices: /device:TPU:32 before, /device:TPU:1 now
where the time goes in v2:
time: 194 us; the launch traced here: 193 us
  blocking collectives  68.8 us (35%)
  waiting for transfers between devices  52.3 us (27%)
  starting transfers between devices  41.5 us (21%)
  between operations  14.3 us (7%)
  local copies, waits for them, and re-layouts  7.5 us (4%)
  matrix products  5.97 us (3%)
  other arithmetic  2.89 us (1%)
    all_to_all x4, blocking collectives, exchange(): return lax.all_to_all(pieces, axes, 0, 0, tiled=True)  68.8 us
    all_to_all x4, waiting for transfers between devices, exchange(): return lax.all_to_all(pieces, axes, 0, 0, tiled=True)  32.3 us
    all_to_all x4, starting transfers between devices, exchange(): return lax.all_to_all(pieces, axes, 0, 0, tiled=True)  29.1 us
    all_gather x1, waiting for transfers between devices, shards(): total = lax.all_gather(part, 'zk', axis=0, tiled=True)  9.67 us
    ppermute x2, starting transfers between devices, transposed(): got.append(lax.ppermute(sent, PLANE, pairs))  9.44 us
    reduce_scatter x1, waiting for transfers between devices, shards(): part = lax.psum_scatter(cut, MP, scatter_dimension=0, tiled=True)  7.61 us
    dot_general x3, matrix products, dot(): lax.dot_general(lhs, rhs, (((lhs_dim,), (rhs_dim,)), ((), ())), precision...  5.97 us
  transfers between devices with their start and end apart: 9, of which 8 were waited for; matrix products, arithmetic and copies ran while one was open for 2% of the time, Pallas kernels for 0%

profile of v2, /device:TPU:1, one launch (start us, length us, event | category | flops | bytes accessed | tf_op | source)
XLA Modules:
  0.0 193.3 jit_solution(9477022793621613023)
XLA Ops:
  7.2 3.2 %copy.69 = f32[8,2,64,512]{3,2,1,0:T(8,128)} copy(f32[8,2,64,512]{3,2,0,1:T(8,128)} %bitcast.36) | data formatting | bytes 4194304 | tf_op jit(solution)/shard_map/transpose | solution.py:60
  10.4 0.7 copy-done.2
  11.1 0.6 collective-permute-start
  11.7 8.8 %collective-permute-start.1 = (f32[2,512]{1,0:T(2,128)S(1)}, f32[2,512]{1,0:T(2,128)S(1)}, u32[]{:S(2)}, u32[]{:S(2)}) collective-permute-start(f32[2,512]{1,0:T(2,128)S(1)} %get-tuple-element.32), channel_id=1, source_target_pairs={{0,1},{1,0},{2,9},{3,8},{4,17},{5,16},{6,25},{7,24},{8,3},{9,2},{1... | collective-permute-start | bytes 12296 | tf_op jit(solution)/shard_map/ppermute | solution.py:47
  20.6 0.8 collective-permute-done.1
  21.4 21.5 %all_to_all.40 = f32[16,2,2,512]{3,2,1,0:T(2,128)S(1)} all-to-all(f32[16,2,2,512]{3,2,1,0:T(2,128)S(1)} %broadcast_in_dim.23), channel_id=1, replica_groups=mesh['zk'=8,'zb'=2,'trow'=4,'tcol'=8] {'zk','zb'}, dimensions={0} | all-to-all | bytes 262144 | tf_op jit(solution)/shard_map/all_to_all | solution.py:23
  43.1 20.6 %all_to_all.41 = f32[4,64,512]{2,1,0:T(8,128)S(1)} all-to-all(f32[4,64,512]{2,1,0:T(8,128)S(1)} %broadcast_in_dim.25), channel_id=1, replica_groups=mesh['zk'=8,'zb'=2,'trow'=4,'tcol'=8] {'trow'}, dimensions={0} | all-to-all | bytes 1048576 | tf_op jit(solution)/shard_map/all_to_all | solution.py:23
  63.7 2.9 %fusion = f32[8,32,1024]{2,1,0:T(8,128)} fusion(f32[8,32,512]{2,1,0:T(8,128)S(1)} %bitcast.38, f32[1,1024,512]{2,1,0:T(8,128)S(1)} %copy-done), kind=kOutput, calls=%fused_computation | convolution fusion | flops 1610612736 | bytes 3670016 | tf_op jit(solution)/shard_map/dot_general | solution.py:13
  66.6 8.8 %all-to-all-start.2 = ((f32[8,32,1024]{2,1,0:T(8,128)}), f32[8,32,1024]{2,1,0:T(8,128)S(1)}, u32[]{:S(2)}, u32[]{:S(2)}) async-start(f32[8,32,1024]{2,1,0:T(8,128)} %fusion), calls=%async_computation.2 | async-start | bytes 2097152 | tf_op jit(solution)/shard_map/all_to_all | solution.py:23
  75.4 7.6 %reduce-scatter.2.cloned.1.call-done = f32[64,512]{1,0:T(8,128)} async-done(((f32[1024,512]{1,0:T(8,128)}), f32[64,512]{1,0:T(8,128)}) %reduce-scatter.2.cloned.1.call-update) | async-done | bytes 131088 | tf_op jit(solution)/shard_map/reduce_scatter | solution.py:61
  83.0 7.5 %all-to-all-done.2 = f32[8,32,1024]{2,1,0:T(8,128)S(1)} async-done(((f32[8,32,1024]{2,1,0:T(8,128)}), f32[8,32,1024]{2,1,0:T(8,128)S(1)}, u32[]{:S(2)}, u32[]{:S(2)}) %all-to-all-start.2) | async-done | bytes 1048608 | tf_op jit(solution)/shard_map/all_to_all | solution.py:23
  90.6 0.7 reshape.118
  91.3 5.5 %all-to-all-start.3 = ((f32[16,2,1024]{2,1,0:T(2,128)}), f32[16,2,1024]{2,1,0:T(2,128)S(1)}, u32[]{:S(2)}, u32[]{:S(2)}) async-start(f32[16,2,1024]{2,1,0:T(2,128)} %reshape.118), calls=%async_computation.3 | async-start | bytes 262144 | tf_op jit(solution)/shard_map/all_to_all | solution.py:23
  96.8 12.1 %all-to-all-done.3 = f32[16,2,1024]{2,1,0:T(2,128)S(1)} async-done(((f32[16,2,1024]{2,1,0:T(2,128)}), f32[16,2,1024]{2,1,0:T(2,128)S(1)}, u32[]{:S(2)}, u32[]{:S(2)}) %all-to-all-start.3) | async-done | bytes 131104 | tf_op jit(solution)/shard_map/all_to_all | solution.py:23
  108.9 2.8 %collective-permute-start.2 = (f32[2,512]{1,0:T(2,128)S(1)}, f32[2,512]{1,0:T(2,128)S(1)}, u32[]{:S(2)}, u32[]{:S(2)}) collective-permute-start(f32[2,512]{1,0:T(2,128)S(1)} %broadcast_select_fusion.5), channel_id=1, source_target_pairs={{0,32},{32,0},{1,33},{33,1},{2,34},{34,2},{3,35},{35,3},{4,36},{36... | collective-permute-start | bytes 12296 | tf_op jit(solution)/shard_map/ppermute | solution.py:78
  111.8 2.0 %collective-permute-done.2 = f32[2,512]{1,0:T(2,128)S(1)} collective-permute-done((f32[2,512]{1,0:T(2,128)S(1)}, f32[2,512]{1,0:T(2,128)S(1)}, u32[]{:S(2)}, u32[]{:S(2)}) %collective-permute-start.2) | collective-permute-done | bytes 4128 | tf_op jit(solution)/shard_map/ppermute | solution.py:78
  113.9 19.2 %all_to_all.42 = f32[8,4,512]{2,1,0:T(4,128)S(1)} all-to-all(f32[8,4,512]{2,1,0:T(4,128)S(1)} %broadcast_in_dim.26), channel_id=1, replica_groups=mesh['zk'=8,'zb'=2,'trow'=4,'tcol'=8] {'tcol'}, dimensions={0} | all-to-all | bytes 131072 | tf_op jit(solution)/shard_map/all_to_all | solution.py:23
  133.1 9.7 %all-gather.2.cloned.1.call-done = f32[512,512]{1,0:T(8,128)} async-done(((f32[64,512]{1,0:T(8,128)}), f32[512,512]{1,0:T(8,128)}) %all-gather.2.cloned.1.call-update) | async-done | bytes 1048592 | tf_op jit(solution)/shard_map/all_gather | solution.py:62
  142.8 2.0 %fusion.11 = f32[32,512]{1,0:T(8,128)S(1)} fusion(f32[32,512]{1,0:T(8,128)S(1)} %reshape.119, f32[512,512]{1,0:T(8,128)} %all-gather.2.cloned.1.call-done), kind=kOutput, calls=%fused_computation.52 | convolution fusion | flops 100663296 | bytes 1179648 | tf_op jit(solution)/shard_map/dot_general | solution.py:13
  144.8 0.9 broadcast_in_dim.27
  145.7 3.7 %all-to-all-start.5 = ((f32[8,32,512]{2,1,0:T(8,128)}), f32[8,32,512]{2,1,0:T(8,128)S(1)}, u32[]{:S(2)}, u32[]{:S(2)}) async-start(f32[8,32,512]{2,1,0:T(8,128)} %broadcast_in_dim.27), calls=%async_computation.6 | async-start | bytes 1048576 | tf_op jit(solution)/shard_map/all_to_all | solution.py:23
  149.4 7.5 %all-to-all-done.5 = f32[8,32,512]{2,1,0:T(8,128)S(1)} async-done(((f32[8,32,512]{2,1,0:T(8,128)}), f32[8,32,512]{2,1,0:T(8,128)S(1)}, u32[]{:S(2)}, u32[]{:S(2)}) %all-to-all-start.5) | async-done | bytes 524320 | tf_op jit(solution)/shard_map/all_to_all | solution.py:23
  157.0 1.0 fusion.12
  158.1 0.7 reshape.121
  158.7 11.2 %all-to-all-start.6 = ((f32[8,4,1024]{2,1,0:T(4,128)}), f32[8,4,1024]{2,1,0:T(4,128)S(1)}, u32[]{:S(2)}, u32[]{:S(2)}) async-start(f32[8,4,1024]{2,1,0:T(4,128)} %reshape.121), calls=%async_computation.7 | async-start | bytes 262144 | tf_op jit(solution)/shard_map/all_to_all | solution.py:23
  170.1 5.2 %all-to-all-done.6 = f32[8,4,1024]{2,1,0:T(4,128)S(1)} async-done(((f32[8,4,1024]{2,1,0:T(4,128)}), f32[8,4,1024]{2,1,0:T(4,128)S(1)}, u32[]{:S(2)}, u32[]{:S(2)}) %all-to-all-start.6) | async-done | bytes 131104 | tf_op jit(solution)/shard_map/all_to_all | solution.py:23
  175.3 0.2 multiply_reduce_fusion.3
  175.5 0.2 multiply_reduce_fusion.1
  175.7 0.2 multiply_reduce_fusion
  176.4 7.5 %all_to_all.43 = f32[8,2,640]{2,1,0:T(2,128)S(1)} all-to-all(f32[8,2,640]{2,1,0:T(2,128)S(1)} %reshape.122), channel_id=1, replica_groups=mesh['zk'=8,'zb'=2,'trow'=4,'tcol'=8] {'trow','zb'}, dimensions={0} | all-to-all | bytes 81920 | tf_op jit(solution)/shard_map/all_to_all | solution.py:23
  185.1 0.7 fusion.7
  185.8 0.7 multiply_add_fusion
  (54 shorter events, 2.4 us)
Async XLA Ops:
  7.2 75.9 %reduce-scatter.2.cloned.1.call-start = ((), (), s32[]{:S(2)}) async-start(), calls=%async_computation.9 | async-start | bytes 2228224 | tf_op jit(solution)/shard_map/reduce_scatter | solution.py:61
  10.4 0.7 copy-start.2
  10.4 53.3 %copy-start = (f32[1,1024,512]{2,1,0:T(8,128)S(1)}, f32[1,1024,512]{2,1,0:T(8,128)}, u32[]{:S(2)}) copy-start(f32[1,1024,512]{2,1,0:T(8,128)} %param.3) | copy-start | bytes 6291460
  11.1 9.5 %collective-permute-start = (f32[2,512]{1,0:T(2,128)S(1)}, f32[2,512]{1,0:T(2,128)S(1)}, u32[]{:S(2)}, u32[]{:S(2)}) collective-permute-start(f32[2,512]{1,0:T(2,128)S(1)} %get-tuple-element.31), channel_id=1, source_target_pairs={{0,0},{1,1},{2,8},{3,9},{4,16},{5,17},{6,24},{7,25},{8,2},{9,3},{1... | collective-permute-start | bytes 12296 | tf_op jit(solution)/shard_map/ppermute | solution.py:47
  11.7 9.6 %collective-permute-start.1 = (f32[2,512]{1,0:T(2,128)S(1)}, f32[2,512]{1,0:T(2,128)S(1)}, u32[]{:S(2)}, u32[]{:S(2)}) collective-permute-start(f32[2,512]{1,0:T(2,128)S(1)} %get-tuple-element.32), channel_id=1, source_target_pairs={{0,1},{1,0},{2,9},{3,8},{4,17},{5,16},{6,25},{7,24},{8,3},{9,2},{1... | collective-permute-start | bytes 12296 | tf_op jit(solution)/shard_map/ppermute | solution.py:47
  66.6 42.3 %copy-start.3 = (f32[2,1024]{1,0:T(2,128)S(1)}, f32[2,1024]{1,0:T(2,128)}, u32[]{:S(2)}) copy-start(f32[2,1024]{1,0:T(2,128)} %param.4) | copy-start | bytes 24580
  66.6 23.9 %all-to-all-start.2 = ((f32[8,32,1024]{2,1,0:T(8,128)}), f32[8,32,1024]{2,1,0:T(8,128)S(1)}, u32[]{:S(2)}, u32[]{:S(2)}) async-start(f32[8,32,1024]{2,1,0:T(8,128)} %fusion), calls=%async_computation.2 | async-start | bytes 2097152 | tf_op jit(solution)/shard_map/all_to_all | solution.py:23
  75.4 67.4 %all-gather.2.cloned.1.call-start = ((), (), s32[]{:S(2)}) async-start(), calls=%async_computation.10 | async-start | bytes 1179648 | tf_op jit(solution)/shard_map/all_gather | solution.py:62
  91.3 17.5 %all-to-all-start.3 = ((f32[16,2,1024]{2,1,0:T(2,128)}), f32[16,2,1024]{2,1,0:T(2,128)S(1)}, u32[]{:S(2)}, u32[]{:S(2)}) async-start(f32[16,2,1024]{2,1,0:T(2,128)} %reshape.118), calls=%async_computation.3 | async-start | bytes 262144 | tf_op jit(solution)/shard_map/all_to_all | solution.py:23
  108.9 4.8 %collective-permute-start.2 = (f32[2,512]{1,0:T(2,128)S(1)}, f32[2,512]{1,0:T(2,128)S(1)}, u32[]{:S(2)}, u32[]{:S(2)}) collective-permute-start(f32[2,512]{1,0:T(2,128)S(1)} %broadcast_select_fusion.5), channel_id=1, source_target_pairs={{0,32},{32,0},{1,33},{33,1},{2,34},{34,2},{3,35},{35,3},{4,36},{36... | collective-permute-start | bytes 12296 | tf_op jit(solution)/shard_map/ppermute | solution.py:78
  142.8 14.2 %copy-start.1 = (f32[512,512]{1,0:T(8,128)S(1)}, f32[512,512]{1,0:T(8,128)}, u32[]{:S(2)}) copy-start(f32[512,512]{1,0:T(8,128)} %all-gather.2.cloned.1.call-done) | copy-start | bytes 3145732
  145.7 11.2 %all-to-all-start.5 = ((f32[8,32,512]{2,1,0:T(8,128)}), f32[8,32,512]{2,1,0:T(8,128)S(1)}, u32[]{:S(2)}, u32[]{:S(2)}) async-start(f32[8,32,512]{2,1,0:T(8,128)} %broadcast_in_dim.27), calls=%async_computation.6 | async-start | bytes 1048576 | tf_op jit(solution)/shard_map/all_to_all | solution.py:23
  158.7 16.5 %all-to-all-start.6 = ((f32[8,4,1024]{2,1,0:T(4,128)}), f32[8,4,1024]{2,1,0:T(4,128)S(1)}, u32[]{:S(2)}, u32[]{:S(2)}) async-start(f32[8,4,1024]{2,1,0:T(4,128)} %reshape.121), calls=%async_computation.7 | async-start | bytes 262144 | tf_op jit(solution)/shard_map/all_to_all | solution.py:23
Sparse Core Ops, SparseCore 0:
  10.8 72.1 reduce-scatter.1
  85.1 57.6 all-gather.1

commit v3 on v2

v3 whole, which is shorter than its diff:
```python
import jax
import jax.numpy as jnp
from jax import lax
from jax.experimental import pallas as pl
from jax.experimental.pallas import tpu as pltpu
from jax.sharding import Mesh, PartitionSpec as P

MP = ("zk", "zb")
TCOL = ("y", "core")
PLANE = ("trow",) + TCOL
SHARD = ("trow", "zb")
HIGHEST = lax.Precision.HIGHEST


def dot(lhs, rhs, lhs_dim, rhs_dim):
    return lax.dot_general(
        lhs,
        rhs,
        (((lhs_dim,), (rhs_dim,)), ((), ())),
        precision=HIGHEST,
        preferred_element_type=jnp.float32,
    )


def exchange(pieces, axes):
    return lax.all_to_all(pieces, axes, 0, 0, tiled=True)


def spread(block, axes, count):
    return exchange(jnp.broadcast_to(block[None], (count,) + block.shape), axes)


def ordered(flag, mine, other):
    return jnp.where(flag == 0, mine, other), jnp.where(flag == 0, other, mine)


def transposed(vector, sizes):
    trow, tcol = sizes["trow"], sizes["y"] * sizes["core"]
    half = vector.shape[1] // 2
    core = lax.axis_index("core")
    halves = (vector[:, :half], vector[:, half:])
    got = []
    for turn in range(2):
        pairs = []
        for i in range(trow):
            for j in range(tcol):
                q, h = j // 2, j % 2
                pairs.append((i * tcol + j, q * tcol + 2 * i + (h ^ turn)))
        sent = jnp.where(core == turn, halves[0], halves[1])
        got.append(lax.ppermute(sent, PLANE, pairs))
    return jnp.stack(got)


def reordered(tile, order, chunk):
    def body(source, target, done):
        copies = [
            pltpu.make_async_copy(
                source.at[pl.ds(n * chunk, chunk)],
                target.at[pl.ds(at * chunk, chunk)],
                done.at[at],
            )
            for at, n in enumerate(order)
        ]
        for copy in copies:
            copy.start()
        for copy in copies:
            copy.wait()

    return pl.pallas_call(
        body,
        out_shape=jax.ShapeDtypeStruct(tile.shape, tile.dtype),
        in_specs=[pl.BlockSpec(memory_space=pl.ANY)],
        out_specs=pl.BlockSpec(memory_space=pl.ANY),
        scratch_shapes=[pltpu.SemaphoreType.DMA((len(order),))],
        cost_estimate=pl.CostEstimate(flops=0, bytes_accessed=2 * tile.size * 4, transcendentals=0),
    )(tile)


def reduced(mp, gram, guess):
    tile = gram[0]
    rows, cols = tile.shape
    chunk = rows // mp
    order = []
    for k in range(mp // 2):
        order += [k, mp - 1 - k]
    cut = reordered(tile, order, chunk)
    cut, guess = lax.optimization_barrier((cut, guess))
    return lax.psum_scatter(cut, "mp", scatter_dimension=0, tiled=True), guess


def gathered(mp, part):
    groups = [list(range(0, mp, 2)), list(range(mp - 1, 0, -2))]
    return lax.all_gather(part, "mp", axis_index_groups=groups, axis=0, tiled=True)


def image_by_model(sizes, gram, guess):
    mp, trow, y = sizes["zk"] * sizes["zb"], sizes["trow"], sizes["y"]
    tile = gram[0]
    rows, cols = tile.shape
    own = guess.shape[0]
    flipped = transposed(guess, sizes)
    over_mp = spread(flipped, MP, mp)
    over_mp = over_mp.transpose(1, 0, 2, 3).reshape(2 * mp * own, cols)
    block = spread(over_mp, "trow", trow).reshape(trow, 2, mp * own, cols)
    given = dot(block[:, 1].reshape(trow * mp * own, cols), tile, 1, 1)
    given = lax.ppermute(given, "core", [(0, 1), (1, 0)])
    terms = dot(block[:, 0].reshape(trow * mp * own, cols), tile, 1, 1) + given
    return exchange(terms.reshape(y, mp * own, rows), "y").sum(0)


def shards(sizes, total, terms, rhs, guess):
    zk, zb, trow, y = sizes["zk"], sizes["zb"], sizes["trow"], sizes["y"]
    mp, tcol = zk * zb, y * sizes["core"]
    part_rows, cols = total.shape
    rows = part_rows * zb
    own = rhs.shape[0]
    half = lax.axis_index("zb")
    swap = [(0, 1), (1, 0)]

    def halves(vector):
        low, high = vector[:, :part_rows], vector[:, part_rows:]
        return jnp.where(half == 0, low, high), jnp.where(half == 0, high, low)

    kept, given = halves(rhs)
    near = jnp.concatenate(ordered(half, kept, lax.ppermute(given, "zb", swap)))
    terms = terms.reshape(zk, zb * own, zb, part_rows).transpose(0, 2, 1, 3)
    terms = exchange(terms.reshape(mp, zb * own, part_rows), MP).sum(0)
    near = near - terms

    wide = spread(near, TCOL, tcol).reshape(tcol * zb * own, part_rows)
    second = spread(dot(wide, total, 1, 0), SHARD, trow * zb).sum(0)
    terms = dot(second, total, 1, 1)
    pieces = jnp.concatenate([terms, second], axis=1).reshape(tcol, zb * own, part_rows + cols)
    pieces = exchange(pieces, TCOL)
    third = pieces[:, :, :part_rows].sum(0)
    second = lax.dynamic_slice(
        pieces, (2 * lax.axis_index("trow"), 0, part_rows), (2, zb * own, cols)
    )
    second = jnp.concatenate([second[0], second[1]], axis=1)

    def inner(u, v):
        return jnp.sum(u * v, axis=1, keepdims=True)

    def inverse(x):
        return jnp.where(x > 0, 1.0 / jnp.where(x > 0, x, 1.0), 0.0)

    here, _ = halves(second)
    f0 = jnp.sqrt(inner(near, near))
    e0 = near * inverse(f0)
    s0 = inner(e0, here)
    rest = here - s0 * e0
    s1 = jnp.sqrt(inner(rest, rest))
    e1 = rest * inverse(s1)
    t0 = inner(e0, third)
    t1 = inner(e1, third - t0 * e0)
    numbers = jnp.pad(jnp.concatenate([f0, s0, s1, t0, t1], axis=1), ((0, 0), (0, 123)))
    known = jnp.concatenate([near, third, numbers], axis=1)
    pieces = jnp.broadcast_to(known[None], (trow,) + known.shape)
    pieces = exchange(pieces.reshape(trow * zb, own, known.shape[1]), SHARD)
    f0, s0, s1, t0, t1 = (pieces[:, :, rows + n : rows + n + 1] for n in range(5))
    pair = lax.dynamic_slice(pieces, (zb * lax.axis_index("trow"), 0, 0), (zb, own, rows))
    first = jnp.concatenate([pair[0, :, :part_rows], pair[1, :, :part_rows]], axis=1)
    third = jnp.concatenate([pair[0, :, part_rows:], pair[1, :, part_rows:]], axis=1)
    second = jnp.where(half == 0, second[:own], second[own:])

    norm_first = jnp.sum(f0 * f0, 0)
    alpha = norm_first / jnp.sum(f0 * s0, 0)
    r0, r1 = f0 - alpha * s0, -alpha * s1
    norm_next = jnp.sum(r0 * r0 + r1 * r1, 0)
    beta = norm_next / norm_first
    d0, d1 = r0 + beta * f0, r1
    i0, i1 = s0 - alpha * t0 + beta * s0, s1 - alpha * t1 + beta * s1
    alpha_next = norm_next / jnp.sum(d0 * i0 + d1 * i1, 0)

    residual = first - alpha * second
    direction = residual + beta * first
    image = second - alpha * third + beta * second
    merged = guess + alpha * first + alpha_next * direction
    return merged, residual - alpha_next * image


def solution(mesh):
    mp, trow, tcol = (mesh.shape[a] for a in ("mp", "trow", "tcol"))
    sizes = {"zk": mp // 2, "zb": 2, "trow": trow, "y": tcol // 2, "core": 2}
    split = Mesh(mesh.devices.reshape(tuple(sizes.values())), tuple(sizes))
    every = ("mp", "trow", "tcol")

    def run(function, where, out, *args):
        axes = every if where is mesh else MP + PLANE
        own = axes[0] if where is mesh else MP
        columns = axes[-1:] if where is mesh else TCOL
        spec = {
            "tile": P(own, "trow", columns),
            "row": P((own,) + columns if where is mesh else MP + TCOL, "trow"),
            "block": P(axes),
        }
        return jax.shard_map(
            function,
            mesh=where,
            in_specs=tuple(spec[kind] for kind, _ in args),
            out_specs=tuple(spec[kind] for kind in out),
            check_vma=False,
        )(*(value for _, value in args))

    def whole(gram, rhs, guess):
        part, early = run(
            lambda gram, guess: reduced(mp, gram, guess),
            mesh, ("block", "row"), ("tile", gram), ("row", guess),
        )
        (terms,) = run(
            lambda gram, guess: (image_by_model(sizes, gram, guess),),
            split, ("block",), ("tile", gram), ("row", early),
        )
        part, _ = lax.optimization_barrier((part, terms))
        (total,) = run(lambda part: (gathered(mp, part),), mesh, ("block",), ("block", part))
        return run(
            lambda *args: shards(sizes, *args),
            split, ("row", "row"), ("block", total), ("block", terms), ("row", rhs), ("row", guess),
        )

    return whole
```

time: 194 us -> 257 us (1.32)
  Pallas kernels: 0 us -> 64.8 us
  waiting for transfers between devices: 52.3 us -> 44.5 us
  blocking collectives: 68.8 us -> 73.6 us
    pallas_call x0 -> x1, Pallas kernels: none -> 64.8 us  [reordered(): pl.pallas_call(body, out_shape=jax.ShapeDtypeStruct(tile.shape, tile.dtyp...]
    reduce_scatter x1, waiting for transfers between devices: 7.61 us -> 0.02 us  [reduced(): return (lax.psum_scatter(cut, 'mp', scatter_dimension=0, tiled=True), guess)]
    ppermute x1 -> x2, starting transfers between devices: 2.84 us -> 10 us  [the longest x1 6.77 us: image_by_model(): given = lax.ppermute(given, 'core', [(0, 1), (1, 0)])]
    all_to_all x4, waiting for transfers between devices: 32.3 us -> 25.2 us  [exchange(): return lax.all_to_all(pieces, axes, 0, 0, tiled=True)]
    all_gather x1, waiting for transfers between devices: 9.67 us -> 15.6 us  [gathered(): lax.all_gather(part, 'mp', axis_index_groups=groups, axis=0, tiled=True)]
    all_to_all x4, starting transfers between devices: 29.1 us -> 23.6 us  [exchange(): return lax.all_to_all(pieces, axes, 0, 0, tiled=True)]
    all_to_all x4, blocking collectives: 68.8 us -> 73.6 us  [exchange(): return lax.all_to_all(pieces, axes, 0, 0, tiled=True)]
    dot_general x3 -> x4, matrix products: 5.97 us -> 7.63 us  [dot(): lax.dot_general(lhs, rhs, (((lhs_dim,), (rhs_dim,)), ((), ())), precision...]
  transfers between devices with their start and end apart: 9 -> 10, of which waited for: 8 -> 8; matrix products, arithmetic and copies ran while one was open for 2% -> 2% of each run, Pallas kernels for 0% -> 0%
where the time goes in v3:
time: 257 us; the launch traced here: 256 us
  blocking collectives  73.6 us (29%)
  Pallas kernels  64.8 us (25%)
  waiting for transfers between devices  44.5 us (17%)
  starting transfers between devices  43.1 us (17%)
  between operations  14.3 us (6%)
  matrix products  7.63 us (3%)
  local copies, waits for them, and re-layouts  5.04 us (2%)
  other arithmetic  2.82 us (1%)
    all_to_all x4, blocking collectives, exchange(): return lax.all_to_all(pieces, axes, 0, 0, tiled=True)  73.6 us
    pallas_call x1, Pallas kernels, reordered(): pl.pallas_call(body, out_shape=jax.ShapeDtypeStruct(tile.shape, tile.dtyp...  64.8 us
    all_to_all x4, waiting for transfers between devices, exchange(): return lax.all_to_all(pieces, axes, 0, 0, tiled=True)  25.2 us
    all_to_all x4, starting transfers between devices, exchange(): return lax.all_to_all(pieces, axes, 0, 0, tiled=True)  23.6 us
    all_gather x1, waiting for transfers between devices, gathered(): lax.all_gather(part, 'mp', axis_index_groups=groups, axis=0, tiled=True)  15.6 us
    ppermute x2, starting transfers between devices, transposed(): got.append(lax.ppermute(sent, PLANE, pairs))  9.44 us
    dot_general x4, matrix products, dot(): lax.dot_general(lhs, rhs, (((lhs_dim,), (rhs_dim,)), ((), ())), precision...  7.63 us
    ppermute x1, starting transfers between devices, image_by_model(): given = lax.ppermute(given, 'core', [(0, 1), (1, 0)])  6.77 us
  transfers between devices with their start and end apart: 10, of which 8 were waited for; matrix products, arithmetic and copies ran while one was open for 2% of the time, Pallas kernels for 0%

profile of v3, /device:TPU:1, one launch (start us, length us, event | category | flops | bytes accessed | tf_op | source)
XLA Modules:
  0.0 255.8 jit_solution(7038221371745067722)
XLA Ops:
  7.2 64.8 %shard_map.145 = f32[1024,512]{1,0:T(8,128)} custom-call(f32[1024,512]{1,0:T(8,128)} %bitcast.41), custom_call_target="tpu_custom_call" | custom-call | bytes 4194304 | tf_op jit(solution)/shard_map/pallas_call | solution.py:69
  72.1 0.6 copy-done.3
  72.7 0.6 collective-permute-start
  73.4 8.8 %collective-permute-start.1 = (f32[2,512]{1,0:T(2,128)S(1)}, f32[2,512]{1,0:T(2,128)S(1)}, u32[]{:S(2)}, u32[]{:S(2)}) collective-permute-start(f32[2,512]{1,0:T(2,128)S(1)} %get-tuple-element.47), channel_id=1, source_target_pairs={{0,1},{1,0},{2,9},{3,8},{4,17},{5,16},{6,25},{7,24},{8,3},{9,2},{1... | collective-permute-start | bytes 12296 | tf_op jit(solution)/shard_map/ppermute | solution.py:50
  82.2 0.8 collective-permute-done.1
  83.0 21.4 %all_to_all.40 = f32[16,2,2,512]{3,2,1,0:T(2,128)S(1)} all-to-all(f32[16,2,2,512]{3,2,1,0:T(2,128)S(1)} %broadcast_in_dim.30), channel_id=1, replica_groups=mesh['zk'=8,'zb'=2,'trow'=4,'y'=4,'core'=2] {'zk','zb'}, dimensions={0} | all-to-all | bytes 262144 | tf_op jit(solution)/shard_map/all_to_all | solution.py:26
  104.6 21.1 %all_to_all.41 = f32[4,64,512]{2,1,0:T(8,128)S(1)} all-to-all(f32[4,64,512]{2,1,0:T(8,128)S(1)} %broadcast_in_dim.32), channel_id=1, replica_groups=mesh['zk'=8,'zb'=2,'trow'=4,'y'=4,'core'=2] {'trow'}, dimensions={0} | all-to-all | bytes 1048576 | tf_op jit(solution)/shard_map/all_to_all | solution.py:26
  125.7 2.3 fusion.6
  128.0 6.8 %collective-permute-start.2 = (f32[128,1024]{1,0:T(8,128)S(1)}, f32[128,1024]{1,0:T(8,128)S(1)}, u32[]{:S(2)}, u32[]{:S(2)}) collective-permute-start(f32[128,1024]{1,0:T(8,128)S(1)} %fusion.6), channel_id=1, source_target_pairs={{0,1},{1,0},{2,3},{3,2},{4,5},{5,4},{6,7},{7,6},{8,9},{9,8},{10,11... | collective-permute-start | bytes 1572872 | tf_op jit(solution)/shard_map/ppermute | solution.py:106
  134.8 1.5 collective-permute-done.2
  136.3 2.3 convolution_add_fusion
  138.6 11.6 %all_to_all.42 = f32[4,32,1024]{2,1,0:T(8,128)S(1)} all-to-all(f32[4,32,1024]{2,1,0:T(8,128)S(1)} %bitcast.43), channel_id=1, replica_groups=mesh['zk'=8,'zb'=2,'trow'=4,'y'=4,'core'=2] {'y'}, dimensions={0} | all-to-all | bytes 1048576 | tf_op jit(solution)/shard_map/all_to_all | solution.py:26
  150.5 0.7 copy.110
  151.1 5.1 %all-to-all-start.3 = ((f32[16,4,512]{2,1,0:T(4,128)}), f32[16,4,512]{2,1,0:T(4,128)S(1)}, u32[]{:S(2)}, u32[]{:S(2)}) async-start(f32[16,4,512]{2,1,0:T(4,128)} %bitcast.9), calls=%async_computation.4 | async-start | bytes 262144 | tf_op jit(solution)/shard_map/all_to_all | solution.py:26
  156.2 3.3 %collective-permute-start.3 = (f32[2,512]{1,0:T(2,128)S(1)}, f32[2,512]{1,0:T(2,128)S(1)}, u32[]{:S(2)}, u32[]{:S(2)}) collective-permute-start(f32[2,512]{1,0:T(2,128)S(1)} %broadcast_select_fusion.3), channel_id=1, source_target_pairs={{0,32},{32,0},{1,33},{33,1},{2,34},{34,2},{3,35},{35,3},{4,36},{36... | collective-permute-start | bytes 12296 | tf_op jit(solution)/shard_map/ppermute | solution.py:125
  159.5 1.3 collective-permute-done.3
  160.8 7.3 %all-to-all-done.3 = f32[16,4,512]{2,1,0:T(4,128)S(1)} async-done(((f32[16,4,512]{2,1,0:T(4,128)}), f32[16,4,512]{2,1,0:T(4,128)S(1)}, u32[]{:S(2)}, u32[]{:S(2)}) %all-to-all-start.3) | async-done | bytes 131104 | tf_op jit(solution)/shard_map/all_to_all | solution.py:26
  168.3 19.5 %all_to_all.43 = f32[8,4,512]{2,1,0:T(4,128)S(1)} all-to-all(f32[8,4,512]{2,1,0:T(4,128)S(1)} %broadcast_in_dim.33), channel_id=1, replica_groups=mesh['zk'=8,'zb'=2,'trow'=4,'y'=4,'core'=2] {'y','core'}, dimensions={0} | all-to-all | bytes 131072 | tf_op jit(solution)/shard_map/all_to_all | solution.py:26
  187.9 15.6 %all-gather.2.cloned.1.call-done = f32[512,512]{1,0:T(8,128)} async-done(((f32[64,512]{1,0:T(8,128)}), f32[512,512]{1,0:T(8,128)}) %all-gather.2.cloned.1.call-update) | async-done | bytes 1048592 | tf_op jit(solution)/shard_map/all_gather | solution.py:93
  203.4 2.0 fusion.13
  205.4 0.9 broadcast_in_dim.34
  206.3 6.3 %all-to-all-start.5 = ((f32[8,32,512]{2,1,0:T(8,128)}), f32[8,32,512]{2,1,0:T(8,128)S(1)}, u32[]{:S(2)}, u32[]{:S(2)}) async-start(f32[8,32,512]{2,1,0:T(8,128)} %broadcast_in_dim.34), calls=%async_computation.6 | async-start | bytes 1048576 | tf_op jit(solution)/shard_map/all_to_all | solution.py:26
  212.7 7.5 %all-to-all-done.5 = f32[8,32,512]{2,1,0:T(8,128)S(1)} async-done(((f32[8,32,512]{2,1,0:T(8,128)}), f32[8,32,512]{2,1,0:T(8,128)S(1)}, u32[]{:S(2)}, u32[]{:S(2)}) %all-to-all-start.5) | async-done | bytes 524320 | tf_op jit(solution)/shard_map/all_to_all | solution.py:26
  220.3 1.0 fusion.14
  221.3 0.7 reshape.141
  222.0 8.8 %all-to-all-start.6 = ((f32[8,4,1024]{2,1,0:T(4,128)}), f32[8,4,1024]{2,1,0:T(4,128)S(1)}, u32[]{:S(2)}, u32[]{:S(2)}) async-start(f32[8,4,1024]{2,1,0:T(4,128)} %reshape.141), calls=%async_computation.7 | async-start | bytes 262144 | tf_op jit(solution)/shard_map/all_to_all | solution.py:26
  230.9 5.2 %all-to-all-done.6 = f32[8,4,1024]{2,1,0:T(4,128)S(1)} async-done(((f32[8,4,1024]{2,1,0:T(4,128)}), f32[8,4,1024]{2,1,0:T(4,128)S(1)}, u32[]{:S(2)}, u32[]{:S(2)}) %all-to-all-start.6) | async-done | bytes 131104 | tf_op jit(solution)/shard_map/all_to_all | solution.py:26
  237.3 0.7 reshape.142
  237.9 3.4 %all-to-all-start.7 = ((f32[8,2,1152]{2,1,0:T(2,128)}), f32[8,2,1152]{2,1,0:T(2,128)S(1)}, u32[]{:S(2)}, u32[]{:S(2)}) async-start(f32[8,2,1152]{2,1,0:T(2,128)} %reshape.142), calls=%async_computation.8 | async-start | bytes 147456 | tf_op jit(solution)/shard_map/all_to_all | solution.py:26
  241.3 5.2 %all-to-all-done.7 = f32[8,2,1152]{2,1,0:T(2,128)S(1)} async-done(((f32[8,2,1152]{2,1,0:T(2,128)}), f32[8,2,1152]{2,1,0:T(2,128)S(1)}, u32[]{:S(2)}, u32[]{:S(2)}) %all-to-all-start.7) | async-done | bytes 73760 | tf_op jit(solution)/shard_map/all_to_all | solution.py:26
  247.6 0.7 fusion.5
  248.3 0.7 multiply_add_fusion
  (57 shorter events, 3.1 us)
Async XLA Ops:
  7.2 143.1 %reduce-scatter.2.cloned.1.call-start = ((), (), s32[]{:S(2)}) async-start(), calls=%async_computation.9 | async-start | bytes 2228224 | tf_op jit(solution)/shard_map/reduce_scatter | solution.py:88
  72.0 0.7 copy-start.3
  72.0 53.7 %copy-start = (f32[1,1024,512]{2,1,0:T(8,128)S(1)}, f32[1,1024,512]{2,1,0:T(8,128)}, u32[]{:S(2)}) copy-start(f32[1,1024,512]{2,1,0:T(8,128)} %param.9) | copy-start | bytes 6291460
  72.0 131.4 %all-gather.2.cloned.1.call-start = ((), (), s32[]{:S(2)}) async-start(), calls=%async_computation.10 | async-start | bytes 1179648 | tf_op jit(solution)/shard_map/all_gather | solution.py:93
  72.7 9.5 %collective-permute-start = (f32[2,512]{1,0:T(2,128)S(1)}, f32[2,512]{1,0:T(2,128)S(1)}, u32[]{:S(2)}, u32[]{:S(2)}) collective-permute-start(f32[2,512]{1,0:T(2,128)S(1)} %get-tuple-element.46), channel_id=1, source_target_pairs={{0,0},{1,1},{2,8},{3,9},{4,16},{5,17},{6,24},{7,25},{8,2},{9,3},{1... | collective-permute-start | bytes 12296 | tf_op jit(solution)/shard_map/ppermute | solution.py:50
  73.4 9.6 %collective-permute-start.1 = (f32[2,512]{1,0:T(2,128)S(1)}, f32[2,512]{1,0:T(2,128)S(1)}, u32[]{:S(2)}, u32[]{:S(2)}) collective-permute-start(f32[2,512]{1,0:T(2,128)S(1)} %get-tuple-element.47), channel_id=1, source_target_pairs={{0,1},{1,0},{2,9},{3,8},{4,17},{5,16},{6,25},{7,24},{8,3},{9,2},{1... | collective-permute-start | bytes 12296 | tf_op jit(solution)/shard_map/ppermute | solution.py:50
  128.0 8.3 %collective-permute-start.2 = (f32[128,1024]{1,0:T(8,128)S(1)}, f32[128,1024]{1,0:T(8,128)S(1)}, u32[]{:S(2)}, u32[]{:S(2)}) collective-permute-start(f32[128,1024]{1,0:T(8,128)S(1)} %fusion.6), channel_id=1, source_target_pairs={{0,1},{1,0},{2,3},{3,2},{4,5},{5,4},{6,7},{7,6},{8,9},{9,8},{10,11... | collective-permute-start | bytes 1572872 | tf_op jit(solution)/shard_map/ppermute | solution.py:106
  138.6 17.6 %copy-start.2 = (f32[2,1024]{1,0:T(2,128)S(1)}, f32[2,1024]{1,0:T(2,128)}, u32[]{:S(2)}) copy-start(f32[2,1024]{1,0:T(2,128)} %param.11) | copy-start | bytes 24580
  151.1 17.0 %all-to-all-start.3 = ((f32[16,4,512]{2,1,0:T(4,128)}), f32[16,4,512]{2,1,0:T(4,128)S(1)}, u32[]{:S(2)}, u32[]{:S(2)}) async-start(f32[16,4,512]{2,1,0:T(4,128)} %bitcast.9), calls=%async_computation.4 | async-start | bytes 262144 | tf_op jit(solution)/shard_map/all_to_all | solution.py:26
  156.2 4.6 %collective-permute-start.3 = (f32[2,512]{1,0:T(2,128)S(1)}, f32[2,512]{1,0:T(2,128)S(1)}, u32[]{:S(2)}, u32[]{:S(2)}) collective-permute-start(f32[2,512]{1,0:T(2,128)S(1)} %broadcast_select_fusion.3), channel_id=1, source_target_pairs={{0,32},{32,0},{1,33},{33,1},{2,34},{34,2},{3,35},{35,3},{4,36},{36... | collective-permute-start | bytes 12296 | tf_op jit(solution)/shard_map/ppermute | solution.py:125
  203.4 16.8 %copy-start.1 = (f32[512,512]{1,0:T(8,128)S(1)}, f32[512,512]{1,0:T(8,128)}, u32[]{:S(2)}) copy-start(f32[512,512]{1,0:T(8,128)} %all-gather.2.cloned.1.call-done) | copy-start | bytes 3145732
  206.3 13.9 %all-to-all-start.5 = ((f32[8,32,512]{2,1,0:T(8,128)}), f32[8,32,512]{2,1,0:T(8,128)S(1)}, u32[]{:S(2)}, u32[]{:S(2)}) async-start(f32[8,32,512]{2,1,0:T(8,128)} %broadcast_in_dim.34), calls=%async_computation.6 | async-start | bytes 1048576 | tf_op jit(solution)/shard_map/all_to_all | solution.py:26
  222.0 14.1 %all-to-all-start.6 = ((f32[8,4,1024]{2,1,0:T(4,128)}), f32[8,4,1024]{2,1,0:T(4,128)S(1)}, u32[]{:S(2)}, u32[]{:S(2)}) async-start(f32[8,4,1024]{2,1,0:T(4,128)} %reshape.141), calls=%async_computation.7 | async-start | bytes 262144 | tf_op jit(solution)/shard_map/all_to_all | solution.py:26
  237.9 8.5 %all-to-all-start.7 = ((f32[8,2,1152]{2,1,0:T(2,128)}), f32[8,2,1152]{2,1,0:T(2,128)S(1)}, u32[]{:S(2)}, u32[]{:S(2)}) async-start(f32[8,2,1152]{2,1,0:T(2,128)} %reshape.142), calls=%async_computation.8 | async-start | bytes 147456 | tf_op jit(solution)/shard_map/all_to_all | solution.py:26
Sparse Core Ops, SparseCore 0:
  72.1 71.9 reduce-scatter.1
  150.5 52.9 all-gather.1

commit v4 on v1

v4 whole, which is shorter than its diff:
```python
import jax
import jax.numpy as jnp
from jax import lax
from jax.sharding import Mesh, PartitionSpec as P

MP = ("zh", "zl")
TCOL = ("y", "core")
PLANE = ("trow",) + TCOL
COPIES = ("zl", "core")
GROUP = ("zh", "y")
HIGHEST = lax.Precision.HIGHEST


def dot(lhs, rhs, lhs_dim, rhs_dim):
    return lax.dot_general(
        lhs,
        rhs,
        (((lhs_dim,), (rhs_dim,)), ((), ())),
        precision=HIGHEST,
        preferred_element_type=jnp.float32,
    )


def exchange(pieces, axes):
    return lax.all_to_all(pieces, axes, 0, 0, tiled=True)


def spread(block, axes, count):
    return exchange(jnp.broadcast_to(block[None], (count,) + block.shape), axes)


def transposed(vector, sizes):
    trow, tcol = sizes["trow"], sizes["y"] * sizes["core"]
    half = vector.shape[1] // 2
    core = lax.axis_index("core")
    halves = (vector[:, :half], vector[:, half:])
    got = []
    for turn in range(2):
        pairs = []
        for i in range(trow):
            for j in range(tcol):
                q, h = j // 2, j % 2
                pairs.append((i * tcol + j, q * tcol + 2 * i + (h ^ turn)))
        sent = jnp.where(core == turn, halves[0], halves[1])
        got.append(lax.ppermute(sent, PLANE, pairs))
    return jnp.stack(got)


def shards(sizes, gram, rhs, guess):
    zh, zl, trow, y, core = sizes.values()
    mp, tcol = zh * zl, y * core
    tile = gram[0]
    rows, cols = tile.shape
    own = rhs.shape[0]
    tall, thin = rows // zl, cols // zh
    group = zh * y

    cut = tile.reshape(zl, tall, zh, thin).transpose(2, 0, 1, 3).reshape(mp * tall, thin)
    cut, guess_after = lax.optimization_barrier((cut, guess))
    part = lax.psum_scatter(cut, MP, scatter_dimension=0, tiled=True)

    flipped = transposed(guess_after, sizes)
    over_mp = spread(flipped, MP, mp)
    over_mp = over_mp.transpose(1, 0, 2, 3).reshape(2 * mp * own, cols)
    block = spread(over_mp, "trow", trow).reshape(trow, 2, mp * own, cols)
    given = dot(block[:, 1].reshape(trow * mp * own, cols), tile, 1, 1)
    given = lax.ppermute(given, "core", [(0, 1), (1, 0)])
    terms = dot(block[:, 0].reshape(trow * mp * own, cols), tile, 1, 1) + given
    terms = exchange(terms.reshape(y, mp * own, rows), "y").sum(0)
    part, _ = lax.optimization_barrier((part, terms))
    terms = exchange(terms.reshape(mp, own, rows), MP).sum(0)
    first = rhs - terms

    total = lax.all_gather(part, COPIES, axis=0, tiled=True).reshape(zl, core, tall, thin)
    total = total.transpose(0, 2, 1, 3).reshape(rows, core * thin)

    wide = spread(first, GROUP, group).reshape(group * own, rows)
    second = spread(dot(wide, total, 1, 0), "trow", trow).sum(0)
    terms = dot(second, total, 1, 1)
    pieces = jnp.concatenate([terms, second], axis=1).reshape(group, own, rows + core * thin)
    pieces = exchange(pieces, GROUP)
    third = pieces[:, :, :rows].sum(0)
    second = pieces[:, :, rows:].reshape(zh, y, own, core, thin)
    second = lax.dynamic_index_in_dim(second, lax.axis_index("trow"), 1, keepdims=False)
    second = second.transpose(1, 2, 0, 3).reshape(own, rows)

    def inner(u, v):
        return jnp.sum(u * v, axis=1, keepdims=True)

    def inverse(x):
        return jnp.where(x > 0, 1.0 / jnp.where(x > 0, x, 1.0), 0.0)

    f0 = jnp.sqrt(inner(first, first))
    e0 = first * inverse(f0)
    s0 = inner(e0, second)
    rest = second - s0 * e0
    s1 = jnp.sqrt(inner(rest, rest))
    e1 = rest * inverse(s1)
    t0 = inner(e0, third)
    t1 = inner(e1, third - t0 * e0)
    known = spread(jnp.concatenate([f0, s0, s1, t0, t1], axis=1), "trow", trow)
    f0, s0, s1, t0, t1 = (known[:, :, n : n + 1] for n in range(5))

    norm_first = jnp.sum(f0 * f0, 0)
    alpha = norm_first / jnp.sum(f0 * s0, 0)
    r0, r1 = f0 - alpha * s0, -alpha * s1
    norm_next = jnp.sum(r0 * r0 + r1 * r1, 0)
    beta = norm_next / norm_first
    d0, d1 = r0 + beta * f0, r1
    i0, i1 = s0 - alpha * t0 + beta * s0, s1 - alpha * t1 + beta * s1
    alpha_next = norm_next / jnp.sum(d0 * i0 + d1 * i1, 0)

    residual = first - alpha * second
    direction = residual + beta * first
    image = second - alpha * third + beta * second
    merged = guess + alpha * first + alpha_next * direction
    return merged, residual - alpha_next * image


def solution(mesh):
    mp, trow, tcol = (mesh.shape[a] for a in ("mp", "trow", "tcol"))
    zl = 4 if mp > 4 else 2
    sizes = {"zh": mp // zl, "zl": zl, "trow": trow, "y": tcol // 2, "core": 2}
    split = Mesh(mesh.devices.reshape(tuple(sizes.values())), tuple(sizes))
    gram_spec = P(MP, "trow", TCOL)
    spec = P(MP + TCOL, "trow")

    def body(gram, rhs, guess):
        return shards(sizes, gram, rhs, guess)

    return jax.shard_map(
        body,
        mesh=split,
        in_specs=(gram_spec, spec, spec),
        out_specs=(spec, spec),
        check_vma=False,
    )
```

time: 203 us -> 197 us (0.970)
  the two profiles are of different devices: /device:TPU:32 before, /device:TPU:8 now
where the time goes in v4:
time: 197 us; the launch traced here: 196 us
  blocking collectives  121 us (61%)
  waiting for transfers between devices  23.7 us (12%)
  starting transfers between devices  20.6 us (10%)
  between operations  14.3 us (7%)
  local copies, waits for them, and re-layouts  8.56 us (4%)
  matrix products  6.23 us (3%)
  other arithmetic  2.17 us (1%)
    all_to_all x7, blocking collectives, exchange(): return lax.all_to_all(pieces, axes, 0, 0, tiled=True)  121 us
    all_to_all x1, waiting for transfers between devices, exchange(): return lax.all_to_all(pieces, axes, 0, 0, tiled=True)  13.8 us
    all_to_all x1, starting transfers between devices, exchange(): return lax.all_to_all(pieces, axes, 0, 0, tiled=True)  12.7 us
    dot_general x4, matrix products, dot(): lax.dot_general(lhs, rhs, (((lhs_dim,), (rhs_dim,)), ((), ())), precision...  6.23 us
    ppermute x2, starting transfers between devices, transposed(): got.append(lax.ppermute(sent, PLANE, pairs))  5.89 us
    reduce_scatter x1, waiting for transfers between devices, shards(): part = lax.psum_scatter(cut, MP, scatter_dimension=0, tiled=True)  4.76 us
  transfers between devices with their start and end apart: 6, of which 5 were waited for; matrix products, arithmetic and copies ran while one was open for 3% of the time, Pallas kernels for 0%

profile of v4, /device:TPU:8, one launch (start us, length us, event | category | flops | bytes accessed | tf_op | source)
XLA Modules:
  0.0 196.1 jit_solution(9572095589167143140)
XLA Ops:
  7.2 1.9 reshape_squeeze.9
  9.2 1.6 copy.58
  10.8 0.6 copy-done.1
  11.4 3.3 %collective-permute-start = (f32[2,512]{1,0:T(2,128)S(1)}, f32[2,512]{1,0:T(2,128)S(1)}, u32[]{:S(2)}, u32[]{:S(2)}) collective-permute-start(f32[2,512]{1,0:T(2,128)S(1)} %get-tuple-element.20), channel_id=1, source_target_pairs={{0,0},{1,1},{2,8},{3,9},{4,16},{5,17},{6,24},{7,25},{8,2},{9,3},{1... | collective-permute-start | bytes 12296 | tf_op jit(solution)/shard_map/ppermute | solution.py:45
  14.7 2.6 %collective-permute-start.1 = (f32[2,512]{1,0:T(2,128)S(1)}, f32[2,512]{1,0:T(2,128)S(1)}, u32[]{:S(2)}, u32[]{:S(2)}) collective-permute-start(f32[2,512]{1,0:T(2,128)S(1)} %get-tuple-element.21), channel_id=1, source_target_pairs={{0,1},{1,0},{2,9},{3,8},{4,17},{5,16},{6,25},{7,24},{8,3},{9,2},{1... | collective-permute-start | bytes 12296 | tf_op jit(solution)/shard_map/ppermute | solution.py:45
  17.3 0.5 collective-permute-done
  17.8 2.7 %collective-permute-done.1 = f32[2,512]{1,0:T(2,128)S(1)} collective-permute-done((f32[2,512]{1,0:T(2,128)S(1)}, f32[2,512]{1,0:T(2,128)S(1)}, u32[]{:S(2)}, u32[]{:S(2)}) %collective-permute-start.1) | collective-permute-done | bytes 4128 | tf_op jit(solution)/shard_map/ppermute | solution.py:45
  20.6 31.7 %all_to_all.40 = f32[16,2,2,512]{3,2,1,0:T(2,128)S(1)} all-to-all(f32[16,2,2,512]{3,2,1,0:T(2,128)S(1)} %broadcast_in_dim.23), channel_id=1, replica_groups=mesh['zh'=4,'zl'=4,'trow'=4,'y'=4,'core'=2] {'zh','zl'}, dimensions={0} | all-to-all | bytes 262144 | tf_op jit(solution)/shard_map/all_to_all | solution.py:25
  52.4 14.9 %all_to_all.41 = f32[4,64,512]{2,1,0:T(8,128)S(1)} all-to-all(f32[4,64,512]{2,1,0:T(8,128)S(1)} %broadcast_in_dim.25), channel_id=1, replica_groups=mesh['zh'=4,'zl'=4,'trow'=4,'y'=4,'core'=2] {'trow'}, dimensions={0} | all-to-all | bytes 1048576 | tf_op jit(solution)/shard_map/all_to_all | solution.py:25
  67.3 2.3 %fusion = f32[128,1024]{1,0:T(8,128)S(1)} fusion(f32[128,512]{1,0:T(8,128)S(1)} %bitcast.49, f32[1,1024,512]{2,1,0:T(8,128)S(1)} %copy-done), kind=kOutput, calls=%fused_computation | convolution fusion | flops 805306368 | bytes 2883584 | tf_op jit(solution)/shard_map/dot_general | solution.py:15
  69.6 1.9 collective-permute-start.2
  71.6 1.9 collective-permute-done.2
  73.4 2.3 %fusion.4 = f32[128,1024]{1,0:T(8,128)S(1)} fusion(f32[128,1024]{1,0:T(8,128)S(1)} %collective-permute-done.2, f32[128,512]{1,0:T(8,128)S(1)} %bitcast.48, f32[1,1024,512]{2,1,0:T(8,128)S(1)} %copy-done), kind=kOutput, calls=%fused_computation.4 | convolution fusion | flops 805437440 | bytes 3407872 | tf_op jit(solution)/shard_map/dot_general | solution.py:15
  75.7 11.9 %all_to_all.42 = f32[4,32,1024]{2,1,0:T(8,128)S(1)} all-to-all(f32[4,32,1024]{2,1,0:T(8,128)S(1)} %bitcast.46), channel_id=1, replica_groups=mesh['zh'=4,'zl'=4,'trow'=4,'y'=4,'core'=2] {'y'}, dimensions={0} | all-to-all | bytes 1048576 | tf_op jit(solution)/shard_map/all_to_all | solution.py:25
  87.7 4.8 %reduce-scatter.2.cloned.1.call-done = f32[256,128]{1,0:T(8,128)} async-done(((f32[4096,128]{1,0:T(8,128)}), f32[256,128]{1,0:T(8,128)}) %reduce-scatter.2.cloned.1.call-update) | async-done | bytes 131088 | tf_op jit(solution)/shard_map/reduce_scatter | solution.py:60
  92.6 21.7 %all_to_all.43 = f32[16,2,1024]{2,1,0:T(2,128)S(1)} all-to-all(f32[16,2,1024]{2,1,0:T(2,128)S(1)} %reshape.132), channel_id=1, replica_groups=mesh['zh'=4,'zl'=4,'trow'=4,'y'=4,'core'=2] {'zh','zl'}, dimensions={0} | all-to-all | bytes 262144 | tf_op jit(solution)/shard_map/all_to_all | solution.py:25
  114.5 22.5 %all_to_all.44 = f32[16,2,1024]{2,1,0:T(2,128)S(1)} all-to-all(f32[16,2,1024]{2,1,0:T(2,128)S(1)} %broadcast_in_dim.26), channel_id=1, replica_groups=mesh['zh'=4,'zl'=4,'trow'=4,'y'=4,'core'=2] {'zh','y'}, dimensions={0} | all-to-all | bytes 262144 | tf_op jit(solution)/shard_map/all_to_all | solution.py:25
  137.2 2.0 %copy.61 = f32[4,2,256,128]{3,1,2,0:T(2,128)S(1)} copy(f32[4,2,256,128]{3,2,1,0:T(8,128)} %bitcast.47) | data formatting | bytes 2097152 | tf_op jit(solution)/shard_map/reshape | solution.py:74
  139.2 0.6 fusion.9
  139.8 10.2 %all_to_all.45 = f32[4,32,256]{2,1,0:T(8,128)S(1)} all-to-all(f32[4,32,256]{2,1,0:T(8,128)S(1)} %broadcast_in_dim.27), channel_id=1, replica_groups=mesh['zh'=4,'zl'=4,'trow'=4,'y'=4,'core'=2] {'trow'}, dimensions={0} | all-to-all | bytes 262144 | tf_op jit(solution)/shard_map/all_to_all | solution.py:25
  150.1 1.1 fusion.7
  151.2 0.7 reshape.136
  151.9 12.7 %all-to-all-start.6 = ((f32[16,2,1280]{2,1,0:T(2,128)}), f32[16,2,1280]{2,1,0:T(2,128)S(1)}, u32[]{:S(2)}, u32[]{:S(2)}) async-start(f32[16,2,1280]{2,1,0:T(2,128)} %reshape.136), calls=%async_computation.7 | async-start | bytes 327680 | tf_op jit(solution)/shard_map/all_to_all | solution.py:25
  164.8 13.8 %all-to-all-done.6 = f32[16,2,1280]{2,1,0:T(2,128)S(1)} async-done(((f32[16,2,1280]{2,1,0:T(2,128)}), f32[16,2,1280]{2,1,0:T(2,128)S(1)}, u32[]{:S(2)}, u32[]{:S(2)}) %all-to-all-start.6) | async-done | bytes 163872 | tf_op jit(solution)/shard_map/all_to_all | solution.py:25
  178.6 0.2 multiply_reduce_fusion.3
  179.0 0.2 multiply_reduce_fusion.1
  179.2 0.2 multiply_reduce_fusion
  179.8 7.6 %all_to_all.46 = f32[4,2,5]{2,1,0:T(2,128)S(1)} all-to-all(f32[4,2,5]{2,1,0:T(2,128)S(1)} %broadcast_in_dim.31), channel_id=1, replica_groups=mesh['zh'=4,'zl'=4,'trow'=4,'y'=4,'core'=2] {'trow'}, dimensions={0} | all-to-all | bytes 320 | tf_op jit(solution)/shard_map/all_to_all | solution.py:25
  188.0 0.2 multiply_reduce_fusion.5
  188.1 0.2 add_reduce_fusion.1
  188.4 0.2 add_reduce_fusion
  188.6 0.7 multiply_subtract_fusion
  (50 shorter events, 2.1 us)
Async XLA Ops:
  7.2 85.3 %reduce-scatter.2.cloned.1.call-start = ((), (), s32[]{:S(2)}) async-start(), calls=%async_computation.9 | async-start | bytes 2228224 | tf_op jit(solution)/shard_map/reduce_scatter | solution.py:60
  10.7 0.7 copy-start.1
  10.8 56.6 %copy-start = (f32[1,1024,512]{2,1,0:T(8,128)S(1)}, f32[1,1024,512]{2,1,0:T(8,128)}, u32[]{:S(2)}) copy-start(f32[1,1024,512]{2,1,0:T(8,128)} %param.3) | copy-start | bytes 6291460
  10.8 126.4 %all-gather.2.cloned.1.call-start = ((), (), s32[]{:S(2)}) async-start(), calls=%async_computation.10 | async-start | bytes 1179648 | tf_op jit(solution)/shard_map/all_gather | solution.py:74
  11.4 6.4 %collective-permute-start = (f32[2,512]{1,0:T(2,128)S(1)}, f32[2,512]{1,0:T(2,128)S(1)}, u32[]{:S(2)}, u32[]{:S(2)}) collective-permute-start(f32[2,512]{1,0:T(2,128)S(1)} %get-tuple-element.20), channel_id=1, source_target_pairs={{0,0},{1,1},{2,8},{3,9},{4,16},{5,17},{6,24},{7,25},{8,2},{9,3},{1... | collective-permute-start | bytes 12296 | tf_op jit(solution)/shard_map/ppermute | solution.py:45
  14.7 5.8 %collective-permute-start.1 = (f32[2,512]{1,0:T(2,128)S(1)}, f32[2,512]{1,0:T(2,128)S(1)}, u32[]{:S(2)}, u32[]{:S(2)}) collective-permute-start(f32[2,512]{1,0:T(2,128)S(1)} %get-tuple-element.21), channel_id=1, source_target_pairs={{0,1},{1,0},{2,9},{3,8},{4,17},{5,16},{6,25},{7,24},{8,3},{9,2},{1... | collective-permute-start | bytes 12296 | tf_op jit(solution)/shard_map/ppermute | solution.py:45
  69.6 3.8 %collective-permute-start.2 = (f32[128,1024]{1,0:T(8,128)S(1)}, f32[128,1024]{1,0:T(8,128)S(1)}, u32[]{:S(2)}, u32[]{:S(2)}) collective-permute-start(f32[128,1024]{1,0:T(8,128)S(1)} %fusion), channel_id=1, source_target_pairs={{0,1},{1,0},{2,3},{3,2},{4,5},{5,4},{6,7},{7,6},{8,9},{9,8},{10,11... | collective-permute-start | bytes 1572872 | tf_op jit(solution)/shard_map/ppermute | solution.py:67
  75.7 38.6 %copy-start.2 = (f32[2,1024]{1,0:T(2,128)S(1)}, f32[2,1024]{1,0:T(2,128)}, u32[]{:S(2)}) copy-start(f32[2,1024]{1,0:T(2,128)} %param.4) | copy-start | bytes 24580
  151.9 26.6 %all-to-all-start.6 = ((f32[16,2,1280]{2,1,0:T(2,128)}), f32[16,2,1280]{2,1,0:T(2,128)S(1)}, u32[]{:S(2)}, u32[]{:S(2)}) async-start(f32[16,2,1280]{2,1,0:T(2,128)} %reshape.136), calls=%async_computation.7 | async-start | bytes 327680 | tf_op jit(solution)/shard_map/all_to_all | solution.py:25
Sparse Core Ops, SparseCore 0:
  10.9 81.5 reduce-scatter.1
  94.6 41.6 all-gather.1

commit v5 on v4

--- a/solution.py
+++ b/solution.py
@@ -1,13 +1,12 @@
 import jax
 import jax.numpy as jnp
 from jax import lax
+from jax.experimental import pallas as pl
+from jax.experimental.pallas import tpu as pltpu
 from jax.sharding import Mesh, PartitionSpec as P
 
-MP = ("zh", "zl")
 TCOL = ("y", "core")
 PLANE = ("trow",) + TCOL
-COPIES = ("zl", "core")
-GROUP = ("zh", "y")
 HIGHEST = lax.Precision.HIGHEST
 
 
@@ -46,43 +45,66 @@
     return jnp.stack(got)
 
 
+def both_images(first, total, trow):
+    blocks, part, cols = total.shape
+    _, count, wide = first.shape
+    each = wide // cols
+
+    def body(first_ref, total_ref, second_ref, third_ref):
+        second = jnp.zeros((count, part), jnp.float32)
+        for n in range(blocks):
+            x, at = n // each, n % each * cols
+            second += dot(first_ref[x, :, at : at + cols], total_ref[n], 1, 1)
+        second_ref[...] = second
+        for n in range(blocks):
+            x, at = n // each, n % each * cols
+            third_ref[x, :, at : at + cols] = dot(second, total_ref[n], 1, 0)
+
+    return pl.pallas_call(
+        body,
+        out_shape=(
+            jax.ShapeDtypeStruct((count, part), jnp.float32),
+            jax.ShapeDtypeStruct(first.shape, jnp.float32),
+        ),
+        in_specs=[pl.BlockSpec(memory_space=pltpu.VMEM)] * 2,
+        out_specs=(pl.BlockSpec(memory_space=pltpu.VMEM),) * 2,
+        cost_estimate=pl.CostEstimate(
+            flops=4 * count * total.size, bytes_accessed=4 * (total.size + 2 * first.size), transcendentals=0
+        ),
+        compiler_params=pltpu.CompilerParams(vmem_limit_bytes=16 * 2**20),
+    )(first, total)
+
+
 def shards(sizes, gram, rhs, guess):
-    zh, zl, trow, y, core = sizes.values()
-    mp, tcol = zh * zl, y * core
+    mp, trow, y, core = sizes.values()
+    tcol = y * core
     tile = gram[0]
     rows, cols = tile.shape
     own = rhs.shape[0]
-    tall, thin = rows // zl, cols // zh
-    group = zh * y
+    share = rows // mp
 
-    cut = tile.reshape(zl, tall, zh, thin).transpose(2, 0, 1, 3).reshape(mp * tall, thin)
-    cut, guess_after = lax.optimization_barrier((cut, guess))
-    part = lax.psum_scatter(cut, MP, scatter_dimension=0, tiled=True)
+    part = lax.psum_scatter(tile, "mp", scatter_dimension=0, tiled=True)
 
-    flipped = transposed(guess_after, sizes)
-    over_mp = spread(flipped, MP, mp)
+    over_mp = lax.all_gather(transposed(guess, sizes), "mp", axis=0)
     over_mp = over_mp.transpose(1, 0, 2, 3).reshape(2 * mp * own, cols)
     block = spread(over_mp, "trow", trow).reshape(trow, 2, mp * own, cols)
     given = dot(block[:, 1].reshape(trow * mp * own, cols), tile, 1, 1)
     given = lax.ppermute(given, "core", [(0, 1), (1, 0)])
     terms = dot(block[:, 0].reshape(trow * mp * own, cols), tile, 1, 1) + given
     terms = exchange(terms.reshape(y, mp * own, rows), "y").sum(0)
-    part, _ = lax.optimization_barrier((part, terms))
-    terms = exchange(terms.reshape(mp, own, rows), MP).sum(0)
+    terms = exchange(terms.reshape(mp, own, rows), "mp").sum(0)
     first = rhs - terms
 
-    total = lax.all_gather(part, COPIES, axis=0, tiled=True).reshape(zl, core, tall, thin)
-    total = total.transpose(0, 2, 1, 3).reshape(rows, core * thin)
+    part, _ = lax.optimization_barrier((part, first))
+    total = lax.all_gather(part, TCOL, axis=0)
 
-    wide = spread(first, GROUP, group).reshape(group * own, rows)
-    second = spread(dot(wide, total, 1, 0), "trow", trow).sum(0)
-    terms = dot(second, total, 1, 1)
-    pieces = jnp.concatenate([terms, second], axis=1).reshape(group, own, rows + core * thin)
-    pieces = exchange(pieces, GROUP)
+    wide = lax.all_gather(first, "mp", axis=0).reshape(mp * own, rows)
+    second, terms = both_images(spread(wide, "trow", trow), total, trow)
+    terms = exchange(terms, "trow").sum(0)
+    pieces = jnp.concatenate([terms, second], axis=1).reshape(mp, own, rows + share)
+    pieces = exchange(pieces, "mp")
     third = pieces[:, :, :rows].sum(0)
-    second = pieces[:, :, rows:].reshape(zh, y, own, core, thin)
-    second = lax.dynamic_index_in_dim(second, lax.axis_index("trow"), 1, keepdims=False)
-    second = second.transpose(1, 2, 0, 3).reshape(own, rows)
+    second = pieces[:, :, rows:].transpose(1, 0, 2).reshape(own, rows)
 
     def inner(u, v):
         return jnp.sum(u * v, axis=1, keepdims=True)
@@ -119,11 +141,10 @@
 
 def solution(mesh):
     mp, trow, tcol = (mesh.shape[a] for a in ("mp", "trow", "tcol"))
-    zl = 4 if mp > 4 else 2
-    sizes = {"zh": mp // zl, "zl": zl, "trow": trow, "y": tcol // 2, "core": 2}
+    sizes = {"mp": mp, "trow": trow, "y": tcol // 2, "core": 2}
     split = Mesh(mesh.devices.reshape(tuple(sizes.values())), tuple(sizes))
-    gram_spec = P(MP, "trow", TCOL)
-    spec = P(MP + TCOL, "trow")
+    gram_spec = P("mp", "trow", TCOL)
+    spec = P(("mp",) + TCOL, "trow")
 
     def body(gram, rhs, guess):
         return shards(sizes, gram, rhs, guess)

time: 197 us -> 202 us (1.025)
  blocking collectives: 121 us -> 144 us
  starting transfers between devices: 20.6 us -> 11.5 us
  local copies, waits for them, and re-layouts: 8.56 us -> 3.6 us
  waiting for transfers between devices: 23.7 us -> 18.9 us
  Pallas kernels: 0 us -> 2.25 us
    all_gather x0 -> x2, blocking collectives: none -> 65.2 us  [the longest x1 36.2 us: shards(): over_mp = lax.all_gather(transposed(guess, sizes), 'mp', axis=0)]
    all_to_all x7 -> x6, blocking collectives: 121 us -> 79 us  [exchange(): return lax.all_to_all(pieces, axes, 0, 0, tiled=True)]
    all_to_all x1, starting transfers between devices: 12.7 us -> 3.51 us  [exchange(): return lax.all_to_all(pieces, axes, 0, 0, tiled=True)]
    reduce_scatter x1, waiting for transfers between devices: 4.76 us -> 0.01 us  [shards(): part = lax.psum_scatter(tile, 'mp', scatter_dimension=0, tiled=True)]
    pallas_call x0 -> x1, Pallas kernels: none -> 2.25 us  [both_images(): pl.pallas_call(body, out_shape=(jax.ShapeDtypeStruct((count, part), jnp.f...]
    reshape x6 -> x3, local copies, waits for them, and re-layouts: 3 us -> 0.89 us  [the longest x1 0.74 us: shards(): jnp.concatenate([terms, second], axis=1).reshape(mp, own, rows + share)]
    dot_general x4 -> x2, matrix products: 6.23 us -> 4.56 us  [dot(): lax.dot_general(lhs, rhs, (((lhs_dim,), (rhs_dim,)), ((), ())), precision...]
  transfers between devices with their start and end apart: 6 -> 6, of which waited for: 5 -> 4; matrix products, arithmetic and copies ran while one was open for 3% -> 3% of each run, Pallas kernels for 0% -> 0%
where the time goes in v5:
time: 202 us
  blocking collectives  144 us (71%)
  waiting for transfers between devices  18.9 us (9%)
  between operations  14.2 us (7%)
  starting transfers between devices  11.5 us (6%)
  matrix products  4.56 us (2%)
  local copies, waits for them, and re-layouts  3.6 us (2%)
  Pallas kernels  2.25 us (1%)
  other arithmetic  2.19 us (1%)
    all_to_all x6, blocking collectives, exchange(): return lax.all_to_all(pieces, axes, 0, 0, tiled=True)  79 us
    all_gather x1, blocking collectives, shards(): over_mp = lax.all_gather(transposed(guess, sizes), 'mp', axis=0)  36.2 us
    all_gather x1, blocking collectives, shards(): wide = lax.all_gather(first, 'mp', axis=0).reshape(mp * own, rows)  29 us
    all_to_all x1, waiting for transfers between devices, exchange(): return lax.all_to_all(pieces, axes, 0, 0, tiled=True)  13.1 us
    ppermute x2, starting transfers between devices, transposed(): got.append(lax.ppermute(sent, PLANE, pairs))  6.03 us
    dot_general x2, matrix products, dot(): lax.dot_general(lhs, rhs, (((lhs_dim,), (rhs_dim,)), ((), ())), precision...  4.56 us
  transfers between devices with their start and end apart: 6, of which 4 were waited for; matrix products, arithmetic and copies ran while one was open for 3% of the time, Pallas kernels for 0%

profile of v5, /device:TPU:8, one launch (start us, length us, event | category | flops | bytes accessed | tf_op | source)
XLA Modules:
  0.0 201.5 jit_solution(3970752550524526015)
XLA Ops:
  7.2 0.7 reduce-scatter.2.cloned.1.call-update
  8.0 3.4 %collective-permute-start = (f32[2,512]{1,0:T(2,128)S(1)}, f32[2,512]{1,0:T(2,128)S(1)}, u32[]{:S(2)}, u32[]{:S(2)}) collective-permute-start(f32[2,512]{1,0:T(2,128)S(1)} %get-tuple-element.20), channel_id=1, source_target_pairs={{0,0},{1,1},{2,8},{3,9},{4,16},{5,17},{6,24},{7,25},{8,2},{9,3},{1... | collective-permute-start | bytes 12296 | tf_op jit(solution)/shard_map/ppermute | solution.py:44
  11.4 2.6 %collective-permute-start.1 = (f32[2,512]{1,0:T(2,128)S(1)}, f32[2,512]{1,0:T(2,128)S(1)}, u32[]{:S(2)}, u32[]{:S(2)}) collective-permute-start(f32[2,512]{1,0:T(2,128)S(1)} %get-tuple-element.21), channel_id=1, source_target_pairs={{0,1},{1,0},{2,9},{3,8},{4,17},{5,16},{6,25},{7,24},{8,3},{9,2},{1... | collective-permute-start | bytes 12296 | tf_op jit(solution)/shard_map/ppermute | solution.py:44
  14.0 0.5 collective-permute-done
  14.5 2.7 %collective-permute-done.1 = f32[2,512]{1,0:T(2,128)S(1)} collective-permute-done((f32[2,512]{1,0:T(2,128)S(1)}, f32[2,512]{1,0:T(2,128)S(1)}, u32[]{:S(2)}, u32[]{:S(2)}) %collective-permute-start.1) | collective-permute-done | bytes 4128 | tf_op jit(solution)/shard_map/ppermute | solution.py:44
  17.2 36.2 %all-gather = f32[32,2,512]{2,1,0:T(2,128)S(1)} all-gather(f32[2,2,512]{2,1,0:T(2,128)S(1)} %pad_maximum_fusion.1), channel_id=2, replica_groups=mesh['mp'=16,'trow'=4,'y'=4,'core'=2] {'mp'}, dimensions={0}, use_global_device_ids=true | all-gather | bytes 139264 | tf_op jit(solution)/shard_map/all_gather | solution.py:88
  53.6 16.7 %all_to_all.35 = f32[4,64,512]{2,1,0:T(8,128)S(1)} all-to-all(f32[4,64,512]{2,1,0:T(8,128)S(1)} %broadcast_in_dim.22), channel_id=1, replica_groups=mesh['mp'=16,'trow'=4,'y'=4,'core'=2] {'trow'}, dimensions={0} | all-to-all | bytes 1048576 | tf_op jit(solution)/shard_map/all_to_all | solution.py:24
  70.4 2.3 %fusion = f32[128,1024]{1,0:T(8,128)S(1)} fusion(f32[128,512]{1,0:T(8,128)S(1)} %bitcast.33, f32[1,1024,512]{2,1,0:T(8,128)S(1)} %copy-done.1), kind=kOutput, calls=%fused_computation.29 | convolution fusion | flops 805306368 | bytes 2883584 | tf_op jit(solution)/shard_map/dot_general | solution.py:14
  72.7 1.9 collective-permute-start.2
  74.6 1.9 collective-permute-done.2
  76.5 2.3 %convolution_add_fusion = f32[128,1024]{1,0:T(8,128)S(1)} fusion(f32[128,1024]{1,0:T(8,128)S(1)} %collective-permute-done.2, f32[128,512]{1,0:T(8,128)S(1)} %bitcast.32, f32[1,1024,512]{2,1,0:T(8,128)S(1)} %copy-done.1), kind=kOutput, calls=%fused_computation | convolution fusion | flops 805437440 | bytes 3407872 | tf_op jit(solution)/shard_map/dot_general | solution.py:14
  78.8 11.7 %all_to_all.36 = f32[4,32,1024]{2,1,0:T(8,128)S(1)} all-to-all(f32[4,32,1024]{2,1,0:T(8,128)S(1)} %bitcast.31), channel_id=1, replica_groups=mesh['mp'=16,'trow'=4,'y'=4,'core'=2] {'y'}, dimensions={0} | all-to-all | bytes 1048576 | tf_op jit(solution)/shard_map/all_to_all | solution.py:24
  90.6 20.6 %all_to_all.37 = f32[16,2,1024]{2,1,0:T(2,128)S(1)} all-to-all(f32[16,2,1024]{2,1,0:T(2,128)S(1)} %reshape.114), channel_id=1, replica_groups=mesh['mp'=16,'trow'=4,'y'=4,'core'=2] {'mp'}, dimensions={0} | all-to-all | bytes 262144 | tf_op jit(solution)/shard_map/all_to_all | solution.py:24
  111.3 0.1 multiply_reduce_fusion.4
  111.5 29.0 %all-gather.3 = f32[16,2,1024]{2,1,0:T(2,128)S(1)} all-gather(f32[1,2,1024]{2,1,0:T(2,128)S(1)} %bitcast.36), channel_id=3, replica_groups=mesh['mp'=16,'trow'=4,'y'=4,'core'=2] {'mp'}, dimensions={0}, use_global_device_ids=true | all-gather | bytes 139264 | tf_op jit(solution)/shard_map/all_gather | solution.py:101
  140.6 11.9 %all_to_all.38.first_ref = f32[4,32,1024]{2,1,0:T(8,128)S(1)} all-to-all(f32[4,32,1024]{2,1,0:T(8,128)S(1)} %broadcast_in_dim.46), channel_id=1, replica_groups=mesh['mp'=16,'trow'=4,'y'=4,'core'=2] {'trow'}, dimensions={0} | all-to-all | bytes 1048576 | tf_op jit(solution)/shard_map/all_to_all | solution.py:24
  152.5 1.2 copy-done
  153.7 2.3 %shard_map.50 = (f32[32,64]{1,0:T(8,128)S(1)}, f32[4,32,1024]{2,1,0:T(8,128)S(1)}) custom-call(f32[4,32,1024]{2,1,0:T(8,128)S(1)} %all_to_all.38.first_ref, f32[8,64,512]{2,1,0:T(8,128)S(1)} %bitcast.28), custom_call_target="tpu_custom_call" | custom-call | flops 33554432 | bytes 2097152 | tf_op jit(solution)/shard_map/pallas_call | solution.py:63
  156.0 10.5 %all_to_all.39 = f32[4,32,1024]{2,1,0:T(8,128)S(1)} all-to-all(f32[4,32,1024]{2,1,0:T(8,128)S(1)} %get-tuple-element.6), channel_id=1, replica_groups=mesh['mp'=16,'trow'=4,'y'=4,'core'=2] {'trow'}, dimensions={0} | all-to-all | bytes 1048576 | tf_op jit(solution)/shard_map/all_to_all | solution.py:24
  166.5 0.7 reshape.115
  167.2 3.5 %all-to-all-start.5 = ((f32[16,2,1088]{2,1,0:T(2,128)}), f32[16,2,1088]{2,1,0:T(2,128)S(1)}, u32[]{:S(2)}, u32[]{:S(2)}) async-start(f32[16,2,1088]{2,1,0:T(2,128)} %reshape.115), calls=%async_computation.6 | async-start | bytes 294912 | tf_op jit(solution)/shard_map/all_to_all | solution.py:24
  170.9 13.1 %all-to-all-done.5 = f32[16,2,1088]{2,1,0:T(2,128)S(1)} async-done(((f32[16,2,1088]{2,1,0:T(2,128)}), f32[16,2,1088]{2,1,0:T(2,128)S(1)}, u32[]{:S(2)}, u32[]{:S(2)}) %all-to-all-start.5) | async-done | bytes 139296 | tf_op jit(solution)/shard_map/all_to_all | solution.py:24
  184.0 0.2 multiply_reduce_fusion.3
  184.3 0.2 multiply_reduce_fusion.1
  184.5 0.2 multiply_reduce_fusion
  185.1 0.1 concatenate.7
  185.2 7.6 %all_to_all.40 = f32[4,2,5]{2,1,0:T(2,128)S(1)} all-to-all(f32[4,2,5]{2,1,0:T(2,128)S(1)} %broadcast_in_dim.50), channel_id=1, replica_groups=mesh['mp'=16,'trow'=4,'y'=4,'core'=2] {'trow'}, dimensions={0} | all-to-all | bytes 320 | tf_op jit(solution)/shard_map/all_to_all | solution.py:24
  193.2 0.2 multiply_reduce_fusion.5
  193.4 0.2 add_reduce_fusion.1
  193.6 0.1 copy.64
  193.8 0.2 add_reduce_fusion
  194.0 0.7 multiply_subtract_fusion
  (45 shorter events, 1.8 us)
Async XLA Ops:
  7.2 0.8 copy-start.2
  7.2 104.3 %reduce-scatter.2.cloned.1.call-start = ((), (), s32[]{:S(2)}) async-start(), calls=%async_computation.8 | async-start | bytes 2228224 | tf_op jit(solution)/shard_map/reduce_scatter | solution.py:86
  7.9 62.5 %copy-start.1 = (f32[1,1024,512]{2,1,0:T(8,128)S(1)}, f32[1,1024,512]{2,1,0:T(8,128)}, u32[]{:S(2)}) copy-start(f32[1,1024,512]{2,1,0:T(8,128)} %param.3) | copy-start | bytes 6291460
  7.9 144.6 %all-gather.6.cloned.1.call-start = ((), (), s32[]{:S(2)}) async-start(), calls=%async_computation.9 | async-start | bytes 1179648 | tf_op jit(solution)/shard_map/all_gather | solution.py:99
  8.0 6.5 %collective-permute-start = (f32[2,512]{1,0:T(2,128)S(1)}, f32[2,512]{1,0:T(2,128)S(1)}, u32[]{:S(2)}, u32[]{:S(2)}) collective-permute-start(f32[2,512]{1,0:T(2,128)S(1)} %get-tuple-element.20), channel_id=1, source_target_pairs={{0,0},{1,1},{2,8},{3,9},{4,16},{5,17},{6,24},{7,25},{8,2},{9,3},{1... | collective-permute-start | bytes 12296 | tf_op jit(solution)/shard_map/ppermute | solution.py:44
  11.4 5.8 %collective-permute-start.1 = (f32[2,512]{1,0:T(2,128)S(1)}, f32[2,512]{1,0:T(2,128)S(1)}, u32[]{:S(2)}, u32[]{:S(2)}) collective-permute-start(f32[2,512]{1,0:T(2,128)S(1)} %get-tuple-element.21), channel_id=1, source_target_pairs={{0,1},{1,0},{2,9},{3,8},{4,17},{5,16},{6,25},{7,24},{8,3},{9,2},{1... | collective-permute-start | bytes 12296 | tf_op jit(solution)/shard_map/ppermute | solution.py:44
  72.7 3.8 %collective-permute-start.2 = (f32[128,1024]{1,0:T(8,128)S(1)}, f32[128,1024]{1,0:T(8,128)S(1)}, u32[]{:S(2)}, u32[]{:S(2)}) collective-permute-start(f32[128,1024]{1,0:T(8,128)S(1)} %fusion), channel_id=1, source_target_pairs={{0,1},{1,0},{2,3},{3,2},{4,5},{5,4},{6,7},{7,6},{8,9},{9,8},{10,11... | collective-permute-start | bytes 1572872 | tf_op jit(solution)/shard_map/ppermute | solution.py:92
  76.5 34.8 %copy-start.3 = (f32[2,1024]{1,0:T(2,128)S(1)}, f32[2,1024]{1,0:T(2,128)}, u32[]{:S(2)}) copy-start(f32[2,1024]{1,0:T(2,128)} %param.4) | copy-start | bytes 24580
  152.5 1.2 copy-start
  167.2 16.7 %all-to-all-start.5 = ((f32[16,2,1088]{2,1,0:T(2,128)}), f32[16,2,1088]{2,1,0:T(2,128)S(1)}, u32[]{:S(2)}, u32[]{:S(2)}) async-start(f32[16,2,1088]{2,1,0:T(2,128)} %reshape.115), calls=%async_computation.6 | async-start | bytes 294912 | tf_op jit(solution)/shard_map/all_to_all | solution.py:24
Sparse Core Ops, SparseCore 0:
  10.8 77.7 reduce-scatter.1
  111.6 19.9 all-gather.5

commit v6 on v5

--- a/solution.py
+++ b/solution.py
@@ -85,7 +85,7 @@
 
     part = lax.psum_scatter(tile, "mp", scatter_dimension=0, tiled=True)
 
-    over_mp = lax.all_gather(transposed(guess, sizes), "mp", axis=0)
+    over_mp = spread(transposed(guess, sizes), "mp", mp)
     over_mp = over_mp.transpose(1, 0, 2, 3).reshape(2 * mp * own, cols)
     block = spread(over_mp, "trow", trow).reshape(trow, 2, mp * own, cols)
     given = dot(block[:, 1].reshape(trow * mp * own, cols), tile, 1, 1)
@@ -98,7 +98,7 @@
     part, _ = lax.optimization_barrier((part, first))
     total = lax.all_gather(part, TCOL, axis=0)
 
-    wide = lax.all_gather(first, "mp", axis=0).reshape(mp * own, rows)
+    wide = spread(first, "mp", mp).reshape(mp * own, rows)
     second, terms = both_images(spread(wide, "trow", trow), total, trow)
     terms = exchange(terms, "trow").sum(0)
     pieces = jnp.concatenate([terms, second], axis=1).reshape(mp, own, rows + share)

time: 202 us -> 191 us (0.946)
  the two profiles are of different devices: /device:TPU:8 before, /device:TPU:32 now
where the time goes in v6:
time: 191 us; the launch traced here: 190 us
  blocking collectives  130 us (68%)
  waiting for transfers between devices  17.5 us (9%)
  starting transfers between devices  15.6 us (8%)
  between operations  14.3 us (7%)
  matrix products  4.56 us (2%)
  local copies, waits for them, and re-layouts  3.67 us (2%)
  Pallas kernels  2.25 us (1%)
  other arithmetic  2.19 us (1%)
    all_to_all x8, blocking collectives, exchange(): return lax.all_to_all(pieces, axes, 0, 0, tiled=True)  130 us
    all_to_all x1, waiting for transfers between devices, exchange(): return lax.all_to_all(pieces, axes, 0, 0, tiled=True)  13.8 us
    all_to_all x1, starting transfers between devices, exchange(): return lax.all_to_all(pieces, axes, 0, 0, tiled=True)  10.9 us
    dot_general x2, matrix products, dot(): lax.dot_general(lhs, rhs, (((lhs_dim,), (rhs_dim,)), ((), ())), precision...  4.56 us
  transfers between devices with their start and end apart: 6, of which 3 were waited for; matrix products, arithmetic and copies ran while one was open for 3% of the time, Pallas kernels for 0%

profile of v6, /device:TPU:32, one launch (start us, length us, event | category | flops | bytes accessed | tf_op | source)
XLA Modules:
  0.0 190.5 jit_solution(3009500748451649817)
XLA Ops:
  7.2 0.7 reduce-scatter.2.cloned.1.call-update
  8.0 0.8 collective-permute-start
  8.8 1.9 %collective-permute-start.1 = (f32[2,512]{1,0:T(2,128)S(1)}, f32[2,512]{1,0:T(2,128)S(1)}, u32[]{:S(2)}, u32[]{:S(2)}) collective-permute-start(f32[2,512]{1,0:T(2,128)S(1)} %get-tuple-element.21), channel_id=1, source_target_pairs={{0,1},{1,0},{2,9},{3,8},{4,17},{5,16},{6,25},{7,24},{8,3},{9,2},{1... | collective-permute-start | bytes 12296 | tf_op jit(solution)/shard_map/ppermute | solution.py:44
  10.7 1.1 collective-permute-done.1
  11.9 28.9 %all_to_all.45 = f32[16,2,2,512]{3,2,1,0:T(2,128)S(1)} all-to-all(f32[16,2,2,512]{3,2,1,0:T(2,128)S(1)} %broadcast_in_dim.25), channel_id=1, replica_groups=mesh['mp'=16,'trow'=4,'y'=4,'core'=2] {'mp'}, dimensions={0} | all-to-all | bytes 262144 | tf_op jit(solution)/shard_map/all_to_all | solution.py:24
  41.0 23.3 %all_to_all.46 = f32[4,64,512]{2,1,0:T(8,128)S(1)} all-to-all(f32[4,64,512]{2,1,0:T(8,128)S(1)} %broadcast_in_dim.27), channel_id=1, replica_groups=mesh['mp'=16,'trow'=4,'y'=4,'core'=2] {'trow'}, dimensions={0} | all-to-all | bytes 1048576 | tf_op jit(solution)/shard_map/all_to_all | solution.py:24
  64.3 2.3 %fusion = f32[128,1024]{1,0:T(8,128)S(1)} fusion(f32[128,512]{1,0:T(8,128)S(1)} %bitcast.29, f32[1,1024,512]{2,1,0:T(8,128)S(1)} %copy-done.1), kind=kOutput, calls=%fused_computation.28 | convolution fusion | flops 805306368 | bytes 2883584 | tf_op jit(solution)/shard_map/dot_general | solution.py:14
  66.6 1.9 %collective-permute-start.2 = (f32[128,1024]{1,0:T(8,128)S(1)}, f32[128,1024]{1,0:T(8,128)S(1)}, u32[]{:S(2)}, u32[]{:S(2)}) collective-permute-start(f32[128,1024]{1,0:T(8,128)S(1)} %fusion), channel_id=1, source_target_pairs={{0,1},{1,0},{2,3},{3,2},{4,5},{5,4},{6,7},{7,6},{8,9},{9,8},{10,11... | collective-permute-start | bytes 1572872 | tf_op jit(solution)/shard_map/ppermute | solution.py:92
  68.6 1.9 collective-permute-done.2
  70.4 2.3 %convolution_add_fusion = f32[128,1024]{1,0:T(8,128)S(1)} fusion(f32[128,1024]{1,0:T(8,128)S(1)} %collective-permute-done.2, f32[128,512]{1,0:T(8,128)S(1)} %bitcast.28, f32[1,1024,512]{2,1,0:T(8,128)S(1)} %copy-done.1), kind=kOutput, calls=%fused_computation | convolution fusion | flops 805437440 | bytes 3407872 | tf_op jit(solution)/shard_map/dot_general | solution.py:14
  72.7 12.5 %all_to_all.47 = f32[4,32,1024]{2,1,0:T(8,128)S(1)} all-to-all(f32[4,32,1024]{2,1,0:T(8,128)S(1)} %bitcast.27), channel_id=1, replica_groups=mesh['mp'=16,'trow'=4,'y'=4,'core'=2] {'y'}, dimensions={0} | all-to-all | bytes 1048576 | tf_op jit(solution)/shard_map/all_to_all | solution.py:24
  85.3 19.1 %all_to_all.48 = f32[16,2,1024]{2,1,0:T(2,128)S(1)} all-to-all(f32[16,2,1024]{2,1,0:T(2,128)S(1)} %reshape.116), channel_id=1, replica_groups=mesh['mp'=16,'trow'=4,'y'=4,'core'=2] {'mp'}, dimensions={0} | all-to-all | bytes 262144 | tf_op jit(solution)/shard_map/all_to_all | solution.py:24
  104.5 0.1 multiply_reduce_fusion.4
  104.7 17.1 %all_to_all.49 = f32[16,2,1024]{2,1,0:T(2,128)S(1)} all-to-all(f32[16,2,1024]{2,1,0:T(2,128)S(1)} %broadcast_in_dim.28), channel_id=1, replica_groups=mesh['mp'=16,'trow'=4,'y'=4,'core'=2] {'mp'}, dimensions={0} | all-to-all | bytes 262144 | tf_op jit(solution)/shard_map/all_to_all | solution.py:24
  121.9 11.4 %all_to_all.50.first_ref = f32[4,32,1024]{2,1,0:T(8,128)S(1)} all-to-all(f32[4,32,1024]{2,1,0:T(8,128)S(1)} %broadcast_in_dim.30), channel_id=1, replica_groups=mesh['mp'=16,'trow'=4,'y'=4,'core'=2] {'trow'}, dimensions={0} | all-to-all | bytes 1048576 | tf_op jit(solution)/shard_map/all_to_all | solution.py:24
  133.3 1.2 copy-done
  134.5 2.3 %shard_map.50 = (f32[32,64]{1,0:T(8,128)S(1)}, f32[4,32,1024]{2,1,0:T(8,128)S(1)}) custom-call(f32[4,32,1024]{2,1,0:T(8,128)S(1)} %all_to_all.50.first_ref, f32[8,64,512]{2,1,0:T(8,128)S(1)} %bitcast.24), custom_call_target="tpu_custom_call" | custom-call | flops 33554432 | bytes 2097152 | tf_op jit(solution)/shard_map/pallas_call | solution.py:63
  136.8 10.5 %all_to_all.51 = f32[4,32,1024]{2,1,0:T(8,128)S(1)} all-to-all(f32[4,32,1024]{2,1,0:T(8,128)S(1)} %get-tuple-element.6), channel_id=1, replica_groups=mesh['mp'=16,'trow'=4,'y'=4,'core'=2] {'trow'}, dimensions={0} | all-to-all | bytes 1048576 | tf_op jit(solution)/shard_map/all_to_all | solution.py:24
  147.3 0.7 reshape.117
  148.1 10.9 %all-to-all-start.7 = ((f32[16,2,1088]{2,1,0:T(2,128)}), f32[16,2,1088]{2,1,0:T(2,128)S(1)}, u32[]{:S(2)}, u32[]{:S(2)}) async-start(f32[16,2,1088]{2,1,0:T(2,128)} %reshape.117), calls=%async_computation.8 | async-start | bytes 294912 | tf_op jit(solution)/shard_map/all_to_all | solution.py:24
  159.1 13.8 %all-to-all-done.7 = f32[16,2,1088]{2,1,0:T(2,128)S(1)} async-done(((f32[16,2,1088]{2,1,0:T(2,128)}), f32[16,2,1088]{2,1,0:T(2,128)S(1)}, u32[]{:S(2)}, u32[]{:S(2)}) %all-to-all-start.7) | async-done | bytes 139296 | tf_op jit(solution)/shard_map/all_to_all | solution.py:24
  173.0 0.2 multiply_reduce_fusion.3
  173.2 0.2 multiply_reduce_fusion.1
  173.5 0.2 multiply_reduce_fusion
  174.1 0.1 concatenate.7
  174.2 7.6 %all_to_all.52 = f32[4,2,5]{2,1,0:T(2,128)S(1)} all-to-all(f32[4,2,5]{2,1,0:T(2,128)S(1)} %broadcast_in_dim.64), channel_id=1, replica_groups=mesh['mp'=16,'trow'=4,'y'=4,'core'=2] {'trow'}, dimensions={0} | all-to-all | bytes 320 | tf_op jit(solution)/shard_map/all_to_all | solution.py:24
  181.9 0.1 copy.59
  182.2 0.2 multiply_reduce_fusion.5
  182.3 0.2 add_reduce_fusion.1
  182.5 0.1 copy.62
  182.7 0.2 add_reduce_fusion
  182.9 0.7 multiply_subtract_fusion
  (47 shorter events, 1.8 us)
Async XLA Ops:
  7.2 0.8 copy-start.2
  7.2 97.4 %reduce-scatter.2.cloned.1.call-start = ((), (), s32[]{:S(2)}) async-start(), calls=%async_computation.10 | async-start | bytes 2228224 | tf_op jit(solution)/shard_map/reduce_scatter | solution.py:86
  7.9 56.4 %copy-start.1 = (f32[1,1024,512]{2,1,0:T(8,128)S(1)}, f32[1,1024,512]{2,1,0:T(8,128)}, u32[]{:S(2)}) copy-start(f32[1,1024,512]{2,1,0:T(8,128)} %param.3) | copy-start | bytes 6291460
  7.9 125.4 %all-gather.3.cloned.1.call-start = ((), (), s32[]{:S(2)}) async-start(), calls=%async_computation.11 | async-start | bytes 1179648 | tf_op jit(solution)/shard_map/all_gather | solution.py:99
  8.0 2.7 %collective-permute-start = (f32[2,512]{1,0:T(2,128)S(1)}, f32[2,512]{1,0:T(2,128)S(1)}, u32[]{:S(2)}, u32[]{:S(2)}) collective-permute-start(f32[2,512]{1,0:T(2,128)S(1)} %get-tuple-element.20), channel_id=1, source_target_pairs={{0,0},{1,1},{2,8},{3,9},{4,16},{5,17},{6,24},{7,25},{8,2},{9,3},{1... | collective-permute-start | bytes 12296 | tf_op jit(solution)/shard_map/ppermute | solution.py:44
  8.8 3.1 %collective-permute-start.1 = (f32[2,512]{1,0:T(2,128)S(1)}, f32[2,512]{1,0:T(2,128)S(1)}, u32[]{:S(2)}, u32[]{:S(2)}) collective-permute-start(f32[2,512]{1,0:T(2,128)S(1)} %get-tuple-element.21), channel_id=1, source_target_pairs={{0,1},{1,0},{2,9},{3,8},{4,17},{5,16},{6,25},{7,24},{8,3},{9,2},{1... | collective-permute-start | bytes 12296 | tf_op jit(solution)/shard_map/ppermute | solution.py:44
  66.6 3.8 %collective-permute-start.2 = (f32[128,1024]{1,0:T(8,128)S(1)}, f32[128,1024]{1,0:T(8,128)S(1)}, u32[]{:S(2)}, u32[]{:S(2)}) collective-permute-start(f32[128,1024]{1,0:T(8,128)S(1)} %fusion), channel_id=1, source_target_pairs={{0,1},{1,0},{2,3},{3,2},{4,5},{5,4},{6,7},{7,6},{8,9},{9,8},{10,11... | collective-permute-start | bytes 1572872 | tf_op jit(solution)/shard_map/ppermute | solution.py:92
  70.4 34.0 %copy-start.3 = (f32[2,1024]{1,0:T(2,128)S(1)}, f32[2,1024]{1,0:T(2,128)}, u32[]{:S(2)}) copy-start(f32[2,1024]{1,0:T(2,128)} %param.4) | copy-start | bytes 24580
  133.3 1.2 copy-start
  148.1 24.9 %all-to-all-start.7 = ((f32[16,2,1088]{2,1,0:T(2,128)}), f32[16,2,1088]{2,1,0:T(2,128)S(1)}, u32[]{:S(2)}, u32[]{:S(2)}) async-start(f32[16,2,1088]{2,1,0:T(2,128)} %reshape.117), calls=%async_computation.8 | async-start | bytes 294912 | tf_op jit(solution)/shard_map/all_to_all | solution.py:24
Sparse Core Ops, SparseCore 0:
  10.8 77.3 reduce-scatter.1
  104.8 23.2 all-gather.2

commit v7 on v6

--- a/solution.py
+++ b/solution.py
@@ -45,34 +45,47 @@
     return jnp.stack(got)
 
 
-def both_images(first, total, trow):
-    blocks, part, cols = total.shape
-    _, count, wide = first.shape
-    each = wide // cols
-
-    def body(first_ref, total_ref, second_ref, third_ref):
-        second = jnp.zeros((count, part), jnp.float32)
-        for n in range(blocks):
-            x, at = n // each, n % each * cols
-            second += dot(first_ref[x, :, at : at + cols], total_ref[n], 1, 1)
-        second_ref[...] = second
-        for n in range(blocks):
-            x, at = n // each, n % each * cols
-            third_ref[x, :, at : at + cols] = dot(second, total_ref[n], 1, 0)
-
+def vmem_call(body, out_shape, flops, *args):
+    place = pl.BlockSpec(memory_space=pltpu.VMEM)
+    moved = 4 * sum(arg.size for arg in args) + 4 * out_shape.size
     return pl.pallas_call(
         body,
-        out_shape=(
-            jax.ShapeDtypeStruct((count, part), jnp.float32),
-            jax.ShapeDtypeStruct(first.shape, jnp.float32),
-        ),
-        in_specs=[pl.BlockSpec(memory_space=pltpu.VMEM)] * 2,
-        out_specs=(pl.BlockSpec(memory_space=pltpu.VMEM),) * 2,
-        cost_estimate=pl.CostEstimate(
-            flops=4 * count * total.size, bytes_accessed=4 * (total.size + 2 * first.size), transcendentals=0
-        ),
+        out_shape=out_shape,
+        in_specs=[place] * len(args),
+        out_specs=place,
+        cost_estimate=pl.CostEstimate(flops=flops, bytes_accessed=moved, transcendentals=0),
         compiler_params=pltpu.CompilerParams(vmem_limit_bytes=16 * 2**20),
-    )(first, total)
+    )(*args)
+
+
+def partial_second(first, total, copies):
+    count, part = first.shape[0], total.shape[0]
+
+    def body(first_ref, total_ref, out_ref):
+        second = dot(first_ref[...], total_ref[...], 1, 1)
+        for n in range(copies):
+            out_ref[n] = second
+
+    out = jax.ShapeDtypeStruct((copies, count, part), jnp.float32)
+    return vmem_call(body, out, 2 * count * total.size, first, total)
+
+
+def partial_third(shares, total, pieces):
+    count, part = shares.shape[1:]
+    rows = total.shape[1]
+    own = count // pieces
+
+    def body(shares_ref, total_ref, out_ref):
+        second = shares_ref[0]
+        for n in range(1, shares.shape[0]):
+            second += shares_ref[n]
+        third = dot(second, total_ref[...], 1, 0)
+        for n in range(pieces):
+            out_ref[n, :, :rows] = third[n * own : (n + 1) * own]
+            out_ref[n, :, rows:] = second[n * own : (n + 1) * own]
+
+    out = jax.ShapeDtypeStruct((pieces, own, rows + part), jnp.float32)
+    return vmem_call(body, out, 2 * count * total.size, shares, total)
 
 
 def shards(sizes, gram, rhs, guess):
@@ -81,9 +94,9 @@
     tile = gram[0]
     rows, cols = tile.shape
     own = rhs.shape[0]
-    share = rows // mp
+    share = cols // mp
 
-    part = lax.psum_scatter(tile, "mp", scatter_dimension=0, tiled=True)
+    part = lax.psum_scatter(tile.T, "mp", scatter_dimension=0, tiled=True)
 
     over_mp = spread(transposed(guess, sizes), "mp", mp)
     over_mp = over_mp.transpose(1, 0, 2, 3).reshape(2 * mp * own, cols)
@@ -92,19 +105,19 @@
     given = lax.ppermute(given, "core", [(0, 1), (1, 0)])
     terms = dot(block[:, 0].reshape(trow * mp * own, cols), tile, 1, 1) + given
     terms = exchange(terms.reshape(y, mp * own, rows), "y").sum(0)
+    part, _ = lax.optimization_barrier((part, terms))
     terms = exchange(terms.reshape(mp, own, rows), "mp").sum(0)
     first = rhs - terms
 
-    part, _ = lax.optimization_barrier((part, first))
-    total = lax.all_gather(part, TCOL, axis=0)
+    total = lax.all_gather(part, TCOL, axis=0, tiled=True)
 
     wide = spread(first, "mp", mp).reshape(mp * own, rows)
-    second, terms = both_images(spread(wide, "trow", trow), total, trow)
-    terms = exchange(terms, "trow").sum(0)
-    pieces = jnp.concatenate([terms, second], axis=1).reshape(mp, own, rows + share)
-    pieces = exchange(pieces, "mp")
+    shares = exchange(partial_second(wide, total, trow), "trow")
+    pieces = exchange(partial_third(shares, total, mp), "mp")
     third = pieces[:, :, :rows].sum(0)
-    second = pieces[:, :, rows:].transpose(1, 0, 2).reshape(own, rows)
+    second = pieces[:, :, rows:].reshape(mp, own, trow, core, share)
+    second = lax.dynamic_index_in_dim(second, lax.axis_index("trow"), 2, keepdims=False)
+    second = second.transpose(1, 2, 0, 3).reshape(own, rows)
 
     def inner(u, v):
         return jnp.sum(u * v, axis=1, keepdims=True)

time: 191 us -> 182 us (0.953)
  the two profiles are of different devices: /device:TPU:32 before, /device:TPU:2 now
where the time goes in v7:
time: 182 us
  blocking collectives  115 us (63%)
  waiting for transfers between devices  25 us (14%)
  between operations  14.3 us (8%)
  starting transfers between devices  11.9 us (7%)
  local copies, waits for them, and re-layouts  6.62 us (4%)
  matrix products  4.57 us (3%)
  Pallas kernels  2.37 us (1%)
  other arithmetic  2.14 us (1%)
    all_to_all x7, blocking collectives, exchange(): return lax.all_to_all(pieces, axes, 0, 0, tiled=True)  115 us
    all_to_all x1, waiting for transfers between devices, exchange(): return lax.all_to_all(pieces, axes, 0, 0, tiled=True)  14.4 us
    ppermute x2, starting transfers between devices, transposed(): got.append(lax.ppermute(sent, PLANE, pairs))  5.89 us
    reduce_scatter x1, waiting for transfers between devices, shards(): part = lax.psum_scatter(tile.T, 'mp', scatter_dimension=0, tiled=True)  5.32 us
    unnamed x17, local copies, waits for them, and re-layouts  5.28 us
    dot_general x2, matrix products, dot(): lax.dot_general(lhs, rhs, (((lhs_dim,), (rhs_dim,)), ((), ())), precision...  4.57 us
    all_to_all x1, starting transfers between devices, exchange(): return lax.all_to_all(pieces, axes, 0, 0, tiled=True)  4.03 us
  transfers between devices with their start and end apart: 6, of which 5 were waited for; matrix products, arithmetic and copies ran while one was open for 3% of the time, Pallas kernels for 0%

profile of v7, /device:TPU:2, one launch (start us, length us, event | category | flops | bytes accessed | tf_op | source)
XLA Modules:
  0.0 181.5 jit_solution(7170340067213954256)
XLA Ops:
  7.2 3.0 %copy.51 = f32[1,1024,512]{1,2,0:T(8,128)} copy(f32[1,1024,512]{2,1,0:T(8,128)} %param.3) | data formatting | bytes 4194304 | tf_op args[0]
  10.3 0.6 copy-done.3
  10.9 3.4 %collective-permute-start = (f32[2,512]{1,0:T(2,128)S(1)}, f32[2,512]{1,0:T(2,128)S(1)}, u32[]{:S(2)}, u32[]{:S(2)}) collective-permute-start(f32[2,512]{1,0:T(2,128)S(1)} %get-tuple-element.16), channel_id=1, source_target_pairs={{0,0},{1,1},{2,8},{3,9},{4,16},{5,17},{6,24},{7,25},{8,2},{9,3},{1... | collective-permute-start | bytes 12296 | tf_op jit(solution)/shard_map/ppermute | solution.py:44
  14.3 2.4 %collective-permute-start.1 = (f32[2,512]{1,0:T(2,128)S(1)}, f32[2,512]{1,0:T(2,128)S(1)}, u32[]{:S(2)}, u32[]{:S(2)}) collective-permute-start(f32[2,512]{1,0:T(2,128)S(1)} %get-tuple-element.17), channel_id=1, source_target_pairs={{0,1},{1,0},{2,9},{3,8},{4,17},{5,16},{6,25},{7,24},{8,3},{9,2},{1... | collective-permute-start | bytes 12296 | tf_op jit(solution)/shard_map/ppermute | solution.py:44
  16.8 0.5 collective-permute-done
  17.3 2.9 %collective-permute-done.1 = f32[2,512]{1,0:T(2,128)S(1)} collective-permute-done((f32[2,512]{1,0:T(2,128)S(1)}, f32[2,512]{1,0:T(2,128)S(1)}, u32[]{:S(2)}, u32[]{:S(2)}) %collective-permute-start.1) | collective-permute-done | bytes 4128 | tf_op jit(solution)/shard_map/ppermute | solution.py:44
  20.2 30.7 %all_to_all.40 = f32[16,2,2,512]{3,2,1,0:T(2,128)S(1)} all-to-all(f32[16,2,2,512]{3,2,1,0:T(2,128)S(1)} %broadcast_in_dim.21), channel_id=1, replica_groups=mesh['mp'=16,'trow'=4,'y'=4,'core'=2] {'mp'}, dimensions={0} | all-to-all | bytes 262144 | tf_op jit(solution)/shard_map/all_to_all | solution.py:24
  51.1 15.4 %all_to_all.41 = f32[4,64,512]{2,1,0:T(8,128)S(1)} all-to-all(f32[4,64,512]{2,1,0:T(8,128)S(1)} %broadcast_in_dim.23), channel_id=1, replica_groups=mesh['mp'=16,'trow'=4,'y'=4,'core'=2] {'trow'}, dimensions={0} | all-to-all | bytes 1048576 | tf_op jit(solution)/shard_map/all_to_all | solution.py:24
  66.5 2.3 %fusion = f32[128,1024]{1,0:T(8,128)S(1)} fusion(f32[128,512]{1,0:T(8,128)S(1)} %bitcast.38, f32[1,1024,512]{2,1,0:T(8,128)S(1)} %copy-done.2), kind=kOutput, calls=%fused_computation | convolution fusion | flops 805306368 | bytes 2883584 | tf_op jit(solution)/shard_map/dot_general | solution.py:14
  68.8 1.9 %collective-permute-start.2 = (f32[128,1024]{1,0:T(8,128)S(1)}, f32[128,1024]{1,0:T(8,128)S(1)}, u32[]{:S(2)}, u32[]{:S(2)}) collective-permute-start(f32[128,1024]{1,0:T(8,128)S(1)} %fusion), channel_id=1, source_target_pairs={{0,1},{1,0},{2,3},{3,2},{4,5},{5,4},{6,7},{7,6},{8,9},{9,8},{10,11... | collective-permute-start | bytes 1572872 | tf_op jit(solution)/shard_map/ppermute | solution.py:105
  70.7 1.9 %collective-permute-done.2 = f32[128,1024]{1,0:T(8,128)S(1)} collective-permute-done((f32[128,1024]{1,0:T(8,128)S(1)}, f32[128,1024]{1,0:T(8,128)S(1)}, u32[]{:S(2)}, u32[]{:S(2)}) %collective-permute-start.2) | collective-permute-done | bytes 524320 | tf_op jit(solution)/shard_map/ppermute | solution.py:105
  72.6 2.3 %fusion.4 = f32[128,1024]{1,0:T(8,128)S(1)} fusion(f32[128,1024]{1,0:T(8,128)S(1)} %collective-permute-done.2, f32[128,512]{1,0:T(8,128)S(1)} %bitcast.37, f32[1,1024,512]{2,1,0:T(8,128)S(1)} %copy-done.2), kind=kOutput, calls=%fused_computation.4 | convolution fusion | flops 805437440 | bytes 3407872 | tf_op jit(solution)/shard_map/dot_general | solution.py:14
  74.9 12.5 %all_to_all.42 = f32[4,32,1024]{2,1,0:T(8,128)S(1)} all-to-all(f32[4,32,1024]{2,1,0:T(8,128)S(1)} %bitcast.36), channel_id=1, replica_groups=mesh['mp'=16,'trow'=4,'y'=4,'core'=2] {'y'}, dimensions={0} | all-to-all | bytes 1048576 | tf_op jit(solution)/shard_map/all_to_all | solution.py:24
  87.4 5.3 %reduce-scatter.2.cloned.1.call-done = f32[32,1024]{1,0:T(8,128)} async-done(((f32[512,1024]{1,0:T(8,128)}), f32[32,1024]{1,0:T(8,128)}) %reduce-scatter.2.cloned.1.call-update) | async-done | bytes 131088 | tf_op jit(solution)/shard_map/reduce_scatter | solution.py:99
  92.8 21.6 %all_to_all.43 = f32[16,2,1024]{2,1,0:T(2,128)S(1)} all-to-all(f32[16,2,1024]{2,1,0:T(2,128)S(1)} %reshape.118), channel_id=1, replica_groups=mesh['mp'=16,'trow'=4,'y'=4,'core'=2] {'mp'}, dimensions={0} | all-to-all | bytes 262144 | tf_op jit(solution)/shard_map/all_to_all | solution.py:24
  114.5 0.1 multiply_reduce_fusion.4
  114.6 16.9 %all_to_all.44 = f32[16,2,1024]{2,1,0:T(2,128)S(1)} all-to-all(f32[16,2,1024]{2,1,0:T(2,128)S(1)} %broadcast_in_dim.24), channel_id=1, replica_groups=mesh['mp'=16,'trow'=4,'y'=4,'core'=2] {'mp'}, dimensions={0} | all-to-all | bytes 262144 | tf_op jit(solution)/shard_map/all_to_all | solution.py:24
  131.7 1.2 copy-done
  132.9 1.0 shard_map.50
  133.9 9.9 %all_to_all.45.shares_ref = f32[4,32,256]{2,1,0:T(8,128)S(1)} all-to-all(f32[4,32,256]{2,1,0:T(8,128)S(1)} %shard_map.50), channel_id=1, replica_groups=mesh['mp'=16,'trow'=4,'y'=4,'core'=2] {'trow'}, dimensions={0} | all-to-all | bytes 262144 | tf_op jit(solution)/shard_map/all_to_all | solution.py:24
  143.8 1.3 shard_map.51
  145.1 4.0 %all-to-all-start.6 = ((f32[16,2,1280]{2,1,0:T(2,128)}), f32[16,2,1280]{2,1,0:T(2,128)S(1)}, u32[]{:S(2)}, u32[]{:S(2)}) async-start(f32[16,2,1280]{2,1,0:T(2,128)} %shard_map.51), calls=%async_computation.7 | async-start | bytes 327680 | tf_op jit(solution)/shard_map/all_to_all | solution.py:24
  149.3 14.4 %all-to-all-done.6 = f32[16,2,1280]{2,1,0:T(2,128)S(1)} async-done(((f32[16,2,1280]{2,1,0:T(2,128)}), f32[16,2,1280]{2,1,0:T(2,128)S(1)}, u32[]{:S(2)}, u32[]{:S(2)}) %all-to-all-start.6) | async-done | bytes 163872 | tf_op jit(solution)/shard_map/all_to_all | solution.py:24
  163.7 0.2 reshape.120
  164.0 0.2 multiply_reduce_fusion.3
  164.3 0.2 multiply_reduce_fusion.1
  164.5 0.2 multiply_reduce_fusion
  165.2 7.7 %all_to_all.46 = f32[4,2,5]{2,1,0:T(2,128)S(1)} all-to-all(f32[4,2,5]{2,1,0:T(2,128)S(1)} %broadcast_in_dim.28), channel_id=1, replica_groups=mesh['mp'=16,'trow'=4,'y'=4,'core'=2] {'trow'}, dimensions={0} | all-to-all | bytes 320 | tf_op jit(solution)/shard_map/all_to_all | solution.py:24
  173.2 0.2 multiply_reduce_fusion.5
  173.4 0.2 add_reduce_fusion.1
  173.8 0.2 add_reduce_fusion
  174.0 0.7 multiply_subtract_fusion
  (48 shorter events, 2.0 us)
Async XLA Ops:
  7.2 85.6 %reduce-scatter.2.cloned.1.call-start = ((), (), s32[]{:S(2)}) async-start(), calls=%async_computation.9 | async-start | bytes 2228224 | tf_op jit(solution)/shard_map/reduce_scatter | solution.py:99
  10.2 0.7 copy-start.3
  10.2 56.3 %copy-start.2 = (f32[1,1024,512]{2,1,0:T(8,128)S(1)}, f32[1,1024,512]{2,1,0:T(8,128)}, u32[]{:S(2)}) copy-start(f32[1,1024,512]{2,1,0:T(8,128)} %param.3) | copy-start | bytes 6291460
  10.2 121.5 %all-gather.2.cloned.1.call-start = ((), (), s32[]{:S(2)}) async-start(), calls=%async_computation.10 | async-start | bytes 1179648 | tf_op jit(solution)/shard_map/all_gather | solution.py:112
  10.9 6.4 %collective-permute-start = (f32[2,512]{1,0:T(2,128)S(1)}, f32[2,512]{1,0:T(2,128)S(1)}, u32[]{:S(2)}, u32[]{:S(2)}) collective-permute-start(f32[2,512]{1,0:T(2,128)S(1)} %get-tuple-element.16), channel_id=1, source_target_pairs={{0,0},{1,1},{2,8},{3,9},{4,16},{5,17},{6,24},{7,25},{8,2},{9,3},{1... | collective-permute-start | bytes 12296 | tf_op jit(solution)/shard_map/ppermute | solution.py:44
  14.3 5.8 %collective-permute-start.1 = (f32[2,512]{1,0:T(2,128)S(1)}, f32[2,512]{1,0:T(2,128)S(1)}, u32[]{:S(2)}, u32[]{:S(2)}) collective-permute-start(f32[2,512]{1,0:T(2,128)S(1)} %get-tuple-element.17), channel_id=1, source_target_pairs={{0,1},{1,0},{2,9},{3,8},{4,17},{5,16},{6,25},{7,24},{8,3},{9,2},{1... | collective-permute-start | bytes 12296 | tf_op jit(solution)/shard_map/ppermute | solution.py:44
  68.8 3.8 %collective-permute-start.2 = (f32[128,1024]{1,0:T(8,128)S(1)}, f32[128,1024]{1,0:T(8,128)S(1)}, u32[]{:S(2)}, u32[]{:S(2)}) collective-permute-start(f32[128,1024]{1,0:T(8,128)S(1)} %fusion), channel_id=1, source_target_pairs={{0,1},{1,0},{2,3},{3,2},{4,5},{5,4},{6,7},{7,6},{8,9},{9,8},{10,11... | collective-permute-start | bytes 1572872 | tf_op jit(solution)/shard_map/ppermute | solution.py:105
  74.9 39.5 %copy-start.4 = (f32[2,1024]{1,0:T(2,128)S(1)}, f32[2,1024]{1,0:T(2,128)}, u32[]{:S(2)}) copy-start(f32[2,1024]{1,0:T(2,128)} %param.4) | copy-start | bytes 24580
  131.7 1.2 copy-start
  132.9 10.9 %copy-start.1 = (f32[256,1024]{1,0:T(8,128)S(1)}, f32[256,1024]{1,0:T(8,128)}, u32[]{:S(2)}) copy-start(f32[256,1024]{1,0:T(8,128)} %all-gather.2.cloned.1.call-done.total_ref) | copy-start | bytes 3145732
  145.1 18.6 %all-to-all-start.6 = ((f32[16,2,1280]{2,1,0:T(2,128)}), f32[16,2,1280]{2,1,0:T(2,128)S(1)}, u32[]{:S(2)}, u32[]{:S(2)}) async-start(f32[16,2,1280]{2,1,0:T(2,128)} %shard_map.51), calls=%async_computation.7 | async-start | bytes 327680 | tf_op jit(solution)/shard_map/all_to_all | solution.py:24
Sparse Core Ops, SparseCore 0:
  10.8 81.8 reduce-scatter.1
  94.9 28.6 all-gather.1

commit v8 on v7

--- a/solution.py
+++ b/solution.py
@@ -7,6 +7,7 @@
 
 TCOL = ("y", "core")
 PLANE = ("trow",) + TCOL
+HINT = 10**10
 HIGHEST = lax.Precision.HIGHEST
 
 
@@ -47,15 +48,35 @@
 
 def vmem_call(body, out_shape, flops, *args):
     place = pl.BlockSpec(memory_space=pltpu.VMEM)
-    moved = 4 * sum(arg.size for arg in args) + 4 * out_shape.size
+    outs = jax.tree.leaves(out_shape)
+    moved = 4 * sum(array.size for array in list(args) + outs)
     return pl.pallas_call(
         body,
         out_shape=out_shape,
         in_specs=[place] * len(args),
-        out_specs=place,
+        out_specs=jax.tree.map(lambda _: place, out_shape),
         cost_estimate=pl.CostEstimate(flops=flops, bytes_accessed=moved, transcendentals=0),
         compiler_params=pltpu.CompilerParams(vmem_limit_bytes=16 * 2**20),
     )(*args)
+
+
+def f32(*shape):
+    return jax.ShapeDtypeStruct(shape, jnp.float32)
+
+
+def remainder(terms, rhs, flops):
+    count = terms.shape[0]
+
+    def body(terms_ref, rhs_ref, first_ref, out_ref):
+        total = terms_ref[0]
+        for n in range(1, count):
+            total += terms_ref[n]
+        first = rhs_ref[...] - total
+        first_ref[...] = first
+        for n in range(count):
+            out_ref[n] = first
+
+    return vmem_call(body, (f32(*rhs.shape), f32(*terms.shape)), flops, terms, rhs)
 
 
 def partial_second(first, total, copies):
@@ -66,7 +87,7 @@
         for n in range(copies):
             out_ref[n] = second
 
-    out = jax.ShapeDtypeStruct((copies, count, part), jnp.float32)
+    out = f32(copies, count, part)
     return vmem_call(body, out, 2 * count * total.size, first, total)
 
 
@@ -84,8 +105,75 @@
             out_ref[n, :, :rows] = third[n * own : (n + 1) * own]
             out_ref[n, :, rows:] = second[n * own : (n + 1) * own]
 
-    out = jax.ShapeDtypeStruct((pieces, own, rows + part), jnp.float32)
+    out = f32(pieces, own, rows + part)
     return vmem_call(body, out, 2 * count * total.size, shares, total)
+
+
+def inner(u, v):
+    return jnp.sum(u * v, axis=1, keepdims=True)
+
+
+def inverse(x):
+    return jnp.where(x > 0, 1.0 / jnp.where(x > 0, x, 1.0), 0.0)
+
+
+def coordinates(first, second, pieces, copies):
+    own, rows = first.shape
+
+    def body(first_ref, second_ref, pieces_ref, third_ref, out_ref):
+        first, second = first_ref[...], second_ref[...]
+        third = pieces_ref[0, :, :rows]
+        for n in range(1, pieces.shape[0]):
+            third += pieces_ref[n, :, :rows]
+        third_ref[...] = third
+        f0 = jnp.sqrt(inner(first, first))
+        e0 = first * inverse(f0)
+        s0 = inner(e0, second)
+        rest = second - s0 * e0
+        s1 = jnp.sqrt(inner(rest, rest))
+        e1 = rest * inverse(s1)
+        t0 = inner(e0, third)
+        t1 = inner(e1, third - t0 * e0)
+        lane = lax.broadcasted_iota(jnp.int32, (own, 128), 1)
+        packed = jnp.zeros((own, 128), jnp.float32)
+        for n, number in enumerate((f0, s0, s1, t0, t1)):
+            packed = jnp.where(lane == n, number, packed)
+        for n in range(copies):
+            out_ref[n] = packed
+
+    return vmem_call(body, (f32(own, rows), f32(copies, own, 128)), pieces.size, first, second, pieces)
+
+
+def combined(known, guess, first, second, third):
+    blocks = known.shape[0]
+
+    def body(known_ref, guess_ref, first_ref, second_ref, third_ref, merged_ref, residual_ref):
+        parts = [known_ref[n] for n in range(blocks)]
+        f0, s0, s1, t0, t1 = ([part[:, n : n + 1] for part in parts] for n in range(5))
+
+        def total(*products):
+            return sum(u * v for us, vs in products for u, v in zip(us, vs))
+
+        norm_first = total((f0, f0))
+        alpha = norm_first / total((f0, s0))
+        r0 = [f - alpha * s for f, s in zip(f0, s0)]
+        r1 = [-alpha * s for s in s1]
+        norm_next = total((r0, r0), (r1, r1))
+        beta = norm_next / norm_first
+        d0 = [r + beta * f for r, f in zip(r0, f0)]
+        i0 = [s - alpha * t + beta * s for s, t in zip(s0, t0)]
+        i1 = [s - alpha * t + beta * s for s, t in zip(s1, t1)]
+        alpha_next = norm_next / total((d0, i0), (r1, i1))
+
+        first, second = first_ref[...], second_ref[...]
+        residual = first - alpha * second
+        direction = residual + beta * first
+        image = second - alpha * third_ref[...] + beta * second
+        merged_ref[...] = guess_ref[...] + alpha * first + alpha_next * direction
+        residual_ref[...] = residual - alpha_next * image
+
+    out = (f32(*guess.shape), f32(*guess.shape))
+    return vmem_call(body, out, 16 * guess.size, known, guess, first, second, third)
 
 
 def shards(sizes, gram, rhs, guess):
@@ -106,50 +194,19 @@
     terms = dot(block[:, 0].reshape(trow * mp * own, cols), tile, 1, 1) + given
     terms = exchange(terms.reshape(y, mp * own, rows), "y").sum(0)
     part, _ = lax.optimization_barrier((part, terms))
-    terms = exchange(terms.reshape(mp, own, rows), "mp").sum(0)
-    first = rhs - terms
+    terms = exchange(terms.reshape(mp, own, rows), "mp")
+    first, copies = remainder(terms, rhs, HINT)
 
     total = lax.all_gather(part, TCOL, axis=0, tiled=True)
 
-    wide = spread(first, "mp", mp).reshape(mp * own, rows)
+    wide = exchange(copies, "mp").reshape(mp * own, rows)
     shares = exchange(partial_second(wide, total, trow), "trow")
     pieces = exchange(partial_third(shares, total, mp), "mp")
-    third = pieces[:, :, :rows].sum(0)
     second = pieces[:, :, rows:].reshape(mp, own, trow, core, share)
     second = lax.dynamic_index_in_dim(second, lax.axis_index("trow"), 2, keepdims=False)
     second = second.transpose(1, 2, 0, 3).reshape(own, rows)
-
-    def inner(u, v):
-        return jnp.sum(u * v, axis=1, keepdims=True)
-
-    def inverse(x):
-        return jnp.where(x > 0, 1.0 / jnp.where(x > 0, x, 1.0), 0.0)
-
-    f0 = jnp.sqrt(inner(first, first))
-    e0 = first * inverse(f0)
-    s0 = inner(e0, second)
-    rest = second - s0 * e0
-    s1 = jnp.sqrt(inner(rest, rest))
-    e1 = rest * inverse(s1)
-    t0 = inner(e0, third)
-    t1 = inner(e1, third - t0 * e0)
-    known = spread(jnp.concatenate([f0, s0, s1, t0, t1], axis=1), "trow", trow)
-    f0, s0, s1, t0, t1 = (known[:, :, n : n + 1] for n in range(5))
-
-    norm_first = jnp.sum(f0 * f0, 0)
-    alpha = norm_first / jnp.sum(f0 * s0, 0)
-    r0, r1 = f0 - alpha * s0, -alpha * s1
-    norm_next = jnp.sum(r0 * r0 + r1 * r1, 0)
-    beta = norm_next / norm_first
-    d0, d1 = r0 + beta * f0, r1
-    i0, i1 = s0 - alpha * t0 + beta * s0, s1 - alpha * t1 + beta * s1
-    alpha_next = norm_next / jnp.sum(d0 * i0 + d1 * i1, 0)
-
-    residual = first - alpha * second
-    direction = residual + beta * first
-    image = second - alpha * third + beta * second
-    merged = guess + alpha * first + alpha_next * direction
-    return merged, residual - alpha_next * image
+    third, numbers = coordinates(first, second, pieces, trow)
+    return combined(exchange(numbers, "trow"), guess, first, second, third)
 
 
 def solution(mesh):

time: 182 us -> 183 us (level)
  the two profiles are of different devices: /device:TPU:2 before, /device:TPU:32 now
where the time goes in v8:
time: 183 us; the launch traced here: 182 us
  blocking collectives  99.7 us (54%)
  waiting for transfers between devices  31 us (17%)
  starting transfers between devices  23 us (13%)
  between operations  14.2 us (8%)
  local copies, waits for them, and re-layouts  6.12 us (3%)
  matrix products  4.58 us (3%)
  Pallas kernels  3.73 us (2%)
    all_to_all x6, blocking collectives, exchange(): return lax.all_to_all(pieces, axes, 0, 0, tiled=True)  99.7 us
    all_to_all x2, waiting for transfers between devices, exchange(): return lax.all_to_all(pieces, axes, 0, 0, tiled=True)  26.9 us
    all_to_all x2, starting transfers between devices, exchange(): return lax.all_to_all(pieces, axes, 0, 0, tiled=True)  18.4 us
    unnamed x11, local copies, waits for them, and re-layouts  4.8 us
    dot_general x2, matrix products, dot(): lax.dot_general(lhs, rhs, (((lhs_dim,), (rhs_dim,)), ((), ())), precision...  4.58 us
    pallas_call x5, Pallas kernels, vmem_call(): pl.pallas_call(body, out_shape=out_shape, in_specs=[place] * len(args), o...  3.73 us
  transfers between devices with their start and end apart: 7, of which 5 were waited for; matrix products, arithmetic and copies ran while one was open for 3% of the time, Pallas kernels for 0%

profile of v8, /device:TPU:32, one launch (start us, length us, event | category | flops | bytes accessed | tf_op | source)
XLA Modules:
  0.0 182.4 jit_solution(7873398519137045131)
XLA Ops:
  7.2 2.9 %copy.10 = f32[1,1024,512]{1,2,0:T(8,128)} copy(f32[1,1024,512]{2,1,0:T(8,128)} %param.3) | data formatting | bytes 4194304 | tf_op args[0]
  10.2 0.7 copy-done.2
  10.8 0.6 collective-permute-start
  11.5 1.9 %collective-permute-start.1 = (f32[2,512]{1,0:T(2,128)S(1)}, f32[2,512]{1,0:T(2,128)S(1)}, u32[]{:S(2)}, u32[]{:S(2)}) collective-permute-start(f32[2,512]{1,0:T(2,128)S(1)} %get-tuple-element.15), channel_id=1, source_target_pairs={{0,1},{1,0},{2,9},{3,8},{4,17},{5,16},{6,25},{7,24},{8,3},{9,2},{1... | collective-permute-start | bytes 12296 | tf_op jit(solution)/shard_map/ppermute | solution.py:45
  13.4 1.1 collective-permute-done.1
  14.6 29.5 %all_to_all.40 = f32[16,2,2,512]{3,2,1,0:T(2,128)S(1)} all-to-all(f32[16,2,2,512]{3,2,1,0:T(2,128)S(1)} %broadcast_in_dim.6), channel_id=1, replica_groups=mesh['mp'=16,'trow'=4,'y'=4,'core'=2] {'mp'}, dimensions={0} | all-to-all | bytes 262144 | tf_op jit(solution)/shard_map/all_to_all | solution.py:25
  44.1 0.1 broadcast_in_dim.14
  44.2 0.1 broadcast_in_dim.15
  44.3 23.1 %all_to_all.41 = f32[4,64,512]{2,1,0:T(8,128)S(1)} all-to-all(f32[4,64,512]{2,1,0:T(8,128)S(1)} %broadcast_in_dim.15), channel_id=1, replica_groups=mesh['mp'=16,'trow'=4,'y'=4,'core'=2] {'trow'}, dimensions={0} | all-to-all | bytes 1048576 | tf_op jit(solution)/shard_map/all_to_all | solution.py:25
  67.4 2.3 %fusion = f32[128,1024]{1,0:T(8,128)S(1)} fusion(f32[128,512]{1,0:T(8,128)S(1)} %bitcast.31, f32[1,1024,512]{2,1,0:T(8,128)S(1)} %copy-done.4), kind=kOutput, calls=%fused_computation | convolution fusion | flops 805306368 | bytes 2883584 | tf_op jit(solution)/shard_map/dot_general | solution.py:15
  69.7 1.9 %collective-permute-start.2 = (f32[128,1024]{1,0:T(8,128)S(1)}, f32[128,1024]{1,0:T(8,128)S(1)}, u32[]{:S(2)}, u32[]{:S(2)}) collective-permute-start(f32[128,1024]{1,0:T(8,128)S(1)} %fusion), channel_id=1, source_target_pairs={{0,1},{1,0},{2,3},{3,2},{4,5},{5,4},{6,7},{7,6},{8,9},{9,8},{10,11... | collective-permute-start | bytes 1572872 | tf_op jit(solution)/shard_map/ppermute | solution.py:193
  71.6 1.9 %collective-permute-done.2 = f32[128,1024]{1,0:T(8,128)S(1)} collective-permute-done((f32[128,1024]{1,0:T(8,128)S(1)}, f32[128,1024]{1,0:T(8,128)S(1)}, u32[]{:S(2)}, u32[]{:S(2)}) %collective-permute-start.2) | collective-permute-done | bytes 524320 | tf_op jit(solution)/shard_map/ppermute | solution.py:193
  73.5 2.3 %fusion.4 = f32[128,1024]{1,0:T(8,128)S(1)} fusion(f32[128,1024]{1,0:T(8,128)S(1)} %collective-permute-done.2, f32[128,512]{1,0:T(8,128)S(1)} %bitcast.30, f32[1,1024,512]{2,1,0:T(8,128)S(1)} %copy-done.4), kind=kOutput, calls=%fused_computation.4 | convolution fusion | flops 805437440 | bytes 3407872 | tf_op jit(solution)/shard_map/dot_general | solution.py:15
  75.8 12.5 %all_to_all.42 = f32[4,32,1024]{2,1,0:T(8,128)S(1)} all-to-all(f32[4,32,1024]{2,1,0:T(8,128)S(1)} %bitcast.29), channel_id=1, replica_groups=mesh['mp'=16,'trow'=4,'y'=4,'core'=2] {'y'}, dimensions={0} | all-to-all | bytes 1048576 | tf_op jit(solution)/shard_map/all_to_all | solution.py:25
  88.3 0.7 reshape.26
  89.0 5.7 %all-to-all-start.3 = ((f32[16,2,1024]{2,1,0:T(2,128)}), f32[16,2,1024]{2,1,0:T(2,128)S(1)}, u32[]{:S(2)}, u32[]{:S(2)}) async-start(f32[16,2,1024]{2,1,0:T(2,128)} %reshape.26), calls=%async_computation.3 | async-start | bytes 262144 | tf_op jit(solution)/shard_map/all_to_all | solution.py:25
  94.8 0.7 all-gather.2.cloned.1.call-update
  95.5 12.8 %all-to-all-done.3.terms_ref = f32[16,2,1024]{2,1,0:T(2,128)S(1)} async-done(((f32[16,2,1024]{2,1,0:T(2,128)}), f32[16,2,1024]{2,1,0:T(2,128)S(1)}, u32[]{:S(2)}, u32[]{:S(2)}) %all-to-all-start.3) | async-done | bytes 131104 | tf_op jit(solution)/shard_map/all_to_all | solution.py:25
  108.3 17.0 %all_to_all.43 = f32[16,2,1024]{2,1,0:T(2,128)S(1)} all-to-all(f32[16,2,1024]{2,1,0:T(2,128)S(1)} %get-tuple-element.8), channel_id=1, replica_groups=mesh['mp'=16,'trow'=4,'y'=4,'core'=2] {'mp'}, dimensions={0} | all-to-all | bytes 262144 | tf_op jit(solution)/shard_map/all_to_all | solution.py:25
  125.4 0.1 reshape.27.first_ref
  125.4 0.4 all-gather.2.cloned.1.call-done.total_ref
  125.9 1.2 copy-done
  127.1 1.0 shard_map.51
  128.1 10.0 %all_to_all.44.shares_ref = f32[4,32,256]{2,1,0:T(8,128)S(1)} all-to-all(f32[4,32,256]{2,1,0:T(8,128)S(1)} %shard_map.51), channel_id=1, replica_groups=mesh['mp'=16,'trow'=4,'y'=4,'core'=2] {'trow'}, dimensions={0} | all-to-all | bytes 262144 | tf_op jit(solution)/shard_map/all_to_all | solution.py:25
  138.2 1.4 shard_map.52
  139.5 12.7 %all-to-all-start.6 = ((f32[16,2,1280]{2,1,0:T(2,128)}), f32[16,2,1280]{2,1,0:T(2,128)S(1)}, u32[]{:S(2)}, u32[]{:S(2)}) async-start(f32[16,2,1280]{2,1,0:T(2,128)} %shard_map.52), calls=%async_computation.7 | async-start | bytes 327680 | tf_op jit(solution)/shard_map/all_to_all | solution.py:25
  152.2 14.1 %all-to-all-done.6.pieces_ref = f32[16,2,1280]{2,1,0:T(2,128)S(1)} async-done(((f32[16,2,1280]{2,1,0:T(2,128)}), f32[16,2,1280]{2,1,0:T(2,128)S(1)}, u32[]{:S(2)}, u32[]{:S(2)}) %all-to-all-start.6) | async-done | bytes 163872 | tf_op jit(solution)/shard_map/all_to_all | solution.py:25
  166.3 0.2 reshape.28
  166.5 0.1 reshape.29.second_ref
  166.6 0.4 shard_map.53
  167.0 7.6 %all_to_all.45.known_ref = f32[4,2,128]{2,1,0:T(2,128)S(1)} all-to-all(f32[4,2,128]{2,1,0:T(2,128)S(1)} %get-tuple-element.10), channel_id=1, replica_groups=mesh['mp'=16,'trow'=4,'y'=4,'core'=2] {'trow'}, dimensions={0} | all-to-all | bytes 8192 | tf_op jit(solution)/shard_map/all_to_all | solution.py:25
  174.6 0.9 shard_map.54
  (23 shorter events, 0.3 us)
Async XLA Ops:
  7.2 87.7 %reduce-scatter.2.cloned.1.call-start = ((), (), s32[]{:S(2)}) async-start(), calls=%async_computation.9 | async-start | bytes 2228224 | tf_op jit(solution)/shard_map/reduce_scatter | solution.py:187
  10.1 0.7 copy-start.2
  10.1 57.2 %copy-start.4 = (f32[1,1024,512]{2,1,0:T(8,128)S(1)}, f32[1,1024,512]{2,1,0:T(8,128)}, u32[]{:S(2)}) copy-start(f32[1,1024,512]{2,1,0:T(8,128)} %param.3) | copy-start | bytes 6291460
  10.8 2.6 %collective-permute-start = (f32[2,512]{1,0:T(2,128)S(1)}, f32[2,512]{1,0:T(2,128)S(1)}, u32[]{:S(2)}, u32[]{:S(2)}) collective-permute-start(f32[2,512]{1,0:T(2,128)S(1)} %get-tuple-element.14), channel_id=1, source_target_pairs={{0,0},{1,1},{2,8},{3,9},{4,16},{5,17},{6,24},{7,25},{8,2},{9,3},{1... | collective-permute-start | bytes 12296 | tf_op jit(solution)/shard_map/ppermute | solution.py:45
  11.5 3.1 %collective-permute-start.1 = (f32[2,512]{1,0:T(2,128)S(1)}, f32[2,512]{1,0:T(2,128)S(1)}, u32[]{:S(2)}, u32[]{:S(2)}) collective-permute-start(f32[2,512]{1,0:T(2,128)S(1)} %get-tuple-element.15), channel_id=1, source_target_pairs={{0,1},{1,0},{2,9},{3,8},{4,17},{5,16},{6,25},{7,24},{8,3},{9,2},{1... | collective-permute-start | bytes 12296 | tf_op jit(solution)/shard_map/ppermute | solution.py:45
  69.7 3.8 %collective-permute-start.2 = (f32[128,1024]{1,0:T(8,128)S(1)}, f32[128,1024]{1,0:T(8,128)S(1)}, u32[]{:S(2)}, u32[]{:S(2)}) collective-permute-start(f32[128,1024]{1,0:T(8,128)S(1)} %fusion), channel_id=1, source_target_pairs={{0,1},{1,0},{2,3},{3,2},{4,5},{5,4},{6,7},{7,6},{8,9},{9,8},{10,11... | collective-permute-start | bytes 1572872 | tf_op jit(solution)/shard_map/ppermute | solution.py:193
  73.5 34.8 %copy-start.3 = (f32[2,1024]{1,0:T(2,128)S(1)}, f32[2,1024]{1,0:T(2,128)}, u32[]{:S(2)}) copy-start(f32[2,1024]{1,0:T(2,128)} %rhs_ref.1) | copy-start | bytes 24580
  89.0 19.2 %all-to-all-start.3 = ((f32[16,2,1024]{2,1,0:T(2,128)}), f32[16,2,1024]{2,1,0:T(2,128)S(1)}, u32[]{:S(2)}, u32[]{:S(2)}) async-start(f32[16,2,1024]{2,1,0:T(2,128)} %reshape.26), calls=%async_computation.3 | async-start | bytes 262144 | tf_op jit(solution)/shard_map/all_to_all | solution.py:25
  94.8 31.1 %all-gather.2.cloned.1.call-start = ((), (), s32[]{:S(2)}) async-start(), calls=%async_computation.10 | async-start | bytes 1179648 | tf_op jit(solution)/shard_map/all_gather | solution.py:200
  125.9 1.2 copy-start
  127.1 11.1 %copy-start.1 = (f32[256,1024]{1,0:T(8,128)S(1)}, f32[256,1024]{1,0:T(8,128)}, u32[]{:S(2)}) copy-start(f32[256,1024]{1,0:T(8,128)} %all-gather.2.cloned.1.call-done.total_ref) | copy-start | bytes 3145732
  139.5 26.7 %all-to-all-start.6 = ((f32[16,2,1280]{2,1,0:T(2,128)}), f32[16,2,1280]{2,1,0:T(2,128)S(1)}, u32[]{:S(2)}, u32[]{:S(2)}) async-start(f32[16,2,1280]{2,1,0:T(2,128)} %shard_map.52), calls=%async_computation.7 | async-start | bytes 327680 | tf_op jit(solution)/shard_map/all_to_all | solution.py:25
Sparse Core Ops, SparseCore 0:
  10.8 80.1 reduce-scatter.1
  97.7 28.0 all-gather.1

commit v9 on v8

--- a/solution.py
+++ b/solution.py
@@ -7,7 +7,6 @@
 
 TCOL = ("y", "core")
 PLANE = ("trow",) + TCOL
-HINT = 10**10
 HIGHEST = lax.Precision.HIGHEST
 
 
@@ -64,7 +63,7 @@
     return jax.ShapeDtypeStruct(shape, jnp.float32)
 
 
-def remainder(terms, rhs, flops):
+def remainder(terms, rhs):
     count = terms.shape[0]
 
     def body(terms_ref, rhs_ref, first_ref, out_ref):
@@ -76,7 +75,7 @@
         for n in range(count):
             out_ref[n] = first
 
-    return vmem_call(body, (f32(*rhs.shape), f32(*terms.shape)), flops, terms, rhs)
+    return vmem_call(body, (f32(*rhs.shape), f32(*terms.shape)), terms.size, terms, rhs)
 
 
 def partial_second(first, total, copies):
@@ -195,7 +194,7 @@
     terms = exchange(terms.reshape(y, mp * own, rows), "y").sum(0)
     part, _ = lax.optimization_barrier((part, terms))
     terms = exchange(terms.reshape(mp, own, rows), "mp")
-    first, copies = remainder(terms, rhs, HINT)
+    first, copies = remainder(terms, rhs)
 
     total = lax.all_gather(part, TCOL, axis=0, tiled=True)
 

time: 183 us -> 181 us (0.989)
  the two profiles are of different devices: /device:TPU:32 before, /device:TPU:2 now
where the time goes in v9:
time: 181 us; the launch traced here: 180 us
  blocking collectives  115 us (64%)
  waiting for transfers between devices  24.7 us (14%)
  between operations  14.2 us (8%)
  starting transfers between devices  11.9 us (7%)
  local copies, waits for them, and re-layouts  5.41 us (3%)
  matrix products  4.58 us (3%)
  Pallas kernels  3.71 us (2%)
    all_to_all x7, blocking collectives, exchange(): return lax.all_to_all(pieces, axes, 0, 0, tiled=True)  115 us
    all_to_all x1, waiting for transfers between devices, exchange(): return lax.all_to_all(pieces, axes, 0, 0, tiled=True)  14.4 us
    ppermute x2, starting transfers between devices, transposed(): got.append(lax.ppermute(sent, PLANE, pairs))  5.89 us
    reduce_scatter x1, waiting for transfers between devices, shards(): part = lax.psum_scatter(tile.T, 'mp', scatter_dimension=0, tiled=True)  4.94 us
    unnamed x11, local copies, waits for them, and re-layouts  4.75 us
    dot_general x2, matrix products, dot(): lax.dot_general(lhs, rhs, (((lhs_dim,), (rhs_dim,)), ((), ())), precision...  4.58 us
    all_to_all x1, starting transfers between devices, exchange(): return lax.all_to_all(pieces, axes, 0, 0, tiled=True)  4.03 us
    pallas_call x5, Pallas kernels, vmem_call(): pl.pallas_call(body, out_shape=out_shape, in_specs=[place] * len(args), o...  3.71 us
  transfers between devices with their start and end apart: 6, of which 5 were waited for; matrix products, arithmetic and copies ran while one was open for 3% of the time, Pallas kernels for 0%

profile of v9, /device:TPU:2, one launch (start us, length us, event | category | flops | bytes accessed | tf_op | source)
XLA Modules:
  0.0 179.9 jit_solution(17292657804178603639)
XLA Ops:
  7.2 2.9 %copy.10 = f32[1,1024,512]{1,2,0:T(8,128)} copy(f32[1,1024,512]{2,1,0:T(8,128)} %param.3) | data formatting | bytes 4194304 | tf_op args[0]
  10.2 0.0 all-gather.2.cloned.1.call-start
  10.2 0.6 copy-done.2
  10.8 3.4 %collective-permute-start = (f32[2,512]{1,0:T(2,128)S(1)}, f32[2,512]{1,0:T(2,128)S(1)}, u32[]{:S(2)}, u32[]{:S(2)}) collective-permute-start(f32[2,512]{1,0:T(2,128)S(1)} %get-tuple-element.14), channel_id=1, source_target_pairs={{0,0},{1,1},{2,8},{3,9},{4,16},{5,17},{6,24},{7,25},{8,2},{9,3},{1... | collective-permute-start | bytes 12296 | tf_op jit(solution)/shard_map/ppermute | solution.py:44
  14.3 2.4 %collective-permute-start.1 = (f32[2,512]{1,0:T(2,128)S(1)}, f32[2,512]{1,0:T(2,128)S(1)}, u32[]{:S(2)}, u32[]{:S(2)}) collective-permute-start(f32[2,512]{1,0:T(2,128)S(1)} %get-tuple-element.15), channel_id=1, source_target_pairs={{0,1},{1,0},{2,9},{3,8},{4,17},{5,16},{6,25},{7,24},{8,3},{9,2},{1... | collective-permute-start | bytes 12296 | tf_op jit(solution)/shard_map/ppermute | solution.py:44
  16.7 0.5 collective-permute-done
  17.2 2.9 %collective-permute-done.1 = f32[2,512]{1,0:T(2,128)S(1)} collective-permute-done((f32[2,512]{1,0:T(2,128)S(1)}, f32[2,512]{1,0:T(2,128)S(1)}, u32[]{:S(2)}, u32[]{:S(2)}) %collective-permute-start.1) | collective-permute-done | bytes 4128 | tf_op jit(solution)/shard_map/ppermute | solution.py:44
  20.2 30.6 %all_to_all.40 = f32[16,2,2,512]{3,2,1,0:T(2,128)S(1)} all-to-all(f32[16,2,2,512]{3,2,1,0:T(2,128)S(1)} %broadcast_in_dim.6), channel_id=1, replica_groups=mesh['mp'=16,'trow'=4,'y'=4,'core'=2] {'mp'}, dimensions={0} | all-to-all | bytes 262144 | tf_op jit(solution)/shard_map/all_to_all | solution.py:24
  50.8 0.1 broadcast_in_dim.14
  50.9 0.1 broadcast_in_dim.15
  50.9 15.5 %all_to_all.41 = f32[4,64,512]{2,1,0:T(8,128)S(1)} all-to-all(f32[4,64,512]{2,1,0:T(8,128)S(1)} %broadcast_in_dim.15), channel_id=1, replica_groups=mesh['mp'=16,'trow'=4,'y'=4,'core'=2] {'trow'}, dimensions={0} | all-to-all | bytes 1048576 | tf_op jit(solution)/shard_map/all_to_all | solution.py:24
  66.5 2.3 %fusion = f32[128,1024]{1,0:T(8,128)S(1)} fusion(f32[128,512]{1,0:T(8,128)S(1)} %bitcast.31, f32[1,1024,512]{2,1,0:T(8,128)S(1)} %copy-done.4), kind=kOutput, calls=%fused_computation | convolution fusion | flops 805306368 | bytes 2883584 | tf_op jit(solution)/shard_map/dot_general | solution.py:14
  68.8 1.9 %collective-permute-start.2 = (f32[128,1024]{1,0:T(8,128)S(1)}, f32[128,1024]{1,0:T(8,128)S(1)}, u32[]{:S(2)}, u32[]{:S(2)}) collective-permute-start(f32[128,1024]{1,0:T(8,128)S(1)} %fusion), channel_id=1, source_target_pairs={{0,1},{1,0},{2,3},{3,2},{4,5},{5,4},{6,7},{7,6},{8,9},{9,8},{10,11... | collective-permute-start | bytes 1572872 | tf_op jit(solution)/shard_map/ppermute | solution.py:192
  70.7 1.9 %collective-permute-done.2 = f32[128,1024]{1,0:T(8,128)S(1)} collective-permute-done((f32[128,1024]{1,0:T(8,128)S(1)}, f32[128,1024]{1,0:T(8,128)S(1)}, u32[]{:S(2)}, u32[]{:S(2)}) %collective-permute-start.2) | collective-permute-done | bytes 524320 | tf_op jit(solution)/shard_map/ppermute | solution.py:192
  72.6 2.3 %fusion.4 = f32[128,1024]{1,0:T(8,128)S(1)} fusion(f32[128,1024]{1,0:T(8,128)S(1)} %collective-permute-done.2, f32[128,512]{1,0:T(8,128)S(1)} %bitcast.30, f32[1,1024,512]{2,1,0:T(8,128)S(1)} %copy-done.4), kind=kOutput, calls=%fused_computation.4 | convolution fusion | flops 805437440 | bytes 3407872 | tf_op jit(solution)/shard_map/dot_general | solution.py:14
  74.9 12.5 %all_to_all.42 = f32[4,32,1024]{2,1,0:T(8,128)S(1)} all-to-all(f32[4,32,1024]{2,1,0:T(8,128)S(1)} %bitcast.29), channel_id=1, replica_groups=mesh['mp'=16,'trow'=4,'y'=4,'core'=2] {'y'}, dimensions={0} | all-to-all | bytes 1048576 | tf_op jit(solution)/shard_map/all_to_all | solution.py:24
  87.4 4.9 %reduce-scatter.2.cloned.1.call-done = f32[32,1024]{1,0:T(8,128)} async-done(((f32[512,1024]{1,0:T(8,128)}), f32[32,1024]{1,0:T(8,128)}) %reduce-scatter.2.cloned.1.call-update) | async-done | bytes 131088 | tf_op jit(solution)/shard_map/reduce_scatter | solution.py:186
  92.4 0.1 reshape.26
  92.5 21.9 %all_to_all.43.terms_ref = f32[16,2,1024]{2,1,0:T(2,128)S(1)} all-to-all(f32[16,2,1024]{2,1,0:T(2,128)S(1)} %reshape.26), channel_id=1, replica_groups=mesh['mp'=16,'trow'=4,'y'=4,'core'=2] {'mp'}, dimensions={0} | all-to-all | bytes 262144 | tf_op jit(solution)/shard_map/all_to_all | solution.py:24
  114.4 16.8 %all_to_all.44 = f32[16,2,1024]{2,1,0:T(2,128)S(1)} all-to-all(f32[16,2,1024]{2,1,0:T(2,128)S(1)} %get-tuple-element.8), channel_id=1, replica_groups=mesh['mp'=16,'trow'=4,'y'=4,'core'=2] {'mp'}, dimensions={0} | all-to-all | bytes 262144 | tf_op jit(solution)/shard_map/all_to_all | solution.py:24
  131.2 0.1 reshape.27.first_ref
  131.4 1.2 copy-done
  132.6 1.0 shard_map.51
  133.6 10.4 %all_to_all.45.shares_ref = f32[4,32,256]{2,1,0:T(8,128)S(1)} all-to-all(f32[4,32,256]{2,1,0:T(8,128)S(1)} %shard_map.51), channel_id=1, replica_groups=mesh['mp'=16,'trow'=4,'y'=4,'core'=2] {'trow'}, dimensions={0} | all-to-all | bytes 262144 | tf_op jit(solution)/shard_map/all_to_all | solution.py:24
  144.0 1.4 shard_map.52
  145.4 4.0 %all-to-all-start.6 = ((f32[16,2,1280]{2,1,0:T(2,128)}), f32[16,2,1280]{2,1,0:T(2,128)S(1)}, u32[]{:S(2)}, u32[]{:S(2)}) async-start(f32[16,2,1280]{2,1,0:T(2,128)} %shard_map.52), calls=%async_computation.7 | async-start | bytes 327680 | tf_op jit(solution)/shard_map/all_to_all | solution.py:24
  149.4 14.4 %all-to-all-done.6.pieces_ref = f32[16,2,1280]{2,1,0:T(2,128)S(1)} async-done(((f32[16,2,1280]{2,1,0:T(2,128)}), f32[16,2,1280]{2,1,0:T(2,128)S(1)}, u32[]{:S(2)}, u32[]{:S(2)}) %all-to-all-start.6) | async-done | bytes 163872 | tf_op jit(solution)/shard_map/all_to_all | solution.py:24
  163.9 0.2 reshape.28
  164.1 0.1 reshape.29.second_ref
  164.1 0.4 shard_map.53
  164.5 7.6 %all_to_all.46.known_ref = f32[4,2,128]{2,1,0:T(2,128)S(1)} all-to-all(f32[4,2,128]{2,1,0:T(2,128)S(1)} %get-tuple-element.10), channel_id=1, replica_groups=mesh['mp'=16,'trow'=4,'y'=4,'core'=2] {'trow'}, dimensions={0} | all-to-all | bytes 8192 | tf_op jit(solution)/shard_map/all_to_all | solution.py:24
  172.2 0.9 shard_map.54
  (22 shorter events, 0.3 us)
Async XLA Ops:
  7.2 85.2 %reduce-scatter.2.cloned.1.call-start = ((), (), s32[]{:S(2)}) async-start(), calls=%async_computation.9 | async-start | bytes 2228224 | tf_op jit(solution)/shard_map/reduce_scatter | solution.py:186
  10.1 0.7 copy-start.2
  10.1 56.4 %copy-start.4 = (f32[1,1024,512]{2,1,0:T(8,128)S(1)}, f32[1,1024,512]{2,1,0:T(8,128)}, u32[]{:S(2)}) copy-start(f32[1,1024,512]{2,1,0:T(8,128)} %param.3) | copy-start | bytes 6291460
  10.2 121.2 %all-gather.2.cloned.1.call-start = ((), (), s32[]{:S(2)}) async-start(), calls=%async_computation.10 | async-start | bytes 1179648 | tf_op jit(solution)/shard_map/all_gather | solution.py:199
  10.8 6.4 %collective-permute-start = (f32[2,512]{1,0:T(2,128)S(1)}, f32[2,512]{1,0:T(2,128)S(1)}, u32[]{:S(2)}, u32[]{:S(2)}) collective-permute-start(f32[2,512]{1,0:T(2,128)S(1)} %get-tuple-element.14), channel_id=1, source_target_pairs={{0,0},{1,1},{2,8},{3,9},{4,16},{5,17},{6,24},{7,25},{8,2},{9,3},{1... | collective-permute-start | bytes 12296 | tf_op jit(solution)/shard_map/ppermute | solution.py:44
  14.3 5.8 %collective-permute-start.1 = (f32[2,512]{1,0:T(2,128)S(1)}, f32[2,512]{1,0:T(2,128)S(1)}, u32[]{:S(2)}, u32[]{:S(2)}) collective-permute-start(f32[2,512]{1,0:T(2,128)S(1)} %get-tuple-element.15), channel_id=1, source_target_pairs={{0,1},{1,0},{2,9},{3,8},{4,17},{5,16},{6,25},{7,24},{8,3},{9,2},{1... | collective-permute-start | bytes 12296 | tf_op jit(solution)/shard_map/ppermute | solution.py:44
  68.8 3.8 %collective-permute-start.2 = (f32[128,1024]{1,0:T(8,128)S(1)}, f32[128,1024]{1,0:T(8,128)S(1)}, u32[]{:S(2)}, u32[]{:S(2)}) collective-permute-start(f32[128,1024]{1,0:T(8,128)S(1)} %fusion), channel_id=1, source_target_pairs={{0,1},{1,0},{2,3},{3,2},{4,5},{5,4},{6,7},{7,6},{8,9},{9,8},{10,11... | collective-permute-start | bytes 1572872 | tf_op jit(solution)/shard_map/ppermute | solution.py:192
  72.6 41.7 %copy-start.3 = (f32[2,1024]{1,0:T(2,128)S(1)}, f32[2,1024]{1,0:T(2,128)}, u32[]{:S(2)}) copy-start(f32[2,1024]{1,0:T(2,128)} %rhs_ref.1) | copy-start | bytes 24580
  131.4 1.2 copy-start
  132.6 11.4 %copy-start.1 = (f32[256,1024]{1,0:T(8,128)S(1)}, f32[256,1024]{1,0:T(8,128)}, u32[]{:S(2)}) copy-start(f32[256,1024]{1,0:T(8,128)} %all-gather.2.cloned.1.call-done.total_ref) | copy-start | bytes 3145732
  145.4 18.5 %all-to-all-start.6 = ((f32[16,2,1280]{2,1,0:T(2,128)}), f32[16,2,1280]{2,1,0:T(2,128)S(1)}, u32[]{:S(2)}, u32[]{:S(2)}) async-start(f32[16,2,1280]{2,1,0:T(2,128)} %shard_map.52), calls=%async_computation.7 | async-start | bytes 327680 | tf_op jit(solution)/shard_map/all_to_all | solution.py:24
Sparse Core Ops, SparseCore 0:
  10.8 81.4 reduce-scatter.1
  94.5 29.0 all-gather.1

commit v10 on v9

--- a/solution.py
+++ b/solution.py
@@ -90,22 +90,34 @@
     return vmem_call(body, out, 2 * count * total.size, first, total)
 
 
-def partial_third(shares, total, pieces):
+def partial_third(shares, total, pieces, trow, blocks):
     count, part = shares.shape[1:]
     rows = total.shape[1]
-    own = count // pieces
-
-    def body(shares_ref, total_ref, out_ref):
+    own, near = count // pieces, part // blocks
+
+    def body(shares_ref, total_ref, trow_ref, out_ref):
         second = shares_ref[0]
         for n in range(1, shares.shape[0]):
             second += shares_ref[n]
         third = dot(second, total_ref[...], 1, 0)
+        block = second[:, :near]
+        for n in range(1, blocks):
+            block = jnp.where(trow_ref[0] == n, second[:, n * near : (n + 1) * near], block)
         for n in range(pieces):
             out_ref[n, :, :rows] = third[n * own : (n + 1) * own]
-            out_ref[n, :, rows:] = second[n * own : (n + 1) * own]
-
-    out = f32(pieces, own, rows + part)
-    return vmem_call(body, out, 2 * count * total.size, shares, total)
+            out_ref[n, :, rows:] = block[n * own : (n + 1) * own]
+
+    place = pl.BlockSpec(memory_space=pltpu.VMEM)
+    return pl.pallas_call(
+        body,
+        out_shape=f32(pieces, own, rows + near),
+        in_specs=[place, place, pl.BlockSpec(memory_space=pltpu.SMEM)],
+        out_specs=place,
+        cost_estimate=pl.CostEstimate(
+            flops=2 * count * total.size, bytes_accessed=4 * total.size, transcendentals=0
+        ),
+        compiler_params=pltpu.CompilerParams(vmem_limit_bytes=16 * 2**20),
+    )(shares, total, trow)
 
 
 def inner(u, v):
@@ -185,7 +197,8 @@
 
     part = lax.psum_scatter(tile.T, "mp", scatter_dimension=0, tiled=True)
 
-    over_mp = spread(transposed(guess, sizes), "mp", mp)
+    at, early = lax.optimization_barrier((lax.axis_index("trow").reshape(1), guess))
+    over_mp = spread(transposed(early, sizes), "mp", mp)
     over_mp = over_mp.transpose(1, 0, 2, 3).reshape(2 * mp * own, cols)
     block = spread(over_mp, "trow", trow).reshape(trow, 2, mp * own, cols)
     given = dot(block[:, 1].reshape(trow * mp * own, cols), tile, 1, 1)
@@ -200,9 +213,8 @@
 
     wide = exchange(copies, "mp").reshape(mp * own, rows)
     shares = exchange(partial_second(wide, total, trow), "trow")
-    pieces = exchange(partial_third(shares, total, mp), "mp")
-    second = pieces[:, :, rows:].reshape(mp, own, trow, core, share)
-    second = lax.dynamic_index_in_dim(second, lax.axis_index("trow"), 2, keepdims=False)
+    pieces = exchange(partial_third(shares, total, mp, at, trow), "mp")
+    second = pieces[:, :, rows:].reshape(mp, own, core, share)
     second = second.transpose(1, 2, 0, 3).reshape(own, rows)
     third, numbers = coordinates(first, second, pieces, trow)
     return combined(exchange(numbers, "trow"), guess, first, second, third)

time: 181 us -> 179 us (0.989)
  the two profiles are of different devices: /device:TPU:2 before, /device:TPU:8 now
where the time goes in v10:
time: 179 us; the launch traced here: 178 us
  blocking collectives  133 us (74%)
  between operations  14.2 us (8%)
  waiting for transfers between devices  9.9 us (6%)
  starting transfers between devices  7.89 us (4%)
  local copies, waits for them, and re-layouts  5.34 us (3%)
  matrix products  4.58 us (3%)
  Pallas kernels  3.05 us (2%)
    all_to_all x8, blocking collectives, exchange(): return lax.all_to_all(pieces, axes, 0, 0, tiled=True)  133 us
    ppermute x2, starting transfers between devices, transposed(): got.append(lax.ppermute(sent, PLANE, pairs))  5.89 us
    reduce_scatter x1, waiting for transfers between devices, shards(): part = lax.psum_scatter(tile.T, 'mp', scatter_dimension=0, tiled=True)  4.77 us
    unnamed x11, local copies, waits for them, and re-layouts  4.76 us
    dot_general x2, matrix products, dot(): lax.dot_general(lhs, rhs, (((lhs_dim,), (rhs_dim,)), ((), ())), precision...  4.58 us
  transfers between devices with their start and end apart: 5, of which 4 were waited for; matrix products, arithmetic and copies ran while one was open for 3% of the time, Pallas kernels for 0%

profile of v10, /device:TPU:8, one launch (start us, length us, event | category | flops | bytes accessed | tf_op | source)
XLA Modules:
  0.0 178.4 jit_solution(6779754450193381572)
XLA Ops:
  7.2 0.0 reduce-scatter.2.cloned.1.call-start
  7.2 2.9 %copy.10 = f32[1,1024,512]{1,2,0:T(8,128)} copy(f32[1,1024,512]{2,1,0:T(8,128)} %param.3) | data formatting | bytes 4194304 | tf_op args[0]
  10.2 0.0 all-gather.2.cloned.1.call-start
  10.2 0.6 copy-done.2
  10.8 3.3 %collective-permute-start = (f32[2,512]{1,0:T(2,128)S(1)}, f32[2,512]{1,0:T(2,128)S(1)}, u32[]{:S(2)}, u32[]{:S(2)}) collective-permute-start(f32[2,512]{1,0:T(2,128)S(1)} %get-tuple-element.18), channel_id=1, source_target_pairs={{0,0},{1,1},{2,8},{3,9},{4,16},{5,17},{6,24},{7,25},{8,2},{9,3},{1... | collective-permute-start | bytes 12296 | tf_op jit(solution)/shard_map/ppermute | solution.py:44
  14.1 2.6 %collective-permute-start.1 = (f32[2,512]{1,0:T(2,128)S(1)}, f32[2,512]{1,0:T(2,128)S(1)}, u32[]{:S(2)}, u32[]{:S(2)}) collective-permute-start(f32[2,512]{1,0:T(2,128)S(1)} %get-tuple-element.19), channel_id=1, source_target_pairs={{0,1},{1,0},{2,9},{3,8},{4,17},{5,16},{6,25},{7,24},{8,3},{9,2},{1... | collective-permute-start | bytes 12296 | tf_op jit(solution)/shard_map/ppermute | solution.py:44
  16.7 0.5 collective-permute-done
  17.2 2.7 %collective-permute-done.1 = f32[2,512]{1,0:T(2,128)S(1)} collective-permute-done((f32[2,512]{1,0:T(2,128)S(1)}, f32[2,512]{1,0:T(2,128)S(1)}, u32[]{:S(2)}, u32[]{:S(2)}) %collective-permute-start.1) | collective-permute-done | bytes 4128 | tf_op jit(solution)/shard_map/ppermute | solution.py:44
  20.0 30.5 %all_to_all.40 = f32[16,2,2,512]{3,2,1,0:T(2,128)S(1)} all-to-all(f32[16,2,2,512]{3,2,1,0:T(2,128)S(1)} %broadcast_in_dim.6), channel_id=1, replica_groups=mesh['mp'=16,'trow'=4,'y'=4,'core'=2] {'mp'}, dimensions={0} | all-to-all | bytes 262144 | tf_op jit(solution)/shard_map/all_to_all | solution.py:24
  50.5 0.1 broadcast_in_dim.14
  50.6 0.1 broadcast_in_dim.15
  50.7 16.5 %all_to_all.41 = f32[4,64,512]{2,1,0:T(8,128)S(1)} all-to-all(f32[4,64,512]{2,1,0:T(8,128)S(1)} %broadcast_in_dim.15), channel_id=1, replica_groups=mesh['mp'=16,'trow'=4,'y'=4,'core'=2] {'trow'}, dimensions={0} | all-to-all | bytes 1048576 | tf_op jit(solution)/shard_map/all_to_all | solution.py:24
  67.2 2.3 %fusion = f32[128,1024]{1,0:T(8,128)S(1)} fusion(f32[128,512]{1,0:T(8,128)S(1)} %bitcast.30, f32[1,1024,512]{2,1,0:T(8,128)S(1)} %copy-done.4), kind=kOutput, calls=%fused_computation | convolution fusion | flops 805306368 | bytes 2883584 | tf_op jit(solution)/shard_map/dot_general | solution.py:14
  69.5 1.9 %collective-permute-start.2 = (f32[128,1024]{1,0:T(8,128)S(1)}, f32[128,1024]{1,0:T(8,128)S(1)}, u32[]{:S(2)}, u32[]{:S(2)}) collective-permute-start(f32[128,1024]{1,0:T(8,128)S(1)} %fusion), channel_id=1, source_target_pairs={{0,1},{1,0},{2,3},{3,2},{4,5},{5,4},{6,7},{7,6},{8,9},{9,8},{10,11... | collective-permute-start | bytes 1572872 | tf_op jit(solution)/shard_map/ppermute | solution.py:205
  71.4 1.9 %collective-permute-done.2 = f32[128,1024]{1,0:T(8,128)S(1)} collective-permute-done((f32[128,1024]{1,0:T(8,128)S(1)}, f32[128,1024]{1,0:T(8,128)S(1)}, u32[]{:S(2)}, u32[]{:S(2)}) %collective-permute-start.2) | collective-permute-done | bytes 524320 | tf_op jit(solution)/shard_map/ppermute | solution.py:205
  73.3 2.3 %fusion.4 = f32[128,1024]{1,0:T(8,128)S(1)} fusion(f32[128,1024]{1,0:T(8,128)S(1)} %collective-permute-done.2, f32[128,512]{1,0:T(8,128)S(1)} %bitcast.29, f32[1,1024,512]{2,1,0:T(8,128)S(1)} %copy-done.4), kind=kOutput, calls=%fused_computation.4 | convolution fusion | flops 805437440 | bytes 3407872 | tf_op jit(solution)/shard_map/dot_general | solution.py:14
  75.6 11.7 %all_to_all.42 = f32[4,32,1024]{2,1,0:T(8,128)S(1)} all-to-all(f32[4,32,1024]{2,1,0:T(8,128)S(1)} %bitcast.28), channel_id=1, replica_groups=mesh['mp'=16,'trow'=4,'y'=4,'core'=2] {'y'}, dimensions={0} | all-to-all | bytes 1048576 | tf_op jit(solution)/shard_map/all_to_all | solution.py:24
  87.3 4.8 %reduce-scatter.2.cloned.1.call-done = f32[32,1024]{1,0:T(8,128)} async-done(((f32[512,1024]{1,0:T(8,128)}), f32[32,1024]{1,0:T(8,128)}) %reduce-scatter.2.cloned.1.call-update) | async-done | bytes 131088 | tf_op jit(solution)/shard_map/reduce_scatter | solution.py:198
  92.1 0.1 reshape.30
  92.2 22.6 %all_to_all.43.terms_ref = f32[16,2,1024]{2,1,0:T(2,128)S(1)} all-to-all(f32[16,2,1024]{2,1,0:T(2,128)S(1)} %reshape.30), channel_id=1, replica_groups=mesh['mp'=16,'trow'=4,'y'=4,'core'=2] {'mp'}, dimensions={0} | all-to-all | bytes 262144 | tf_op jit(solution)/shard_map/all_to_all | solution.py:24
  114.8 16.9 %all_to_all.44 = f32[16,2,1024]{2,1,0:T(2,128)S(1)} all-to-all(f32[16,2,1024]{2,1,0:T(2,128)S(1)} %get-tuple-element.11), channel_id=1, replica_groups=mesh['mp'=16,'trow'=4,'y'=4,'core'=2] {'mp'}, dimensions={0} | all-to-all | bytes 262144 | tf_op jit(solution)/shard_map/all_to_all | solution.py:24
  131.8 0.1 reshape.31.first_ref
  131.9 1.2 copy-done
  133.1 1.0 shard_map.51
  134.2 10.4 %all_to_all.45.shares_ref = f32[4,32,256]{2,1,0:T(8,128)S(1)} all-to-all(f32[4,32,256]{2,1,0:T(8,128)S(1)} %shard_map.51), channel_id=1, replica_groups=mesh['mp'=16,'trow'=4,'y'=4,'core'=2] {'trow'}, dimensions={0} | all-to-all | bytes 262144 | tf_op jit(solution)/shard_map/all_to_all | solution.py:24
  144.6 0.7 shard_map.52
  145.3 17.2 %all_to_all.46.pieces_ref = f32[16,2,1088]{2,1,0:T(2,128)S(1)} all-to-all(f32[16,2,1088]{2,1,0:T(2,128)S(1)} %shard_map.52), channel_id=1, replica_groups=mesh['mp'=16,'trow'=4,'y'=4,'core'=2] {'mp'}, dimensions={0} | all-to-all | bytes 278528 | tf_op jit(solution)/shard_map/all_to_all | solution.py:24
  162.5 0.1 reshape.32
  162.6 0.1 reshape.33.second_ref
  162.7 0.4 shard_map.53
  163.1 7.6 %all_to_all.47.known_ref = f32[4,2,128]{2,1,0:T(2,128)S(1)} all-to-all(f32[4,2,128]{2,1,0:T(2,128)S(1)} %get-tuple-element.14), channel_id=1, replica_groups=mesh['mp'=16,'trow'=4,'y'=4,'core'=2] {'trow'}, dimensions={0} | all-to-all | bytes 8192 | tf_op jit(solution)/shard_map/all_to_all | solution.py:24
  170.7 0.9 shard_map.54
  (20 shorter events, 0.2 us)
Async XLA Ops:
  7.2 84.9 %reduce-scatter.2.cloned.1.call-start = ((), (), s32[]{:S(2)}) async-start(), calls=%async_computation.9 | async-start | bytes 2228224 | tf_op jit(solution)/shard_map/reduce_scatter | solution.py:198
  10.1 0.7 copy-start.2
  10.2 57.0 %copy-start.4 = (f32[1,1024,512]{2,1,0:T(8,128)S(1)}, f32[1,1024,512]{2,1,0:T(8,128)}, u32[]{:S(2)}) copy-start(f32[1,1024,512]{2,1,0:T(8,128)} %param.3) | copy-start | bytes 6291460
  10.2 121.7 %all-gather.2.cloned.1.call-start = ((), (), s32[]{:S(2)}) async-start(), calls=%async_computation.10 | async-start | bytes 1179648 | tf_op jit(solution)/shard_map/all_gather | solution.py:212
  10.8 6.4 %collective-permute-start = (f32[2,512]{1,0:T(2,128)S(1)}, f32[2,512]{1,0:T(2,128)S(1)}, u32[]{:S(2)}, u32[]{:S(2)}) collective-permute-start(f32[2,512]{1,0:T(2,128)S(1)} %get-tuple-element.18), channel_id=1, source_target_pairs={{0,0},{1,1},{2,8},{3,9},{4,16},{5,17},{6,24},{7,25},{8,2},{9,3},{1... | collective-permute-start | bytes 12296 | tf_op jit(solution)/shard_map/ppermute | solution.py:44
  14.1 5.8 %collective-permute-start.1 = (f32[2,512]{1,0:T(2,128)S(1)}, f32[2,512]{1,0:T(2,128)S(1)}, u32[]{:S(2)}, u32[]{:S(2)}) collective-permute-start(f32[2,512]{1,0:T(2,128)S(1)} %get-tuple-element.19), channel_id=1, source_target_pairs={{0,1},{1,0},{2,9},{3,8},{4,17},{5,16},{6,25},{7,24},{8,3},{9,2},{1... | collective-permute-start | bytes 12296 | tf_op jit(solution)/shard_map/ppermute | solution.py:44
  69.5 3.8 %collective-permute-start.2 = (f32[128,1024]{1,0:T(8,128)S(1)}, f32[128,1024]{1,0:T(8,128)S(1)}, u32[]{:S(2)}, u32[]{:S(2)}) collective-permute-start(f32[128,1024]{1,0:T(8,128)S(1)} %fusion), channel_id=1, source_target_pairs={{0,1},{1,0},{2,3},{3,2},{4,5},{5,4},{6,7},{7,6},{8,9},{9,8},{10,11... | collective-permute-start | bytes 1572872 | tf_op jit(solution)/shard_map/ppermute | solution.py:205
  73.3 41.6 %copy-start.3 = (f32[2,1024]{1,0:T(2,128)S(1)}, f32[2,1024]{1,0:T(2,128)}, u32[]{:S(2)}) copy-start(f32[2,1024]{1,0:T(2,128)} %rhs_ref.1) | copy-start | bytes 24580
  131.9 1.2 copy-start
  133.1 11.5 %copy-start.1 = (f32[256,1024]{1,0:T(8,128)S(1)}, f32[256,1024]{1,0:T(8,128)}, u32[]{:S(2)}) copy-start(f32[256,1024]{1,0:T(8,128)} %all-gather.2.cloned.1.call-done.total_ref) | copy-start | bytes 3145732
Sparse Core Ops, SparseCore 0:
  10.8 81.2 reduce-scatter.1
  94.2 27.8 all-gather.1

commit v11 on v10

--- a/solution.py
+++ b/solution.py
@@ -75,7 +75,7 @@
         for n in range(count):
             out_ref[n] = first
 
-    return vmem_call(body, (f32(*rhs.shape), f32(*terms.shape)), terms.size, terms, rhs)
+    return vmem_call(body, (f32(*rhs.shape), f32(*terms.shape)), 10**10, terms, rhs)
 
 
 def partial_second(first, total, copies):

time: 179 us -> 181 us (1.011)
  the two profiles are of different devices: /device:TPU:8 before, /device:TPU:32 now
where the time goes in v11:
time: 181 us
  blocking collectives  126 us (70%)
  waiting for transfers between devices  16.9 us (9%)
  between operations  14.2 us (8%)
  starting transfers between devices  10.3 us (6%)
  local copies, waits for them, and re-layouts  6.04 us (3%)
  matrix products  4.59 us (3%)
  Pallas kernels  3.05 us (2%)
    all_to_all x7, blocking collectives, exchange(): return lax.all_to_all(pieces, axes, 0, 0, tiled=True)  126 us
    all_to_all x1, waiting for transfers between devices, exchange(): return lax.all_to_all(pieces, axes, 0, 0, tiled=True)  12.8 us
    all_to_all x1, starting transfers between devices, exchange(): return lax.all_to_all(pieces, axes, 0, 0, tiled=True)  5.72 us
    unnamed x11, local copies, waits for them, and re-layouts  4.8 us
    dot_general x2, matrix products, dot(): lax.dot_general(lhs, rhs, (((lhs_dim,), (rhs_dim,)), ((), ())), precision...  4.59 us
  transfers between devices with their start and end apart: 6, of which 4 were waited for; matrix products, arithmetic and copies ran while one was open for 3% of the time, Pallas kernels for 0%

profile of v11, /device:TPU:32, one launch (start us, length us, event | category | flops | bytes accessed | tf_op | source)
XLA Modules:
  0.0 180.8 jit_solution(3822346474197834384)
XLA Ops:
  7.2 0.0 reduce-scatter.2.cloned.1.call-start
  7.2 2.9 %copy.10 = f32[1,1024,512]{1,2,0:T(8,128)} copy(f32[1,1024,512]{2,1,0:T(8,128)} %param.3) | data formatting | bytes 4194304 | tf_op args[0]
  10.2 0.7 copy-done.2
  10.8 0.6 collective-permute-start
  11.5 1.9 %collective-permute-start.1 = (f32[2,512]{1,0:T(2,128)S(1)}, f32[2,512]{1,0:T(2,128)S(1)}, u32[]{:S(2)}, u32[]{:S(2)}) collective-permute-start(f32[2,512]{1,0:T(2,128)S(1)} %get-tuple-element.19), channel_id=1, source_target_pairs={{0,1},{1,0},{2,9},{3,8},{4,17},{5,16},{6,25},{7,24},{8,3},{9,2},{1... | collective-permute-start | bytes 12296 | tf_op jit(solution)/shard_map/ppermute | solution.py:44
  13.4 1.1 collective-permute-done.1
  14.6 29.6 %all_to_all.40 = f32[16,2,2,512]{3,2,1,0:T(2,128)S(1)} all-to-all(f32[16,2,2,512]{3,2,1,0:T(2,128)S(1)} %broadcast_in_dim.6), channel_id=1, replica_groups=mesh['mp'=16,'trow'=4,'y'=4,'core'=2] {'mp'}, dimensions={0} | all-to-all | bytes 262144 | tf_op jit(solution)/shard_map/all_to_all | solution.py:24
  44.2 0.1 broadcast_in_dim.14
  44.3 0.1 broadcast_in_dim.15
  44.3 23.0 %all_to_all.41 = f32[4,64,512]{2,1,0:T(8,128)S(1)} all-to-all(f32[4,64,512]{2,1,0:T(8,128)S(1)} %broadcast_in_dim.15), channel_id=1, replica_groups=mesh['mp'=16,'trow'=4,'y'=4,'core'=2] {'trow'}, dimensions={0} | all-to-all | bytes 1048576 | tf_op jit(solution)/shard_map/all_to_all | solution.py:24
  67.4 2.3 %fusion = f32[128,1024]{1,0:T(8,128)S(1)} fusion(f32[128,512]{1,0:T(8,128)S(1)} %bitcast.30, f32[1,1024,512]{2,1,0:T(8,128)S(1)} %copy-done.4), kind=kOutput, calls=%fused_computation | convolution fusion | flops 805306368 | bytes 2883584 | tf_op jit(solution)/shard_map/dot_general | solution.py:14
  69.7 1.9 %collective-permute-start.2 = (f32[128,1024]{1,0:T(8,128)S(1)}, f32[128,1024]{1,0:T(8,128)S(1)}, u32[]{:S(2)}, u32[]{:S(2)}) collective-permute-start(f32[128,1024]{1,0:T(8,128)S(1)} %fusion), channel_id=1, source_target_pairs={{0,1},{1,0},{2,3},{3,2},{4,5},{5,4},{6,7},{7,6},{8,9},{9,8},{10,11... | collective-permute-start | bytes 1572872 | tf_op jit(solution)/shard_map/ppermute | solution.py:205
  71.6 1.9 %collective-permute-done.2 = f32[128,1024]{1,0:T(8,128)S(1)} collective-permute-done((f32[128,1024]{1,0:T(8,128)S(1)}, f32[128,1024]{1,0:T(8,128)S(1)}, u32[]{:S(2)}, u32[]{:S(2)}) %collective-permute-start.2) | collective-permute-done | bytes 524320 | tf_op jit(solution)/shard_map/ppermute | solution.py:205
  73.5 2.3 %fusion.4 = f32[128,1024]{1,0:T(8,128)S(1)} fusion(f32[128,1024]{1,0:T(8,128)S(1)} %collective-permute-done.2, f32[128,512]{1,0:T(8,128)S(1)} %bitcast.29, f32[1,1024,512]{2,1,0:T(8,128)S(1)} %copy-done.4), kind=kOutput, calls=%fused_computation.4 | convolution fusion | flops 805437440 | bytes 3407872 | tf_op jit(solution)/shard_map/dot_general | solution.py:14
  75.8 12.5 %all_to_all.42 = f32[4,32,1024]{2,1,0:T(8,128)S(1)} all-to-all(f32[4,32,1024]{2,1,0:T(8,128)S(1)} %bitcast.28), channel_id=1, replica_groups=mesh['mp'=16,'trow'=4,'y'=4,'core'=2] {'y'}, dimensions={0} | all-to-all | bytes 1048576 | tf_op jit(solution)/shard_map/all_to_all | solution.py:24
  88.3 0.7 reshape.30
  89.0 5.7 %all-to-all-start.3 = ((f32[16,2,1024]{2,1,0:T(2,128)}), f32[16,2,1024]{2,1,0:T(2,128)S(1)}, u32[]{:S(2)}, u32[]{:S(2)}) async-start(f32[16,2,1024]{2,1,0:T(2,128)} %reshape.30), calls=%async_computation.3 | async-start | bytes 262144 | tf_op jit(solution)/shard_map/all_to_all | solution.py:24
  94.8 0.7 all-gather.2.cloned.1.call-update
  95.5 12.8 %all-to-all-done.3.terms_ref = f32[16,2,1024]{2,1,0:T(2,128)S(1)} async-done(((f32[16,2,1024]{2,1,0:T(2,128)}), f32[16,2,1024]{2,1,0:T(2,128)S(1)}, u32[]{:S(2)}, u32[]{:S(2)}) %all-to-all-start.3) | async-done | bytes 131104 | tf_op jit(solution)/shard_map/all_to_all | solution.py:24
  108.3 17.0 %all_to_all.43 = f32[16,2,1024]{2,1,0:T(2,128)S(1)} all-to-all(f32[16,2,1024]{2,1,0:T(2,128)S(1)} %get-tuple-element.11), channel_id=1, replica_groups=mesh['mp'=16,'trow'=4,'y'=4,'core'=2] {'mp'}, dimensions={0} | all-to-all | bytes 262144 | tf_op jit(solution)/shard_map/all_to_all | solution.py:24
  125.4 0.1 reshape.31.first_ref
  125.4 0.4 all-gather.2.cloned.1.call-done.total_ref
  125.9 1.2 copy-done
  127.1 1.0 shard_map.51
  128.1 10.0 %all_to_all.44.shares_ref = f32[4,32,256]{2,1,0:T(8,128)S(1)} all-to-all(f32[4,32,256]{2,1,0:T(8,128)S(1)} %shard_map.51), channel_id=1, replica_groups=mesh['mp'=16,'trow'=4,'y'=4,'core'=2] {'trow'}, dimensions={0} | all-to-all | bytes 262144 | tf_op jit(solution)/shard_map/all_to_all | solution.py:24
  138.2 0.7 shard_map.52
  138.9 26.0 %all_to_all.45.pieces_ref = f32[16,2,1088]{2,1,0:T(2,128)S(1)} all-to-all(f32[16,2,1088]{2,1,0:T(2,128)S(1)} %shard_map.52), channel_id=1, replica_groups=mesh['mp'=16,'trow'=4,'y'=4,'core'=2] {'mp'}, dimensions={0} | all-to-all | bytes 278528 | tf_op jit(solution)/shard_map/all_to_all | solution.py:24
  164.8 0.1 reshape.32
  165.0 0.1 reshape.33.second_ref
  165.1 0.4 shard_map.53
  165.4 7.6 %all_to_all.46.known_ref = f32[4,2,128]{2,1,0:T(2,128)S(1)} all-to-all(f32[4,2,128]{2,1,0:T(2,128)S(1)} %get-tuple-element.14), channel_id=1, replica_groups=mesh['mp'=16,'trow'=4,'y'=4,'core'=2] {'trow'}, dimensions={0} | all-to-all | bytes 8192 | tf_op jit(solution)/shard_map/all_to_all | solution.py:24
  173.1 0.9 shard_map.54
  (21 shorter events, 0.3 us)
Async XLA Ops:
  7.2 87.7 %reduce-scatter.2.cloned.1.call-start = ((), (), s32[]{:S(2)}) async-start(), calls=%async_computation.9 | async-start | bytes 2228224 | tf_op jit(solution)/shard_map/reduce_scatter | solution.py:198
  10.1 0.7 copy-start.2
  10.1 57.2 %copy-start.4 = (f32[1,1024,512]{2,1,0:T(8,128)S(1)}, f32[1,1024,512]{2,1,0:T(8,128)}, u32[]{:S(2)}) copy-start(f32[1,1024,512]{2,1,0:T(8,128)} %param.3) | copy-start | bytes 6291460
  10.8 2.6 %collective-permute-start = (f32[2,512]{1,0:T(2,128)S(1)}, f32[2,512]{1,0:T(2,128)S(1)}, u32[]{:S(2)}, u32[]{:S(2)}) collective-permute-start(f32[2,512]{1,0:T(2,128)S(1)} %get-tuple-element.18), channel_id=1, source_target_pairs={{0,0},{1,1},{2,8},{3,9},{4,16},{5,17},{6,24},{7,25},{8,2},{9,3},{1... | collective-permute-start | bytes 12296 | tf_op jit(solution)/shard_map/ppermute | solution.py:44
  11.5 3.1 %collective-permute-start.1 = (f32[2,512]{1,0:T(2,128)S(1)}, f32[2,512]{1,0:T(2,128)S(1)}, u32[]{:S(2)}, u32[]{:S(2)}) collective-permute-start(f32[2,512]{1,0:T(2,128)S(1)} %get-tuple-element.19), channel_id=1, source_target_pairs={{0,1},{1,0},{2,9},{3,8},{4,17},{5,16},{6,25},{7,24},{8,3},{9,2},{1... | collective-permute-start | bytes 12296 | tf_op jit(solution)/shard_map/ppermute | solution.py:44
  69.7 3.8 %collective-permute-start.2 = (f32[128,1024]{1,0:T(8,128)S(1)}, f32[128,1024]{1,0:T(8,128)S(1)}, u32[]{:S(2)}, u32[]{:S(2)}) collective-permute-start(f32[128,1024]{1,0:T(8,128)S(1)} %fusion), channel_id=1, source_target_pairs={{0,1},{1,0},{2,3},{3,2},{4,5},{5,4},{6,7},{7,6},{8,9},{9,8},{10,11... | collective-permute-start | bytes 1572872 | tf_op jit(solution)/shard_map/ppermute | solution.py:205
  73.5 34.8 %copy-start.3 = (f32[2,1024]{1,0:T(2,128)S(1)}, f32[2,1024]{1,0:T(2,128)}, u32[]{:S(2)}) copy-start(f32[2,1024]{1,0:T(2,128)} %rhs_ref.1) | copy-start | bytes 24580
  89.0 19.2 %all-to-all-start.3 = ((f32[16,2,1024]{2,1,0:T(2,128)}), f32[16,2,1024]{2,1,0:T(2,128)S(1)}, u32[]{:S(2)}, u32[]{:S(2)}) async-start(f32[16,2,1024]{2,1,0:T(2,128)} %reshape.30), calls=%async_computation.3 | async-start | bytes 262144 | tf_op jit(solution)/shard_map/all_to_all | solution.py:24
  94.8 31.1 %all-gather.2.cloned.1.call-start = ((), (), s32[]{:S(2)}) async-start(), calls=%async_computation.10 | async-start | bytes 1179648 | tf_op jit(solution)/shard_map/all_gather | solution.py:212
  125.9 1.2 copy-start
  127.1 11.1 %copy-start.1 = (f32[256,1024]{1,0:T(8,128)S(1)}, f32[256,1024]{1,0:T(8,128)}, u32[]{:S(2)}) copy-start(f32[256,1024]{1,0:T(8,128)} %all-gather.2.cloned.1.call-done.total_ref) | copy-start | bytes 3145732
Sparse Core Ops, SparseCore 0:
  10.8 80.1 reduce-scatter.1
  97.7 28.0 all-gather.1

commit v12 on v10

--- a/solution.py
+++ b/solution.py
@@ -79,15 +79,36 @@
 
 
 def partial_second(first, total, copies):
-    count, part = first.shape[0], total.shape[0]
-
-    def body(first_ref, total_ref, out_ref):
-        second = dot(first_ref[...], total_ref[...], 1, 1)
+    count, (part, rows) = first.shape[0], total.shape
+    steps = 4 if rows % 512 == 0 else 1
+    chunk = rows // steps
+
+    def body(first_ref, total_ref, out_ref, held, done):
+        moves = [
+            pltpu.make_async_copy(total_ref.at[:, pl.ds(n * chunk, chunk)], held.at[n], done.at[n])
+            for n in range(steps)
+        ]
+        for move in moves:
+            move.start()
+        second = jnp.zeros((count, part), jnp.float32)
+        for n, move in enumerate(moves):
+            move.wait()
+            second += dot(first_ref[:, n * chunk : (n + 1) * chunk], held[n], 1, 1)
         for n in range(copies):
             out_ref[n] = second
 
-    out = f32(copies, count, part)
-    return vmem_call(body, out, 2 * count * total.size, first, total)
+    place = pl.BlockSpec(memory_space=pltpu.VMEM)
+    return pl.pallas_call(
+        body,
+        out_shape=f32(copies, count, part),
+        in_specs=[place, pl.BlockSpec(memory_space=pl.ANY)],
+        out_specs=place,
+        scratch_shapes=[pltpu.VMEM((steps, part, chunk), jnp.float32), pltpu.SemaphoreType.DMA((steps,))],
+        cost_estimate=pl.CostEstimate(
+            flops=2 * count * total.size, bytes_accessed=4*total.size, transcendentals=0
+        ),
+        compiler_params=pltpu.CompilerParams(vmem_limit_bytes=60 * 2**20),
+    )(first, total)
 
 
 def partial_third(shares, total, pieces, trow, blocks):

time: 179 us -> 182 us (1.017)
  Pallas kernels: 3.05 us -> 6.6 us
    pallas_call x0 -> x1, Pallas kernels: none -> 4.59 us  [partial_second(): pl.pallas_call(body, out_shape=f32(copies, count, part), in_specs=[place,...]
    unnamed x11 -> x9, local copies, waits for them, and re-layouts: 4.76 us -> 3.53 us
where the time goes in v12:
time: 182 us
  blocking collectives  134 us (74%)
  between operations  14.2 us (8%)
  waiting for transfers between devices  9.66 us (5%)
  starting transfers between devices  7.89 us (4%)
  Pallas kernels  6.6 us (4%)
  local copies, waits for them, and re-layouts  4.75 us (3%)
  matrix products  4.58 us (3%)
    all_to_all x8, blocking collectives, exchange(): return lax.all_to_all(pieces, axes, 0, 0, tiled=True)  134 us
    ppermute x2, starting transfers between devices, transposed(): got.append(lax.ppermute(sent, PLANE, pairs))  5.89 us
    pallas_call x1, Pallas kernels, partial_second(): pl.pallas_call(body, out_shape=f32(copies, count, part), in_specs=[place,...  4.59 us
    dot_general x2, matrix products, dot(): lax.dot_general(lhs, rhs, (((lhs_dim,), (rhs_dim,)), ((), ())), precision...  4.58 us
    reduce_scatter x1, waiting for transfers between devices, shards(): part = lax.psum_scatter(tile.T, 'mp', scatter_dimension=0, tiled=True)  4.54 us
  transfers between devices with their start and end apart: 5, of which 4 were waited for; matrix products, arithmetic and copies ran while one was open for 3% of the time, Pallas kernels for 0%

profile of v12, /device:TPU:8, one launch (start us, length us, event | category | flops | bytes accessed | tf_op | source)
XLA Modules:
  0.0 181.6 jit_solution(5093118053323257964)
XLA Ops:
  7.2 0.0 reduce-scatter.2.cloned.1.call-start
  7.2 2.9 %copy.10 = f32[1,1024,512]{1,2,0:T(8,128)} copy(f32[1,1024,512]{2,1,0:T(8,128)} %param.3) | data formatting | bytes 4194304 | tf_op args[0]
  10.1 0.0 reduce-scatter.2.cloned.1.call-update
  10.2 0.0 all-gather.2.cloned.1.call-start
  10.2 0.6 copy-done.1
  10.8 3.3 %collective-permute-start = (f32[2,512]{1,0:T(2,128)S(1)}, f32[2,512]{1,0:T(2,128)S(1)}, u32[]{:S(2)}, u32[]{:S(2)}) collective-permute-start(f32[2,512]{1,0:T(2,128)S(1)} %get-tuple-element.18), channel_id=1, source_target_pairs={{0,0},{1,1},{2,8},{3,9},{4,16},{5,17},{6,24},{7,25},{8,2},{9,3},{1... | collective-permute-start | bytes 12296 | tf_op jit(solution)/shard_map/ppermute | solution.py:44
  14.1 2.6 %collective-permute-start.1 = (f32[2,512]{1,0:T(2,128)S(1)}, f32[2,512]{1,0:T(2,128)S(1)}, u32[]{:S(2)}, u32[]{:S(2)}) collective-permute-start(f32[2,512]{1,0:T(2,128)S(1)} %get-tuple-element.19), channel_id=1, source_target_pairs={{0,1},{1,0},{2,9},{3,8},{4,17},{5,16},{6,25},{7,24},{8,3},{9,2},{1... | collective-permute-start | bytes 12296 | tf_op jit(solution)/shard_map/ppermute | solution.py:44
  16.7 0.5 collective-permute-done
  17.2 2.7 %collective-permute-done.1 = f32[2,512]{1,0:T(2,128)S(1)} collective-permute-done((f32[2,512]{1,0:T(2,128)S(1)}, f32[2,512]{1,0:T(2,128)S(1)}, u32[]{:S(2)}, u32[]{:S(2)}) %collective-permute-start.1) | collective-permute-done | bytes 4128 | tf_op jit(solution)/shard_map/ppermute | solution.py:44
  20.0 30.5 %all_to_all.40 = f32[16,2,2,512]{3,2,1,0:T(2,128)S(1)} all-to-all(f32[16,2,2,512]{3,2,1,0:T(2,128)S(1)} %broadcast_in_dim.6), channel_id=1, replica_groups=mesh['mp'=16,'trow'=4,'y'=4,'core'=2] {'mp'}, dimensions={0} | all-to-all | bytes 262144 | tf_op jit(solution)/shard_map/all_to_all | solution.py:24
  50.5 0.1 broadcast_in_dim.14
  50.6 0.1 broadcast_in_dim.15
  50.6 16.5 %all_to_all.41 = f32[4,64,512]{2,1,0:T(8,128)S(1)} all-to-all(f32[4,64,512]{2,1,0:T(8,128)S(1)} %broadcast_in_dim.15), channel_id=1, replica_groups=mesh['mp'=16,'trow'=4,'y'=4,'core'=2] {'trow'}, dimensions={0} | all-to-all | bytes 1048576 | tf_op jit(solution)/shard_map/all_to_all | solution.py:24
  67.1 2.3 %fusion = f32[128,1024]{1,0:T(8,128)S(1)} fusion(f32[128,512]{1,0:T(8,128)S(1)} %bitcast.30, f32[1,1024,512]{2,1,0:T(8,128)S(1)} %copy-done.3), kind=kOutput, calls=%fused_computation | convolution fusion | flops 805306368 | bytes 2883584 | tf_op jit(solution)/shard_map/dot_general | solution.py:14
  69.4 1.9 %collective-permute-start.2 = (f32[128,1024]{1,0:T(8,128)S(1)}, f32[128,1024]{1,0:T(8,128)S(1)}, u32[]{:S(2)}, u32[]{:S(2)}) collective-permute-start(f32[128,1024]{1,0:T(8,128)S(1)} %fusion), channel_id=1, source_target_pairs={{0,1},{1,0},{2,3},{3,2},{4,5},{5,4},{6,7},{7,6},{8,9},{9,8},{10,11... | collective-permute-start | bytes 1572872 | tf_op jit(solution)/shard_map/ppermute | solution.py:226
  71.4 1.9 %collective-permute-done.2 = f32[128,1024]{1,0:T(8,128)S(1)} collective-permute-done((f32[128,1024]{1,0:T(8,128)S(1)}, f32[128,1024]{1,0:T(8,128)S(1)}, u32[]{:S(2)}, u32[]{:S(2)}) %collective-permute-start.2) | collective-permute-done | bytes 524320 | tf_op jit(solution)/shard_map/ppermute | solution.py:226
  73.2 2.3 %fusion.4 = f32[128,1024]{1,0:T(8,128)S(1)} fusion(f32[128,1024]{1,0:T(8,128)S(1)} %collective-permute-done.2, f32[128,512]{1,0:T(8,128)S(1)} %bitcast.29, f32[1,1024,512]{2,1,0:T(8,128)S(1)} %copy-done.3), kind=kOutput, calls=%fused_computation.4 | convolution fusion | flops 805437440 | bytes 3407872 | tf_op jit(solution)/shard_map/dot_general | solution.py:14
  75.5 11.8 %all_to_all.42 = f32[4,32,1024]{2,1,0:T(8,128)S(1)} all-to-all(f32[4,32,1024]{2,1,0:T(8,128)S(1)} %bitcast.28), channel_id=1, replica_groups=mesh['mp'=16,'trow'=4,'y'=4,'core'=2] {'y'}, dimensions={0} | all-to-all | bytes 1048576 | tf_op jit(solution)/shard_map/all_to_all | solution.py:24
  87.3 4.5 %reduce-scatter.2.cloned.1.call-done = f32[32,1024]{1,0:T(8,128)} async-done(((f32[512,1024]{1,0:T(8,128)}), f32[32,1024]{1,0:T(8,128)}) %reduce-scatter.2.cloned.1.call-update) | async-done | bytes 131088 | tf_op jit(solution)/shard_map/reduce_scatter | solution.py:219
  91.9 0.1 reshape.30
  92.0 22.9 %all_to_all.43.terms_ref = f32[16,2,1024]{2,1,0:T(2,128)S(1)} all-to-all(f32[16,2,1024]{2,1,0:T(2,128)S(1)} %reshape.30), channel_id=1, replica_groups=mesh['mp'=16,'trow'=4,'y'=4,'core'=2] {'mp'}, dimensions={0} | all-to-all | bytes 262144 | tf_op jit(solution)/shard_map/all_to_all | solution.py:24
  114.9 17.0 %all_to_all.44 = f32[16,2,1024]{2,1,0:T(2,128)S(1)} all-to-all(f32[16,2,1024]{2,1,0:T(2,128)S(1)} %get-tuple-element.11), channel_id=1, replica_groups=mesh['mp'=16,'trow'=4,'y'=4,'core'=2] {'mp'}, dimensions={0} | all-to-all | bytes 262144 | tf_op jit(solution)/shard_map/all_to_all | solution.py:24
  131.9 0.7 reshape.31.first_ref
  132.6 4.6 %shard_map.51 = f32[4,32,256]{2,1,0:T(8,128)} custom-call(f32[32,1024]{1,0:T(8,128)} %reshape.31.first_ref, f32[256,1024]{1,0:T(8,128)} %all-gather.2.cloned.1.call-done.total_ref), custom_call_target="tpu_custom_call" | custom-call | flops 16777216 | bytes 1048576 | tf_op jit(solution)/shard_map/pallas_call | solution.py:101
  137.2 10.6 %all_to_all.45.shares_ref = f32[4,32,256]{2,1,0:T(8,128)S(1)} all-to-all(f32[4,32,256]{2,1,0:T(8,128)} %shard_map.51), channel_id=1, replica_groups=mesh['mp'=16,'trow'=4,'y'=4,'core'=2] {'trow'}, dimensions={0} | all-to-all | bytes 262144 | tf_op jit(solution)/shard_map/all_to_all | solution.py:24
  147.8 0.7 shard_map.52
  148.5 17.1 %all_to_all.46.pieces_ref = f32[16,2,1088]{2,1,0:T(2,128)S(1)} all-to-all(f32[16,2,1088]{2,1,0:T(2,128)S(1)} %shard_map.52), channel_id=1, replica_groups=mesh['mp'=16,'trow'=4,'y'=4,'core'=2] {'mp'}, dimensions={0} | all-to-all | bytes 278528 | tf_op jit(solution)/shard_map/all_to_all | solution.py:24
  165.6 0.1 reshape.32
  165.7 0.1 reshape.33.second_ref
  165.8 0.4 shard_map.53
  166.2 7.6 %all_to_all.47.known_ref = f32[4,2,128]{2,1,0:T(2,128)S(1)} all-to-all(f32[4,2,128]{2,1,0:T(2,128)S(1)} %get-tuple-element.14), channel_id=1, replica_groups=mesh['mp'=16,'trow'=4,'y'=4,'core'=2] {'trow'}, dimensions={0} | all-to-all | bytes 8192 | tf_op jit(solution)/shard_map/all_to_all | solution.py:24
  173.8 0.9 shard_map.54
  (18 shorter events, 0.2 us)
Async XLA Ops:
  7.2 84.7 %reduce-scatter.2.cloned.1.call-start = ((), (), s32[]{:S(2)}) async-start(), calls=%async_computation.9 | async-start | bytes 2228224 | tf_op jit(solution)/shard_map/reduce_scatter | solution.py:219
  10.1 0.7 copy-start.1
  10.2 57.0 %copy-start.3 = (f32[1,1024,512]{2,1,0:T(8,128)S(1)}, f32[1,1024,512]{2,1,0:T(8,128)}, u32[]{:S(2)}) copy-start(f32[1,1024,512]{2,1,0:T(8,128)} %param.3) | copy-start | bytes 6291460
  10.2 122.5 %all-gather.2.cloned.1.call-start = ((), (), s32[]{:S(2)}) async-start(), calls=%async_computation.10 | async-start | bytes 1179648 | tf_op jit(solution)/shard_map/all_gather | solution.py:233
  10.8 6.4 %collective-permute-start = (f32[2,512]{1,0:T(2,128)S(1)}, f32[2,512]{1,0:T(2,128)S(1)}, u32[]{:S(2)}, u32[]{:S(2)}) collective-permute-start(f32[2,512]{1,0:T(2,128)S(1)} %get-tuple-element.18), channel_id=1, source_target_pairs={{0,0},{1,1},{2,8},{3,9},{4,16},{5,17},{6,24},{7,25},{8,2},{9,3},{1... | collective-permute-start | bytes 12296 | tf_op jit(solution)/shard_map/ppermute | solution.py:44
  14.1 5.8 %collective-permute-start.1 = (f32[2,512]{1,0:T(2,128)S(1)}, f32[2,512]{1,0:T(2,128)S(1)}, u32[]{:S(2)}, u32[]{:S(2)}) collective-permute-start(f32[2,512]{1,0:T(2,128)S(1)} %get-tuple-element.19), channel_id=1, source_target_pairs={{0,1},{1,0},{2,9},{3,8},{4,17},{5,16},{6,25},{7,24},{8,3},{9,2},{1... | collective-permute-start | bytes 12296 | tf_op jit(solution)/shard_map/ppermute | solution.py:44
  69.4 3.8 %collective-permute-start.2 = (f32[128,1024]{1,0:T(8,128)S(1)}, f32[128,1024]{1,0:T(8,128)S(1)}, u32[]{:S(2)}, u32[]{:S(2)}) collective-permute-start(f32[128,1024]{1,0:T(8,128)S(1)} %fusion), channel_id=1, source_target_pairs={{0,1},{1,0},{2,3},{3,2},{4,5},{5,4},{6,7},{7,6},{8,9},{9,8},{10,11... | collective-permute-start | bytes 1572872 | tf_op jit(solution)/shard_map/ppermute | solution.py:226
  73.2 41.7 %copy-start.2 = (f32[2,1024]{1,0:T(2,128)S(1)}, f32[2,1024]{1,0:T(2,128)}, u32[]{:S(2)}) copy-start(f32[2,1024]{1,0:T(2,128)} %rhs_ref.1) | copy-start | bytes 24580
  132.6 15.2 %copy-start = (f32[256,1024]{1,0:T(8,128)S(1)}, f32[256,1024]{1,0:T(8,128)}, u32[]{:S(2)}) copy-start(f32[256,1024]{1,0:T(8,128)} %all-gather.2.cloned.1.call-done.total_ref) | copy-start | bytes 3145732
Sparse Core Ops, SparseCore 0:
  10.8 81.0 reduce-scatter.1
  94.0 28.0 all-gather.1

commit v13 on v10

--- a/solution.py
+++ b/solution.py
@@ -200,7 +200,7 @@
     at, early = lax.optimization_barrier((lax.axis_index("trow").reshape(1), guess))
     over_mp = spread(transposed(early, sizes), "mp", mp)
     over_mp = over_mp.transpose(1, 0, 2, 3).reshape(2 * mp * own, cols)
-    block = spread(over_mp, "trow", trow).reshape(trow, 2, mp * own, cols)
+    block = lax.all_gather(over_mp, "trow", axis=0).reshape(trow, 2, mp * own, cols)
     given = dot(block[:, 1].reshape(trow * mp * own, cols), tile, 1, 1)
     given = lax.ppermute(given, "core", [(0, 1), (1, 0)])
     terms = dot(block[:, 0].reshape(trow * mp * own, cols), tile, 1, 1) + given

time: 179 us -> 179 us (level)
  blocking collectives: 133 us -> 135 us
  waiting for transfers between devices: 9.9 us -> 8.06 us
    all_gather x0 -> x1, blocking collectives: none -> 17.5 us  [shards(): lax.all_gather(over_mp, 'trow', axis=0).reshape(trow, 2, mp * own, cols)]
    all_to_all x8 -> x7, blocking collectives: 133 us -> 118 us  [exchange(): return lax.all_to_all(pieces, axes, 0, 0, tiled=True)]
    reduce_scatter x1, waiting for transfers between devices: 4.77 us -> 2.93 us  [shards(): part = lax.psum_scatter(tile.T, 'mp', scatter_dimension=0, tiled=True)]
where the time goes in v13:
time: 179 us; the launch traced here: 178 us
  blocking collectives  135 us (75%)
  between operations  14.2 us (8%)
  waiting for transfers between devices  8.06 us (5%)
  starting transfers between devices  7.89 us (4%)
  local copies, waits for them, and re-layouts  5.29 us (3%)
  matrix products  4.59 us (3%)
  Pallas kernels  3.05 us (2%)
    all_to_all x7, blocking collectives, exchange(): return lax.all_to_all(pieces, axes, 0, 0, tiled=True)  118 us
    all_gather x1, blocking collectives, shards(): lax.all_gather(over_mp, 'trow', axis=0).reshape(trow, 2, mp * own, cols)  17.5 us
    ppermute x2, starting transfers between devices, transposed(): got.append(lax.ppermute(sent, PLANE, pairs))  5.89 us
    unnamed x11, local copies, waits for them, and re-layouts  4.76 us
    dot_general x2, matrix products, dot(): lax.dot_general(lhs, rhs, (((lhs_dim,), (rhs_dim,)), ((), ())), precision...  4.59 us
  transfers between devices with their start and end apart: 5, of which 4 were waited for; matrix products, arithmetic and copies ran while one was open for 3% of the time, Pallas kernels for 0%

profile of v13, /device:TPU:8, one launch (start us, length us, event | category | flops | bytes accessed | tf_op | source)
XLA Modules:
  0.0 178.4 jit_solution(1922793380537012620)
XLA Ops:
  7.2 0.0 reduce-scatter.2.cloned.1.call-start
  7.2 2.9 %copy.10 = f32[1,1024,512]{1,2,0:T(8,128)} copy(f32[1,1024,512]{2,1,0:T(8,128)} %param.3) | data formatting | bytes 4194304 | tf_op args[0]
  10.2 0.0 all-gather.2.cloned.1.call-start
  10.2 0.6 copy-done.2
  10.8 3.3 %collective-permute-start = (f32[2,512]{1,0:T(2,128)S(1)}, f32[2,512]{1,0:T(2,128)S(1)}, u32[]{:S(2)}, u32[]{:S(2)}) collective-permute-start(f32[2,512]{1,0:T(2,128)S(1)} %get-tuple-element.18), channel_id=1, source_target_pairs={{0,0},{1,1},{2,8},{3,9},{4,16},{5,17},{6,24},{7,25},{8,2},{9,3},{1... | collective-permute-start | bytes 12296 | tf_op jit(solution)/shard_map/ppermute | solution.py:44
  14.1 2.6 %collective-permute-start.1 = (f32[2,512]{1,0:T(2,128)S(1)}, f32[2,512]{1,0:T(2,128)S(1)}, u32[]{:S(2)}, u32[]{:S(2)}) collective-permute-start(f32[2,512]{1,0:T(2,128)S(1)} %get-tuple-element.19), channel_id=1, source_target_pairs={{0,1},{1,0},{2,9},{3,8},{4,17},{5,16},{6,25},{7,24},{8,3},{9,2},{1... | collective-permute-start | bytes 12296 | tf_op jit(solution)/shard_map/ppermute | solution.py:44
  16.7 0.5 collective-permute-done
  17.2 2.7 %collective-permute-done.1 = f32[2,512]{1,0:T(2,128)S(1)} collective-permute-done((f32[2,512]{1,0:T(2,128)S(1)}, f32[2,512]{1,0:T(2,128)S(1)}, u32[]{:S(2)}, u32[]{:S(2)}) %collective-permute-start.1) | collective-permute-done | bytes 4128 | tf_op jit(solution)/shard_map/ppermute | solution.py:44
  20.0 30.5 %all_to_all.35 = f32[16,2,2,512]{3,2,1,0:T(2,128)S(1)} all-to-all(f32[16,2,2,512]{3,2,1,0:T(2,128)S(1)} %broadcast_in_dim.2), channel_id=1, replica_groups=mesh['mp'=16,'trow'=4,'y'=4,'core'=2] {'mp'}, dimensions={0} | all-to-all | bytes 262144 | tf_op jit(solution)/shard_map/all_to_all | solution.py:24
  50.5 0.1 all_gather_reshape.3
  50.6 17.5 %all_gather.6 = f32[4,64,512]{2,1,0:T(8,128)S(1)} all-gather(f32[1,64,512]{2,1,0:T(8,128)S(1)} %all_gather_reshape.3), channel_id=1, replica_groups=mesh['mp'=16,'trow'=4,'y'=4,'core'=2] {'trow'}, dimensions={0}, use_global_device_ids=true | all-gather | bytes 655360 | tf_op jit(solution)/shard_map/all_gather | solution.py:203
  68.1 2.3 %fusion = f32[128,1024]{1,0:T(8,128)S(1)} fusion(f32[128,512]{1,0:T(8,128)S(1)} %bitcast.30, f32[1,1024,512]{2,1,0:T(8,128)S(1)} %copy-done.4), kind=kOutput, calls=%fused_computation | convolution fusion | flops 805306368 | bytes 2883584 | tf_op jit(solution)/shard_map/dot_general | solution.py:14
  70.4 1.9 %collective-permute-start.2 = (f32[128,1024]{1,0:T(8,128)S(1)}, f32[128,1024]{1,0:T(8,128)S(1)}, u32[]{:S(2)}, u32[]{:S(2)}) collective-permute-start(f32[128,1024]{1,0:T(8,128)S(1)} %fusion), channel_id=1, source_target_pairs={{0,1},{1,0},{2,3},{3,2},{4,5},{5,4},{6,7},{7,6},{8,9},{9,8},{10,11... | collective-permute-start | bytes 1572872 | tf_op jit(solution)/shard_map/ppermute | solution.py:205
  72.3 1.9 %collective-permute-done.2 = f32[128,1024]{1,0:T(8,128)S(1)} collective-permute-done((f32[128,1024]{1,0:T(8,128)S(1)}, f32[128,1024]{1,0:T(8,128)S(1)}, u32[]{:S(2)}, u32[]{:S(2)}) %collective-permute-start.2) | collective-permute-done | bytes 524320 | tf_op jit(solution)/shard_map/ppermute | solution.py:205
  74.2 2.3 %fusion.4 = f32[128,1024]{1,0:T(8,128)S(1)} fusion(f32[128,1024]{1,0:T(8,128)S(1)} %collective-permute-done.2, f32[128,512]{1,0:T(8,128)S(1)} %bitcast.29, f32[1,1024,512]{2,1,0:T(8,128)S(1)} %copy-done.4), kind=kOutput, calls=%fused_computation.4 | convolution fusion | flops 805437440 | bytes 3407872 | tf_op jit(solution)/shard_map/dot_general | solution.py:14
  76.5 12.5 %all_to_all.36 = f32[4,32,1024]{2,1,0:T(8,128)S(1)} all-to-all(f32[4,32,1024]{2,1,0:T(8,128)S(1)} %bitcast.28), channel_id=1, replica_groups=mesh['mp'=16,'trow'=4,'y'=4,'core'=2] {'y'}, dimensions={0} | all-to-all | bytes 1048576 | tf_op jit(solution)/shard_map/all_to_all | solution.py:24
  89.0 2.9 %reduce-scatter.2.cloned.1.call-done = f32[32,1024]{1,0:T(8,128)} async-done(((f32[512,1024]{1,0:T(8,128)}), f32[32,1024]{1,0:T(8,128)}) %reduce-scatter.2.cloned.1.call-update) | async-done | bytes 131088 | tf_op jit(solution)/shard_map/reduce_scatter | solution.py:198
  92.0 0.1 reshape.29
  92.1 22.9 %all_to_all.37.terms_ref = f32[16,2,1024]{2,1,0:T(2,128)S(1)} all-to-all(f32[16,2,1024]{2,1,0:T(2,128)S(1)} %reshape.29), channel_id=1, replica_groups=mesh['mp'=16,'trow'=4,'y'=4,'core'=2] {'mp'}, dimensions={0} | all-to-all | bytes 262144 | tf_op jit(solution)/shard_map/all_to_all | solution.py:24
  115.0 16.9 %all_to_all.38 = f32[16,2,1024]{2,1,0:T(2,128)S(1)} all-to-all(f32[16,2,1024]{2,1,0:T(2,128)S(1)} %get-tuple-element.11), channel_id=1, replica_groups=mesh['mp'=16,'trow'=4,'y'=4,'core'=2] {'mp'}, dimensions={0} | all-to-all | bytes 262144 | tf_op jit(solution)/shard_map/all_to_all | solution.py:24
  131.9 0.1 reshape.30.first_ref
  132.0 0.0 all-gather.2.cloned.1.call-done.total_ref
  132.0 1.2 copy-done
  133.3 1.0 shard_map.51
  134.3 10.3 %all_to_all.39.shares_ref = f32[4,32,256]{2,1,0:T(8,128)S(1)} all-to-all(f32[4,32,256]{2,1,0:T(8,128)S(1)} %shard_map.51), channel_id=1, replica_groups=mesh['mp'=16,'trow'=4,'y'=4,'core'=2] {'trow'}, dimensions={0} | all-to-all | bytes 262144 | tf_op jit(solution)/shard_map/all_to_all | solution.py:24
  144.6 0.7 shard_map.52
  145.3 17.2 %all_to_all.40.pieces_ref = f32[16,2,1088]{2,1,0:T(2,128)S(1)} all-to-all(f32[16,2,1088]{2,1,0:T(2,128)S(1)} %shard_map.52), channel_id=1, replica_groups=mesh['mp'=16,'trow'=4,'y'=4,'core'=2] {'mp'}, dimensions={0} | all-to-all | bytes 278528 | tf_op jit(solution)/shard_map/all_to_all | solution.py:24
  162.5 0.1 reshape.31
  162.6 0.1 reshape.32.second_ref
  162.7 0.4 shard_map.53
  163.0 7.6 %all_to_all.41.known_ref = f32[4,2,128]{2,1,0:T(2,128)S(1)} all-to-all(f32[4,2,128]{2,1,0:T(2,128)S(1)} %get-tuple-element.14), channel_id=1, replica_groups=mesh['mp'=16,'trow'=4,'y'=4,'core'=2] {'trow'}, dimensions={0} | all-to-all | bytes 8192 | tf_op jit(solution)/shard_map/all_to_all | solution.py:24
  170.7 0.9 shard_map.54
  (19 shorter events, 0.2 us)
Async XLA Ops:
  7.2 84.8 %reduce-scatter.2.cloned.1.call-start = ((), (), s32[]{:S(2)}) async-start(), calls=%async_computation.8 | async-start | bytes 2228224 | tf_op jit(solution)/shard_map/reduce_scatter | solution.py:198
  10.1 0.7 copy-start.2
  10.1 58.0 %copy-start.4 = (f32[1,1024,512]{2,1,0:T(8,128)S(1)}, f32[1,1024,512]{2,1,0:T(8,128)}, u32[]{:S(2)}) copy-start(f32[1,1024,512]{2,1,0:T(8,128)} %param.3) | copy-start | bytes 6291460
  10.2 121.9 %all-gather.2.cloned.1.call-start = ((), (), s32[]{:S(2)}) async-start(), calls=%async_computation.9 | async-start | bytes 1179648 | tf_op jit(solution)/shard_map/all_gather | solution.py:212
  10.8 6.4 %collective-permute-start = (f32[2,512]{1,0:T(2,128)S(1)}, f32[2,512]{1,0:T(2,128)S(1)}, u32[]{:S(2)}, u32[]{:S(2)}) collective-permute-start(f32[2,512]{1,0:T(2,128)S(1)} %get-tuple-element.18), channel_id=1, source_target_pairs={{0,0},{1,1},{2,8},{3,9},{4,16},{5,17},{6,24},{7,25},{8,2},{9,3},{1... | collective-permute-start | bytes 12296 | tf_op jit(solution)/shard_map/ppermute | solution.py:44
  14.1 5.8 %collective-permute-start.1 = (f32[2,512]{1,0:T(2,128)S(1)}, f32[2,512]{1,0:T(2,128)S(1)}, u32[]{:S(2)}, u32[]{:S(2)}) collective-permute-start(f32[2,512]{1,0:T(2,128)S(1)} %get-tuple-element.19), channel_id=1, source_target_pairs={{0,1},{1,0},{2,9},{3,8},{4,17},{5,16},{6,25},{7,24},{8,3},{9,2},{1... | collective-permute-start | bytes 12296 | tf_op jit(solution)/shard_map/ppermute | solution.py:44
  70.4 3.8 %collective-permute-start.2 = (f32[128,1024]{1,0:T(8,128)S(1)}, f32[128,1024]{1,0:T(8,128)S(1)}, u32[]{:S(2)}, u32[]{:S(2)}) collective-permute-start(f32[128,1024]{1,0:T(8,128)S(1)} %fusion), channel_id=1, source_target_pairs={{0,1},{1,0},{2,3},{3,2},{4,5},{5,4},{6,7},{7,6},{8,9},{9,8},{10,11... | collective-permute-start | bytes 1572872 | tf_op jit(solution)/shard_map/ppermute | solution.py:205
  74.2 40.7 %copy-start.3 = (f32[2,1024]{1,0:T(2,128)S(1)}, f32[2,1024]{1,0:T(2,128)}, u32[]{:S(2)}) copy-start(f32[2,1024]{1,0:T(2,128)} %rhs_ref.1) | copy-start | bytes 24580
  132.0 1.2 copy-start
  133.3 11.3 %copy-start.1 = (f32[256,1024]{1,0:T(8,128)S(1)}, f32[256,1024]{1,0:T(8,128)}, u32[]{:S(2)}) copy-start(f32[256,1024]{1,0:T(8,128)} %all-gather.2.cloned.1.call-done.total_ref) | copy-start | bytes 3145732
Sparse Core Ops, SparseCore 0:
  10.8 81.0 reduce-scatter.1
  94.1 27.9 all-gather.1
